TPU v7x, 32 devices: a whole 2x2x4 slice. The times are simulated.
32 devices in a mesh: grp: 4 (over y, core), wide: 8 (over z, x).
Axes of the slice: x: 2, y: 2, z: 4, core: 2. Of those that a mesh axis runs over, the one named last changes fastest.
Arguments:
- features: bfloat16 [6144, 2304], P(('grp', 'wide')), may hold values from -6 to 6
- labels: int32 [6144], P(('grp', 'wide')), may hold values from 0 to 9
- counts: int32 [32], P(('grp', 'wide')), may hold values from 64 to 192, as said below
- weight6: float32 [2304, 384], P('wide'), may hold values from -0.125 to 0.125
- weight7: float32 [384, 192], P('wide'), may hold values from -0.3125 to 0.3125
- weight8: float32 [192, 10], P('wide'), may hold values from -1.25 to 1.25
- moment6: float32 [2304, 384], P('wide'), may hold values from -0.00390625 to 0.00390625
- moment7: float32 [384, 192], P('wide'), may hold values from -0.0068359375 to 0.0068359375
- moment8: float32 [192, 10], P('wide'), may hold values from -0.01171875 to 0.01171875
- resid6: float32 [73728, 384], P(('grp', 'wide')), may hold values from -4 to 4
- resid7: float32 [12288, 192], P(('grp', 'wide')), may hold values from -8 to 8
- resid8: float32 [6144, 10], P(('grp', 'wide')), may hold values from -12 to 12
- noise6: int32 [73728, 384], P(('grp', 'wide')), may hold values from 0 to 1023
- noise7: int32 [12288, 192], P(('grp', 'wide')), may hold values from 0 to 1023
- noise8: int32 [6144, 10], P(('grp', 'wide')), may hold values from 0 to 1023
- biases: float32 [586], replicated, may hold values from -1.75 to 1.75
- bias_first: float32 [586], replicated
- bias_second: float32 [586], replicated
Outputs:
- new_weight6: float32 [2304, 384], P('wide')
- new_weight7: float32 [384, 192], P('wide')
- new_weight8: float32 [192, 10], P('wide')
- low_weight6: bfloat16 [2304, 384], P('wide')
- low_weight7: bfloat16 [384, 192], P('wide')
- low_weight8: bfloat16 [192, 10], P('wide')
- new_moment6: float32 [2304, 384], P('wide')
- new_moment7: float32 [384, 192], P('wide')
- new_moment8: float32 [192, 10], P('wide')
- new_resid6: float32 [73728, 384], P(('grp', 'wide'))
- new_resid7: float32 [12288, 192], P(('grp', 'wide'))
- new_resid8: float32 [6144, 10], P(('grp', 'wide'))
- new_biases: float32 [586], replicated
- new_bias_first: float32 [586], replicated
- new_bias_second: float32 [586], replicated
- loss_sum: float32 [], replicated
- image_count: float32 [], replicated
Inputs may be any that keep to these rules, and one draw needn't show every extreme that they name: `counts`: varies from worker to worker; some worker holds exactly 192 images and some exactly 64.
All inputs are finite; a program needn't handle non-finite values. Where the computation divides by a largest or mean magnitude, that divisor is 1e-20 or more.
Results may differ from a plain program's by a relative error of at most 0.011.
Values may be sent and summed in bfloat16 or wider, within the bound.
No kernel may reach another device: no remote copies, remote signals or barrier semaphores. Data moves between devices by JAX's collectives and lax.ppermute only.
A program may use at most 128 MiB of HBM per device.

v0:
```python
import jax
import jax.numpy as jnp
from jax import lax
from jax.sharding import PartitionSpec as P

NS_STEPS = 5
ADAM_STEP = 10


highest = lax.Precision.HIGHEST
smoothing = 0.1
clip_width = 2.5
noise_levels = 1024.0
ramp_slope = 2.0
momentum_decay = 0.95
muon_rate = 0.6
decay_rate = 0.01
coef_a = 3.4445
coef_b = -4.775
coef_c = 2.0315
beta_first = 0.9
beta_second = 0.999
bias_rate = 0.05
adam_eps = 1e-08


def dithered_code(clipped, peak, noise):
    ratio = jnp.abs(clipped) / peak
    dither = (noise.astype(jnp.float32) + 0.5) / noise_levels
    return jnp.sign(clipped) * jnp.clip(ramp_slope * (ratio - dither) + ratio, 0.0, 1.0)


def gram_of(iterate):
    return jnp.dot(iterate.T, iterate, precision=highest)


def schulz_step(iterate, gram_matrix):
    mixed = coef_b * gram_matrix + coef_c * jnp.dot(gram_matrix, gram_matrix, precision=highest)
    return coef_a * iterate + jnp.dot(iterate, mixed, precision=highest)


def layer_forward(inputs_b, weight_b, bias_part):
    return jnp.dot(inputs_b, weight_b, preferred_element_type=jnp.float32) + bias_part


def layer_backward(inputs_b, weight_b, grad_pre):
    grad_low = grad_pre.astype(jnp.bfloat16)
    weight_grad = jnp.einsum("ri,ro->io", inputs_b, grad_low, preferred_element_type=jnp.float32)
    bias_grad = jnp.sum(grad_low.astype(jnp.float32), axis=0)
    grad_inputs = jnp.einsum("ro,io->ri", grad_low, weight_b, preferred_element_type=jnp.float32)
    return (weight_grad, bias_grad, grad_inputs)


def on_device(
    features,
    labels,
    counts,
    weight6,
    weight7,
    weight8,
    moment6,
    moment7,
    moment8,
    resid6,
    resid7,
    resid8,
    noise6,
    noise7,
    noise8,
    biases,
    bias_first,
    bias_second,
):
    masters = (weight6, weight7, weight8)
    weights_b = (
        lax.all_gather(weight6.astype(jnp.bfloat16), "wide", axis=0, tiled=True),
        lax.all_gather(weight7.astype(jnp.bfloat16), "wide", axis=0, tiled=True),
        lax.all_gather(weight8.astype(jnp.bfloat16), "wide", axis=0, tiled=True),
    )
    widths = [weights_b[0].shape[1], weights_b[1].shape[1], weights_b[2].shape[1]]
    bias_parts = [
        biases[: widths[0]],
        biases[widths[0] : widths[0] + widths[1]],
        biases[widths[0] + widths[1] :],
    ]
    row_mask = (jnp.arange(features.shape[0]) < counts[0]).astype(jnp.float32)
    inputs_list = [features]
    gelu_backs = []
    logits = None
    for which_layer in range(3):
        pre_act = layer_forward(
            inputs_list[which_layer], weights_b[which_layer], bias_parts[which_layer]
        )
        if which_layer < 2:
            activ, gelu_back = jax.vjp(jax.nn.gelu, pre_act)
            inputs_list.append(activ.astype(jnp.bfloat16))
            gelu_backs.append(gelu_back)
        else:
            logits = pre_act
    logp = jax.nn.log_softmax(logits, axis=-1)
    onehot = (labels[:, None] == jnp.arange(widths[2])[None, :]).astype(jnp.float32)
    target = (1.0 - smoothing) * onehot + smoothing / widths[2]
    worker_loss = jnp.sum(-jnp.sum(target * logp, axis=-1) * row_mask)
    upstream = -target * row_mask[:, None]
    grad_pre = upstream - jnp.exp(logp) * jnp.sum(upstream, axis=-1, keepdims=True)
    weight_grads = [None, None, None]
    bias_grads = [None, None, None]
    for which_layer in (2, 1, 0):
        weight_grads[which_layer], bias_grads[which_layer], grad_inputs = layer_backward(
            inputs_list[which_layer], weights_b[which_layer], grad_pre
        )
        if which_layer > 0:
            grad_pre = gelu_backs[which_layer - 1](grad_inputs)[0]
    resids = (resid6, resid7, resid8)
    noises = (noise6, noise7, noise8)
    accs = [weight_grads[k] + resids[k] for k in range(3)]
    clipped_list = []
    for acc in accs:
        bound = clip_width * jnp.sqrt(jnp.mean(acc * acc))
        clipped_list.append(jnp.clip(acc, -bound, bound))
    peak_list = lax.pmax(
        (
            jnp.max(jnp.abs(clipped_list[0])),
            jnp.max(jnp.abs(clipped_list[1])),
            jnp.max(jnp.abs(clipped_list[2])),
        ),
        ("grp", "wide"),
    )
    peak_list = [p + 1e-06 for p in peak_list]
    code_list = [dithered_code(clipped_list[k], peak_list[k], noises[k]) for k in range(3)]
    new_resids = [accs[k] - peak_list[k] * code_list[k] for k in range(3)]
    loss_total, image_total, bias_total = lax.psum(
        (worker_loss, jnp.sum(row_mask), jnp.concatenate(bias_grads)), ("grp", "wide")
    )
    code_rows = (
        lax.psum_scatter(code_list[0], "wide", scatter_dimension=0, tiled=True),
        lax.psum_scatter(code_list[1], "wide", scatter_dimension=0, tiled=True),
        lax.psum_scatter(code_list[2], "wide", scatter_dimension=0, tiled=True),
    )
    code_sums = lax.psum((code_rows[0], code_rows[1], code_rows[2]), "grp")
    moments = (moment6, moment7, moment8)
    new_moments = [
        momentum_decay * moments[k] + peak_list[k] * code_sums[k] / image_total for k in range(3)
    ]
    full_moments = (
        lax.all_gather(new_moments[0], "wide", axis=0, tiled=True),
        lax.all_gather(new_moments[1], "wide", axis=0, tiled=True),
        lax.all_gather(new_moments[2], "wide", axis=0, tiled=True),
    )
    row_block = lax.axis_index("wide")
    iterates = []
    for k in range(3):
        whole = full_moments[k]
        iterate = whole / (jnp.sqrt(jnp.sum(whole * whole)) + 1e-07)
        for step_num in range(NS_STEPS):
            iterate = schulz_step(iterate, gram_of(iterate))
        row_count = new_moments[k].shape[0]
        iterates.append(lax.dynamic_slice_in_dim(iterate, row_block * row_count, row_count, 0))
    new_weights = [
        masters[k] - muon_rate * (iterates[k] + decay_rate * masters[k]) for k in range(3)
    ]
    bias_grad = bias_total / image_total
    first_new = beta_first * bias_first + (1.0 - beta_first) * bias_grad
    second_new = beta_second * bias_second + (1.0 - beta_second) * bias_grad * bias_grad
    first_hat = first_new / (1.0 - beta_first**ADAM_STEP)
    second_hat = second_new / (1.0 - beta_second**ADAM_STEP)
    biases_new = biases - bias_rate * (
        first_hat / (jnp.sqrt(second_hat) + adam_eps) + decay_rate * biases
    )
    return (
        new_weights[0],
        new_weights[1],
        new_weights[2],
        new_weights[0].astype(jnp.bfloat16),
        new_weights[1].astype(jnp.bfloat16),
        new_weights[2].astype(jnp.bfloat16),
        new_moments[0],
        new_moments[1],
        new_moments[2],
        new_resids[0],
        new_resids[1],
        new_resids[2],
        biases_new,
        first_new,
        second_new,
        loss_total,
        image_total,
    )


def solution(mesh):
    return jax.shard_map(
        on_device,
        mesh=mesh,
        in_specs=(
            P(("grp", "wide"), None),
            P(("grp", "wide")),
            P(("grp", "wide")),
            P("wide", None),
            P("wide", None),
            P("wide", None),
            P("wide", None),
            P("wide", None),
            P("wide", None),
            P(("grp", "wide"), None),
            P(("grp", "wide"), None),
            P(("grp", "wide"), None),
            P(("grp", "wide"), None),
            P(("grp", "wide"), None),
            P(("grp", "wide"), None),
            P(),
            P(),
            P(),
        ),
        out_specs=(
            P("wide", None),
            P("wide", None),
            P("wide", None),
            P("wide", None),
            P("wide", None),
            P("wide", None),
            P("wide", None),
            P("wide", None),
            P("wide", None),
            P(("grp", "wide"), None),
            P(("grp", "wide"), None),
            P(("grp", "wide"), None),
            P(),
            P(),
            P(),
            P(),
            P(),
        ),
        check_vma=False,
    )
```

profile of v0, /device:TPU:0, one launch (start us, length us, event | category | flops | bytes accessed | tf_op | source)
XLA Modules:
  0.0 490.6 jit_solution(4001529569216310789)
XLA Ops:
  7.3 1.8 convert_element_type.60
  9.8 0.8 slice.11
  10.6 5.2 %copy.98 = f32[2304,384]{0,1:T(8,128)} copy(f32[2304,384]{1,0:T(8,128)} %param.27) | data formatting | bytes 7077888 | tf_op args[9]
  15.8 32.3 %all-gather = bf16[8,24,10]{1,2,0:T(8,128)(2,1)S(1)} all-gather(bf16[1,24,10]{1,2,0:T(8,128)(2,1)S(1)} %convert_bitcast_fusion), channel_id=1, replica_groups=mesh['grp'=4,'wide'=8] {'wide'}, dimensions={0}, use_global_device_ids=true | all-gather | bytes 4320 | tf_op jit(solution)/shard_map/all_gather | solution.py:78
  48.9 31.0 %all_gather.19 = bf16[384,192]{1,0:T(8,128)(2,1)S(1)} all-gather(bf16[48,192]{1,0:T(8,128)(2,1)S(1)} %convert_element_type.62), channel_id=1, replica_groups=mesh['grp'=4,'wide'=8] {'wide'}, dimensions={0}, use_global_device_ids=true | all-gather | bytes 165888 | tf_op jit(solution)/shard_map/all_gather | solution.py:77
  79.9 2.2 convolution_add_fusion.9
  83.5 3.1 multiply_reduce_fusion.1
  87.3 0.9 multiply_reduce_fusion.3
  88.9 0.7 multiply_reduce_fusion.6
  90.3 2.9 abs_reduce_fusion
  94.5 5.2 %copy.99 = s32[2304,384]{0,1:T(8,128)} copy(s32[2304,384]{1,0:T(8,128)} %param.30) | data formatting | bytes 7077888 | tf_op args[12]
  99.7 39.8 %all-reduce.2 = (f32[]{:T(128)}, f32[]{:T(128)}, f32[]{:T(128)}) all-reduce(f32[]{:T(128)} %abs_reduce_fusion, f32[]{:T(128)} %abs_reduce_fusion.1, f32[]{:T(128)} %abs_reduce_fusion.2), channel_id=1, replica_groups=mesh['grp'=4,'wide'=8] {'grp','wide'}, use_global_device_ids=true, to_apply=%region_5.6 | all-reduce | flops 3 | bytes 24 | tf_op jit(solution)/shard_map/pmax | solution.py:121
  140.8 0.9 multiply_subtract_fusion.1
  141.7 0.9 copy.116
  142.7 8.5 %multiply_subtract_fusion = (f32[2304,384]{0,1:T(8,128)}, f32[2304,384]{0,1:T(8,128)}) fusion(f32[2304,384]{0,1:T(8,128)} %get-tuple-element.119, f32[]{:T(128)S(6)} %add.261, s32[2304,384]{0,1:T(8,128)} %copy.99, f32[]{:T(128)S(6)} %neg.16, f32[]{:T(128)S(6)} %mul.476), kind=kLoop, calls=%fused_computation.6 | loop fusion | flops 13271040 | bytes 14155788 | tf_op jit(solution)/shard_map/sub | solution.py:131
  151.2 5.2 %copy.114 = f32[2304,384]{1,0:T(8,128)} copy(f32[2304,384]{0,1:T(8,128)} %get-tuple-element.103) | data formatting | bytes 7077888
  156.5 0.8 copy-done.5
  159.6 41.0 %all-reduce.1 = (f32[]{:T(128)}, f32[586]{0:T(1024)S(1)}, f32[]{:T(128)}) all-reduce(f32[]{:T(128)} %get-tuple-element.127, f32[586]{0:T(1024)S(1)} %pad_maximum_fusion, f32[]{:T(128)} %get-tuple-element.126), channel_id=1, replica_groups=mesh['grp'=4,'wide'=8] {'grp','wide'}, use_global_device_ids=true, to_apply=%region_9.10 | all-reduce | flops 588 | bytes 4704 | tf_op jit(solution)/shard_map/psum | solution.py:132
  201.4 5.2 %copy.112 = f32[2304,384]{1,0:T(8,128)} copy(f32[2304,384]{0,1:T(8,128)} %get-tuple-element.102) | data formatting | bytes 7077888
  207.2 37.6 %all-reduce = f32[192,10]{0,1:T(8,128)S(1)} all-reduce(f32[192,10]{0,1:T(8,128)S(1)} %get-tuple-element.99), channel_id=4, replica_groups=mesh['grp'=4,'wide'=8] {'wide'}, use_global_device_ids=true, to_apply=%region_20.21.clone | all-reduce | flops 1920 | bytes 15360
  244.9 1.3 multiply_subtract_fusion.3
  246.2 0.9 copy.117
  247.1 11.7 %all-reduce.3 = (f32[48,192]{0,1:T(8,128)S(1)}, f32[24,10]{0,1:T(8,128)S(1)}) all-reduce(f32[48,192]{0,1:T(8,128)S(1)} %copy.117, f32[24,10]{0,1:T(8,128)S(1)} %constant_dynamic-slice_fusion), channel_id=1, replica_groups=mesh['grp'=4,'wide'=8] {'grp'}, use_global_device_ids=true, to_apply=%region_15.16 | all-reduce | flops 9456 | bytes 75648 | tf_op jit(solution)/shard_map/psum | solution.py:140
  259.6 32.3 %all_gather.22 = f32[384,192]{1,0:T(8,128)S(1)} all-gather(f32[48,192]{1,0:T(8,128)S(1)} %copy.102), channel_id=1, replica_groups=mesh['grp'=4,'wide'=8] {'wide'}, dimensions={0}, use_global_device_ids=true | all-gather | bytes 331776 | tf_op jit(solution)/shard_map/all_gather | solution.py:147
  296.4 2.1 copy.115
  299.1 31.4 %all-reduce.6.cloned.1.call-done = f32[288,384]{0,1:T(8,128)} async-done(((f32[288,384]{0,1:T(8,128)}), f32[288,384]{0,1:T(8,128)}) %all-reduce.6.cloned.1.call-update) | async-done | bytes 442384 | tf_op jit(solution)/shard_map/psum | solution.py:140
  330.4 1.8 divide_add_fusion
  332.2 1.0 copy.100
  338.7 31.2 %all-gather.1 = f32[8,24,10]{1,2,0:T(8,128)S(1)} all-gather(f32[1,24,10]{1,2,0:T(8,128)S(1)} %bitcast.117), channel_id=1, replica_groups=mesh['grp'=4,'wide'=8] {'wide'}, dimensions={0}, use_global_device_ids=true | all-gather | bytes 8640 | tf_op jit(solution)/shard_map/all_gather | solution.py:148
  371.3 0.7 copy.109
  375.2 24.5 %all-gather.7.cloned.1.call-done = f32[2304,384]{1,0:T(8,128)} async-done(((f32[288,384]{1,0:T(8,128)}), f32[2304,384]{1,0:T(8,128)}) %all-gather.7.cloned.1.call-update) | async-done | bytes 3538960 | tf_op jit(solution)/shard_map/all_gather | solution.py:146
  399.7 3.5 multiply_reduce_fusion
  403.9 9.1 %fusion.1 = f32[384,384]{1,0:T(8,128)S(1)} fusion(f32[2304,384]{1,0:T(8,128)} %all-gather.7.cloned.1.call-done, f32[]{:T(128)S(6)} %add.266), kind=kOutput, calls=%fused_computation.13 | convolution fusion | flops 4077748224 | bytes 4128772 | tf_op jit(solution)/shard_map/dot_general | solution.py:34
  413.0 1.3 fusion.2
  414.3 7.9 %convolution_add_fusion.3 = f32[2304,384]{1,0:T(8,128)S(1)} fusion(f32[384,384]{1,0:T(8,128)S(1)} %fusion.2, f32[2304,384]{1,0:T(8,128)S(1)} %copy-done.3, f32[]{:T(128)S(6)} %add.266), kind=kOutput, calls=%fused_computation.3 | convolution fusion | flops 4080402432 | bytes 7667716 | tf_op jit(solution)/shard_map/dot_general | solution.py:39
  422.2 5.9 %fusion.54 = f32[384,384]{1,0:T(8,128)S(1)} fusion(f32[2304,384]{1,0:T(8,128)S(1)} %convolution_add_fusion.3), kind=kOutput, calls=%fused_computation.136 | convolution fusion | flops 4076863488 | bytes 4128768 | tf_op jit(solution)/shard_map/dot_general | solution.py:34
  428.2 1.3 fusion.3
  429.5 7.9 %convolution_add_fusion.2 = f32[2304,384]{1,0:T(8,128)S(1)} fusion(f32[2304,384]{1,0:T(8,128)S(1)} %convolution_add_fusion.3, f32[384,384]{1,0:T(8,128)S(1)} %fusion.3), kind=kOutput, calls=%fused_computation.2 | convolution fusion | flops 4078632960 | bytes 7667712 | tf_op jit(solution)/shard_map/dot_general | solution.py:39
  437.4 6.4 %fusion.55 = f32[384,384]{1,0:T(8,128)S(1)} fusion(f32[2304,384]{1,0:T(8,128)S(1)} %convolution_add_fusion.2), kind=kOutput, calls=%fused_computation.137 | convolution fusion | flops 4076863488 | bytes 4128768 | tf_op jit(solution)/shard_map/dot_general | solution.py:34
  443.7 1.3 fusion.4
  445.0 7.7 %convolution_add_fusion.1 = f32[2304,384]{1,0:T(8,128)S(1)} fusion(f32[2304,384]{1,0:T(8,128)S(1)} %convolution_add_fusion.2, f32[384,384]{1,0:T(8,128)S(1)} %fusion.4), kind=kOutput, calls=%fused_computation.1 | convolution fusion | flops 4078632960 | bytes 7667712 | tf_op jit(solution)/shard_map/dot_general | solution.py:39
  452.7 6.1 %fusion.56 = f32[384,384]{1,0:T(8,128)S(1)} fusion(f32[2304,384]{1,0:T(8,128)S(1)} %convolution_add_fusion.1), kind=kOutput, calls=%fused_computation.138 | convolution fusion | flops 4076863488 | bytes 4128768 | tf_op jit(solution)/shard_map/dot_general | solution.py:34
  458.8 1.3 fusion.5
  460.1 7.7 %convolution_add_fusion = f32[2304,384]{1,0:T(8,128)S(1)} fusion(f32[2304,384]{1,0:T(8,128)S(1)} %convolution_add_fusion.1, f32[384,384]{1,0:T(8,128)S(1)} %fusion.5), kind=kOutput, calls=%fused_computation | convolution fusion | flops 4078632960 | bytes 7667712 | tf_op jit(solution)/shard_map/dot_general | solution.py:39
  467.8 6.2 %fusion.57 = f32[384,384]{1,0:T(8,128)S(1)} fusion(f32[2304,384]{1,0:T(8,128)S(1)} %convolution_add_fusion), kind=kOutput, calls=%fused_computation.139 | convolution fusion | flops 4076863488 | bytes 4128768 | tf_op jit(solution)/shard_map/dot_general | solution.py:34
  474.0 1.3 fusion.6
  475.3 7.4 %fusion.58 = f32[2304,384]{1,0:T(8,128)S(1)} fusion(f32[2304,384]{1,0:T(8,128)S(1)} %convolution_add_fusion, f32[384,384]{1,0:T(8,128)S(1)} %fusion.6), kind=kOutput, calls=%fused_computation.140 | convolution fusion | flops 4076863488 | bytes 7667712 | tf_op jit(solution)/shard_map/dot_general | solution.py:39
  482.8 0.9 fusion.50
  (121 shorter events, 20.4 us)
Async XLA Ops:
  7.2 72.7 %copy-start = (bf16[192,2304]{1,0:T(8,128)(2,1)S(1)}, bf16[192,2304]{1,0:T(8,128)(2,1)}, u32[]{:S(2)}) copy-start(bf16[192,2304]{1,0:T(8,128)(2,1)} %param.18) | copy-start | bytes 2654212
  7.2 72.7 %all-gather.5.cloned.1.call-start = ((), (), s32[]{:S(2)}) async-start(), calls=%async_computation.2 | async-start | bytes 1990656 | tf_op jit(solution)/shard_map/all_gather | solution.py:76
  9.1 237.1 %reduce-scatter.10.cloned.1.call-start = ((), (), s32[]{:S(2)}) async-start(), calls=%async_computation.6 | async-start | bytes 442368
  10.6 5.2 %copy-start.8 = (f32[48,192]{1,0:T(8,128)S(1)}, f32[48,192]{1,0:T(8,128)}, u32[]{:S(2)}) copy-start(f32[48,192]{1,0:T(8,128)} %param.22) | copy-start | bytes 110596
  10.6 5.2 %copy-start.11 = (f32[24,10]{0,1:T(8,128)S(1)}, f32[24,10]{0,1:T(8,128)}, u32[]{:S(2)}) copy-start(f32[24,10]{0,1:T(8,128)} %param.23) | copy-start | bytes 2884
  10.6 69.3 %slice-start = ((f32[586]{0:T(1024)}), f32[384]{0:T(512)S(1)}, s32[]{:S(2)}) async-start(f32[586]{0:T(1024)} %param.33), calls=%async_computation.7 | async-start | bytes 4096 | tf_op jit(solution)/shard_map/slice | solution.py:82
  15.7 66.9 %copy-start.18 = (s32[192]{0:T(256)S(1)}, s32[192]{0:T(256)}, u32[]{:S(2)}) copy-start(s32[192]{0:T(256)} %param.19) | copy-start | bytes 2308
  79.9 3.5 copy-start.2
  83.4 3.8 copy-start.19
  83.5 5.4 %copy-start.12 = (f32[192,10]{0,1:T(8,128)S(1)}, f32[192,10]{0,1:T(8,128)}, u32[]{:S(2)}) copy-start(f32[192,10]{0,1:T(8,128)} %param.29) | copy-start | bytes 23044
  94.5 46.4 %copy-start.6 = (s32[384,192]{0,1:T(8,128)S(1)}, s32[384,192]{0,1:T(8,128)}, u32[]{:S(2)}) copy-start(s32[384,192]{0,1:T(8,128)} %param.31) | copy-start | bytes 884740
  142.7 153.7 %reduce-scatter.8.cloned.1.call-start = ((), (), s32[]{:S(2)}) async-start(), calls=%async_computation.5 | async-start | bytes 3981312
  156.3 1.0 copy-start.5
  156.3 1.2 copy-start.9
  156.3 1.4 copy-start.20
  156.4 174.1 %all-reduce.6.cloned.1.call-start = ((), (), s32[]{:S(2)}) async-start(), calls=%async_computation.3 | async-start | bytes 1179648 | tf_op jit(solution)/shard_map/psum | solution.py:140
  201.3 5.2 %copy-start.13 = (s32[192,10]{0,1:T(8,128)S(1)}, s32[192,10]{0,1:T(8,128)}, u32[]{:S(2)}) copy-start(s32[192,10]{0,1:T(8,128)} %param.32) | copy-start | bytes 23044
  201.3 43.5 %copy-start.14 = (f32[586]{0:T(1024)S(1)}, f32[586]{0:T(1024)}, u32[]{:S(2)}) copy-start(f32[586]{0:T(1024)} %param.33) | copy-start | bytes 7036
  201.3 43.5 %copy-start.16 = (f32[586]{0:T(1024)S(1)}, f32[586]{0:T(1024)}, u32[]{:S(2)}) copy-start(f32[586]{0:T(1024)} %param.34) | copy-start | bytes 7036
  201.4 43.5 %copy-start.17 = (f32[586]{0:T(1024)S(1)}, f32[586]{0:T(1024)}, u32[]{:S(2)}) copy-start(f32[586]{0:T(1024)} %param.35) | copy-start | bytes 7036
  259.6 36.8 %copy-start.7 = (f32[48,192]{1,0:T(8,128)}, f32[48,192]{1,0:T(8,128)S(1)}, u32[]{:S(2)}) copy-start(f32[48,192]{1,0:T(8,128)S(1)} %copy.102) | copy-start | bytes 110596
  298.5 101.2 %all-gather.7.cloned.1.call-start = ((), (), s32[]{:S(2)}) async-start(), calls=%async_computation.4 | async-start | bytes 3981312 | tf_op jit(solution)/shard_map/all_gather | solution.py:146
  333.2 4.8 copy-start.15
  338.7 74.3 %copy-start.10 = (f32[24,10]{0,1:T(8,128)}, f32[24,10]{0,1:T(8,128)S(1)}, u32[]{:S(2)}) copy-start(f32[24,10]{0,1:T(8,128)S(1)} %divide_add_fusion.2) | copy-start | bytes 2884
  403.9 10.4 %copy-start.3 = (f32[2304,384]{1,0:T(8,128)S(1)}, f32[2304,384]{1,0:T(8,128)}, u32[]{:S(2)}) copy-start(f32[2304,384]{1,0:T(8,128)} %all-gather.7.cloned.1.call-done) | copy-start | bytes 10616836
  474.0 9.7 %copy-start.1 = (bf16[192,2304]{1,0:T(8,128)(2,1)S(1)}, bf16[192,2304]{1,0:T(8,128)(2,1)}, u32[]{:S(2)}) copy-start(bf16[192,2304]{1,0:T(8,128)(2,1)} %param.18) | copy-start | bytes 2654212
  475.3 7.5 %copy-start.4 = (f32[288,384]{1,0:T(8,128)S(1)}, f32[288,384]{1,0:T(8,128)}, u32[]{:S(2)}) copy-start(f32[288,384]{1,0:T(8,128)} %param.21) | copy-start | bytes 1327108
Sparse Core Ops, SparseCore 0:
  10.8 50.1 all-gather.4
  142.8 62.0 reduce-scatter.9
  208.5 81.0 reduce-scatter.7
  298.6 31.7 all-reduce.5
  333.3 66.2 all-gather.6
where the time goes:
time: 499 us; the launch traced here: 491 us
  blocking collectives  257 us (52%)
  matrix products  96.6 us (19%)
  waiting for transfers between devices  56 us (11%)
  local copies, waits for them, and re-layouts  30.8 us (6%)
  other arithmetic  27.8 us (6%)
  between operations  22.2 us (4%)
    dot_general x15, matrix products, schulz_step(): return coef_a * iterate + jnp.dot(iterate, mixed, precision=highest)  42.8 us
    psum x1, blocking collectives, on_device(): lax.psum((worker_loss, jnp.sum(row_mask), jnp.concatenate(bias_grads)), (...  41 us
    pmax x1, blocking collectives, on_device(): lax.pmax((jnp.max(jnp.abs(clipped_list[0])), jnp.max(jnp.abs(clipped_list...  39.8 us
    unnamed x1, blocking collectives  37.6 us
    dot_general x15, matrix products, gram_of(): return jnp.dot(iterate.T, iterate, precision=highest)  36.9 us
    all_gather x1, blocking collectives, on_device(): lax.all_gather(weight8.astype(jnp.bfloat16), 'wide', axis=0, tiled=True)  32.3 us
    all_gather x1, blocking collectives, on_device(): lax.all_gather(new_moments[1], 'wide', axis=0, tiled=True)  32.3 us
    psum x1, waiting for transfers between devices, on_device(): code_sums = lax.psum((code_rows[0], code_rows[1], code_rows[2]), 'grp')  31.4 us
  transfers between devices with their start and end apart: 5, of which 2 were waited for; matrix products, arithmetic and copies ran while one was open for 9% of the time, Pallas kernels for 0%

commit v1 on v0

v1 whole, which is shorter than its diff:
```python
import functools

import jax
import jax.numpy as jnp
from jax import lax
from jax.experimental import pallas as pl
from jax.experimental.pallas import tpu as pltpu
from jax.sharding import PartitionSpec as P

NS_STEPS = 5
ADAM_STEP = 10


highest = lax.Precision.HIGHEST
smoothing = 0.1
clip_width = 2.5
noise_levels = 1024.0
ramp_slope = 2.0
momentum_decay = 0.95
muon_rate = 0.6
decay_rate = 0.01
coef_a = 3.4445
coef_b = -4.775
coef_c = 2.0315
beta_first = 0.9
beta_second = 0.999
bias_rate = 0.05
adam_eps = 1e-08

F32 = jnp.float32
BF16 = jnp.bfloat16
LANE = 128
BOTH = ("grp", "wide")
VMEM_LIMIT = 48 * 1024 * 1024


def dithered_code(clipped, peak, noise):
    ratio = jnp.abs(clipped) / peak
    dither = (noise.astype(jnp.float32) + 0.5) / noise_levels
    return jnp.sign(clipped) * jnp.clip(ramp_slope * (ratio - dither) + ratio, 0.0, 1.0)


def gram_of(iterate):
    return jnp.dot(iterate.T, iterate, precision=highest)


def schulz_step(iterate, gram_matrix):
    mixed = coef_b * gram_matrix + coef_c * jnp.dot(gram_matrix, gram_matrix, precision=highest)
    return coef_a * iterate + jnp.dot(iterate, mixed, precision=highest)


def layer_forward(inputs_b, weight_b, bias_part):
    return jnp.dot(inputs_b, weight_b, preferred_element_type=jnp.float32) + bias_part


def layer_backward(inputs_b, weight_b, grad_pre):
    grad_low = grad_pre.astype(jnp.bfloat16)
    weight_grad = jnp.einsum("ri,ro->io", inputs_b, grad_low, preferred_element_type=jnp.float32)
    bias_grad = jnp.sum(grad_low.astype(jnp.float32), axis=0)
    grad_inputs = jnp.einsum("ro,io->ri", grad_low, weight_b, preferred_element_type=jnp.float32)
    return (weight_grad, bias_grad, grad_inputs)


def adam_biases(biases, bias_first, bias_second, bias_grad):
    first_new = beta_first * bias_first + (1.0 - beta_first) * bias_grad
    second_new = beta_second * bias_second + (1.0 - beta_second) * bias_grad * bias_grad
    first_hat = first_new / (1.0 - beta_first**ADAM_STEP)
    second_hat = second_new / (1.0 - beta_second**ADAM_STEP)
    biases_new = biases - bias_rate * (
        first_hat / (jnp.sqrt(second_hat) + adam_eps) + decay_rate * biases
    )
    return biases_new, first_new, second_new


def general_plan(
    features,
    labels,
    counts,
    weight6,
    weight7,
    weight8,
    moment6,
    moment7,
    moment8,
    resid6,
    resid7,
    resid8,
    noise6,
    noise7,
    noise8,
    biases,
    bias_first,
    bias_second,
):
    masters = (weight6, weight7, weight8)
    weights_b = [
        lax.all_gather(weight.astype(jnp.bfloat16), "wide", axis=0, tiled=True)
        for weight in masters
    ]
    widths = [weights_b[0].shape[1], weights_b[1].shape[1], weights_b[2].shape[1]]
    bias_parts = [
        biases[: widths[0]],
        biases[widths[0] : widths[0] + widths[1]],
        biases[widths[0] + widths[1] :],
    ]
    row_mask = (jnp.arange(features.shape[0]) < counts[0]).astype(jnp.float32)
    inputs_list = [features]
    gelu_backs = []
    logits = None
    for which_layer in range(3):
        pre_act = layer_forward(
            inputs_list[which_layer], weights_b[which_layer], bias_parts[which_layer]
        )
        if which_layer < 2:
            activ, gelu_back = jax.vjp(jax.nn.gelu, pre_act)
            inputs_list.append(activ.astype(jnp.bfloat16))
            gelu_backs.append(gelu_back)
        else:
            logits = pre_act
    logp = jax.nn.log_softmax(logits, axis=-1)
    onehot = (labels[:, None] == jnp.arange(widths[2])[None, :]).astype(jnp.float32)
    target = (1.0 - smoothing) * onehot + smoothing / widths[2]
    worker_loss = jnp.sum(-jnp.sum(target * logp, axis=-1) * row_mask)
    upstream = -target * row_mask[:, None]
    grad_pre = upstream - jnp.exp(logp) * jnp.sum(upstream, axis=-1, keepdims=True)
    weight_grads = [None, None, None]
    bias_grads = [None, None, None]
    for which_layer in (2, 1, 0):
        weight_grads[which_layer], bias_grads[which_layer], grad_inputs = layer_backward(
            inputs_list[which_layer], weights_b[which_layer], grad_pre
        )
        if which_layer > 0:
            grad_pre = gelu_backs[which_layer - 1](grad_inputs)[0]
    resids = (resid6, resid7, resid8)
    noises = (noise6, noise7, noise8)
    accs = [weight_grads[k] + resids[k] for k in range(3)]
    clipped_list = []
    for acc in accs:
        bound = clip_width * jnp.sqrt(jnp.mean(acc * acc))
        clipped_list.append(jnp.clip(acc, -bound, bound))
    peak_list = lax.pmax(tuple(jnp.max(jnp.abs(clipped)) for clipped in clipped_list), BOTH)
    peak_list = [p + 1e-06 for p in peak_list]
    code_list = [dithered_code(clipped_list[k], peak_list[k], noises[k]) for k in range(3)]
    new_resids = [accs[k] - peak_list[k] * code_list[k] for k in range(3)]
    loss_total, image_total, bias_total = lax.psum(
        (worker_loss, jnp.sum(row_mask), jnp.concatenate(bias_grads)), BOTH
    )
    code_rows = [
        lax.psum_scatter(code, "wide", scatter_dimension=0, tiled=True) for code in code_list
    ]
    code_sums = lax.psum(tuple(code_rows), "grp")
    moments = (moment6, moment7, moment8)
    new_moments = [
        momentum_decay * moments[k] + peak_list[k] * code_sums[k] / image_total for k in range(3)
    ]
    full_moments = [
        lax.all_gather(moment, "wide", axis=0, tiled=True) for moment in new_moments
    ]
    row_block = lax.axis_index("wide")
    iterates = []
    for k in range(3):
        whole = full_moments[k]
        iterate = whole / (jnp.sqrt(jnp.sum(whole * whole)) + 1e-07)
        for step_num in range(NS_STEPS):
            iterate = schulz_step(iterate, gram_of(iterate))
        row_count = new_moments[k].shape[0]
        iterates.append(lax.dynamic_slice_in_dim(iterate, row_block * row_count, row_count, 0))
    new_weights = [
        masters[k] - muon_rate * (iterates[k] + decay_rate * masters[k]) for k in range(3)
    ]
    new_biases = adam_biases(biases, bias_first, bias_second, bias_total / image_total)
    return (
        *new_weights,
        *[weight.astype(jnp.bfloat16) for weight in new_weights],
        *new_moments,
        *new_resids,
        *new_biases,
        loss_total,
        image_total,
    )


ORDERS = ((1, 2, 4), (2, 1, 4))


def wide_perm(phase):
    return [
        (g * 8 + w, g * 8 + (w ^ ORDERS[g % 2][phase])) for g in range(4) for w in range(8)
    ]


def grp_perm(bit):
    return [(g * 8 + w, (g ^ bit) * 8 + w) for g in range(4) for w in range(8)]


def places(wide, core):
    result = []
    for place in range(8):
        masks = []
        for order in ORDERS:
            mask = 0
            for phase in range(3):
                if place & (4 >> phase):
                    mask |= order[phase]
            masks.append(mask)
        result.append(wide ^ jnp.where(core == 0, masks[0], masks[1]))
    return result


def gather_halves(own):
    first = lax.ppermute(own, BOTH, wide_perm(2))
    two = jnp.concatenate([own, first], axis=0)
    second = lax.ppermute(two, BOTH, wide_perm(1))
    four = jnp.concatenate([two, second], axis=0)
    third = lax.ppermute(four, BOTH, wide_perm(0))
    other_low = lax.ppermute(four, BOTH, grp_perm(1))
    other_high = lax.ppermute(third, BOTH, grp_perm(1))
    return four, third, other_low, other_high


def dims(contract_left, contract_right):
    return (((contract_left,), (contract_right,)), ((), ()))


def mxu(left, right, contract_left=1, contract_right=0):
    return lax.dot_general(
        left, right, dims(contract_left, contract_right), preferred_element_type=F32
    )


def split(value):
    high = value.astype(BF16)
    return high, (value - high.astype(F32)).astype(BF16)


def left_parts(value):
    high, rest = split(value)
    return jnp.concatenate([high, high, rest], axis=1)


def right_parts(value):
    high, rest = split(value)
    return jnp.concatenate([high, rest, high], axis=0)


def eye(size, dtype):
    rows = lax.broadcasted_iota(jnp.int32, (size, size), 0)
    cols = lax.broadcasted_iota(jnp.int32, (size, size), 1)
    return (rows == cols).astype(dtype)


def call(kernel, **options):
    limit = options.pop("vmem_limit_bytes", VMEM_LIMIT)
    return pl.pallas_call(
        kernel, compiler_params=pltpu.CompilerParams(vmem_limit_bytes=limit), **options
    )


def full_spec(shape):
    return pl.BlockSpec(shape, lambda *_: (0,) * len(shape))


def pack_kernel(rows6, h2, classes, tail, core_ref, w6_ref, w7_ref, w8t_ref, out_ref):
    out_ref[0, :rows6, :] = w6_ref[...].astype(BF16)
    rows7 = w7_ref.shape[0]
    out_ref[0, rows6:, :] = jnp.zeros((rows7, out_ref.shape[2]), BF16)
    out_ref[0, rows6:, :h2] = w7_ref[...].astype(BF16)
    rows8 = w8t_ref.shape[1]
    tall = mxu(eye(rows8, BF16), w8t_ref[...].astype(BF16), 1, 1)
    out_ref[0, rows6 : rows6 + rows8, tail : tail + classes] = tall.astype(BF16)


def pack_weights(core, weight6, weight7, weight8):
    h1 = weight6.shape[1]
    h2 = weight7.shape[1]
    classes = weight8.shape[1]
    rows6 = weight6.shape[0] // 2
    rows7 = weight7.shape[0] // 2
    tail = h1 - LANE
    return call(
        functools.partial(pack_kernel, rows6, h2, classes, tail),
        grid_spec=pltpu.PrefetchScalarGridSpec(
            num_scalar_prefetch=1,
            grid=(1,),
            in_specs=[
                pl.BlockSpec((rows6, h1), lambda i, c: (c[0], 0)),
                pl.BlockSpec((rows7, h2), lambda i, c: (c[0], 0)),
                full_spec((classes, weight8.shape[0])),
            ],
            out_specs=full_spec((1, rows6 + rows7, h1)),
        ),
        out_shape=jax.ShapeDtypeStruct((1, rows6 + rows7, h1), BF16),
        name="pack_weights",
    )(core[None], weight6, weight7, weight8.T)


def gelu_pair(pre):
    slope = 0.7978845608028654
    inner = slope * (pre + 0.044715 * pre * pre * pre)
    t = jnp.tanh(inner)
    value = 0.5 * pre * (1.0 + t)
    back = 0.5 * (1.0 + t) + 0.5 * pre * (1.0 - t * t) * slope * (1.0 + 3 * 0.044715 * pre * pre)
    return value, back


def worker_kernel(
    sizes,
    tile,
    table_ref,
    count_ref,
    own_low,
    own_high,
    other_low,
    other_high,
    feat_ref,
    label_ref,
    b6_ref,
    b7_ref,
    b8_ref,
    resid6_ref,
    resid7_ref,
    resid8_ref,
    acc6_ref,
    acc7_ref,
    acc8_ref,
    stats_ref,
    w6,
    w7,
    w8,
    hold,
    in_sem,
    out_sem,
):
    ins, h1, h2, classes, rows6, rows7, rows8, tail = sizes
    tiles = ins // tile

    def resid_copy(t):
        part = pl.ds(t * tile, tile)
        return pltpu.make_async_copy(resid6_ref.at[part], hold.at[part], in_sem.at[t])

    def acc_copy(t):
        part = pl.ds(t * tile, tile)
        return pltpu.make_async_copy(hold.at[part], acc6_ref.at[part], out_sem.at[t])

    for t in range(tiles):
        resid_copy(t).start()

    w8[...] = jnp.zeros(w8.shape, F32)
    for at, ref in enumerate((own_low, own_high, other_low, other_high)):
        for q in range(4):
            half = table_ref[at * 4 + q]
            position = half // 2
            w6[pl.ds(pl.multiple_of(half * rows6, 16), rows6), :] = ref[q, :rows6, :]
            w7[pl.ds(pl.multiple_of(half * rows7, 8), rows7), :] = ref[
                q, rows6 : rows6 + rows7, :h2
            ].astype(F32)
            w8[pl.ds(pl.multiple_of(position * rows8, 8), rows8), :] = ref[
                q, rows6 : rows6 + rows8, tail : tail + LANE
            ].astype(F32)
    w7_low = w7[...].astype(BF16)
    w8_low = w8[...].astype(BF16)

    rows = feat_ref.shape[0]
    row_mask = (lax.broadcasted_iota(jnp.int32, (rows, 1), 0) < count_ref[0]).astype(F32)
    lanes = lax.broadcasted_iota(jnp.int32, (rows, LANE), 1)
    valid = lanes < classes

    pre6 = mxu(feat_ref[...], w6[...]) + b6_ref[...]
    act6, back6 = gelu_pair(pre6)
    act6 = act6.astype(BF16)
    pre7 = mxu(act6, w7_low) + b7_ref[...]
    act7, back7 = gelu_pair(pre7)
    act7 = act7.astype(BF16)
    logits = jnp.where(valid, mxu(act7, w8_low) + b8_ref[...], -1e30)
    top = jnp.max(logits, axis=1, keepdims=True)
    shifted = logits - top
    logp = shifted - jnp.log(jnp.sum(jnp.exp(shifted), axis=1, keepdims=True))
    onehot = (label_ref[...] == lanes).astype(F32)
    target = jnp.where(valid, (1.0 - smoothing) * onehot + smoothing / classes, 0.0)
    loss = jnp.sum(-jnp.sum(target * jnp.where(valid, logp, 0.0), axis=1, keepdims=True) * row_mask)
    weight = jnp.sum(target, axis=1, keepdims=True)
    dlogits = (row_mask * (jnp.exp(logp) * weight - target)).astype(BF16)
    dpre7 = (mxu(dlogits, w8_low, 1, 1) * back7).astype(BF16)
    dpre6 = (mxu(dpre7, w7_low, 1, 1) * back6).astype(BF16)

    square6 = jnp.zeros((8, h1), F32)
    most6 = jnp.zeros((8, h1), F32)
    for t in range(tiles):
        part = slice(t * tile, (t + 1) * tile)
        grad = mxu(feat_ref[:, part], dpre6, 0, 0)
        resid_copy(t).wait()
        acc = hold[part, :] + grad
        hold[part, :] = acc
        acc_copy(t).start()
        square6 = square6 + jnp.sum((acc * acc).reshape(tile // 8, 8, h1), axis=0)
        most6 = jnp.maximum(most6, jnp.max(jnp.abs(acc).reshape(tile // 8, 8, h1), axis=0))
    acc7 = mxu(dpre7, act6, 0, 0) + resid7_ref[...]
    acc7_ref[...] = acc7
    acc8 = mxu(dlogits, act7, 0, 0)[:classes, :] + resid8_ref[...]
    acc8_ref[...] = acc8

    bound6 = clip_width * jnp.sqrt(jnp.sum(square6) * (1.0 / (ins * h1)))
    bound7 = clip_width * jnp.sqrt(jnp.sum(acc7 * acc7) * (1.0 / (h1 * h2)))
    bound8 = clip_width * jnp.sqrt(jnp.sum(acc8 * acc8) * (1.0 / (h2 * classes)))
    peak6 = jnp.minimum(jnp.max(most6), bound6)
    peak7 = jnp.minimum(jnp.max(jnp.abs(acc7)), bound7)
    peak8 = jnp.minimum(jnp.max(jnp.abs(acc8)), bound8)
    lane = lax.broadcasted_iota(jnp.int32, (1, LANE), 1)
    head = jnp.zeros((1, LANE), F32)
    count = count_ref[0].astype(F32)
    for k, value in enumerate((peak6, peak7, peak8, loss, count, bound6, bound7, bound8)):
        head = jnp.where(lane == k, value, head)
    db6 = jnp.sum(dpre6.astype(F32), axis=0, keepdims=True)
    db7 = jnp.sum(dpre7.astype(F32), axis=0, keepdims=True)
    db8 = jnp.sum(dlogits.astype(F32), axis=0, keepdims=True)
    db7 = jnp.concatenate([db7, jnp.zeros((1, 2 * LANE - h2), F32)], axis=1)
    tiled = jnp.concatenate(
        [head]
        + [db6[:, k * LANE : (k + 1) * LANE] for k in range(h1 // LANE)]
        + [db7[:, :LANE], db7[:, LANE:], db8, jnp.zeros((1, LANE), F32)],
        axis=0,
    )
    stats_ref[...] = jnp.broadcast_to(tiled[None], stats_ref.shape)
    for t in range(tiles):
        acc_copy(t).wait()


def code_of(acc, bound, scale, noise):
    ramp = jnp.minimum(jnp.abs(acc), bound) * scale - (
        noise.astype(F32) * (ramp_slope / noise_levels) + 0.5 * ramp_slope / noise_levels
    )
    ramp = jnp.clip(ramp, 0.0, 1.0)
    return jnp.where(acc < 0, -ramp, ramp)


def code_kernel(
    sizes,
    small,
    table_ref,
    stats_ref,
    mine_ref,
    acc6_ref,
    noise6_ref,
    acc7_ref,
    noise7_ref,
    acc8_ref,
    noise8_ref,
    *refs,
):
    ins, h1, h2, classes, rows6, rows7, rows8, tail = sizes
    if small:
        code_ref, resid6_ref, resid7_ref, resid8_ref, code7, code8, peaks = refs
    else:
        code_ref, resid6_ref, code7, code8, peaks = refs
    step = pl.program_id(0)

    @pl.when(step == 0)
    def _():
        most = jnp.max(stats_ref[:, 0, :], axis=0, keepdims=True)
        lane = lax.broadcasted_iota(jnp.int32, (1, LANE), 1)
        for k in range(3):
            peaks[k] = jnp.max(jnp.where(lane == k, most, 0.0)) + 1e-06
            peaks[3 + k] = jnp.max(jnp.where(lane == 5 + k, mine_ref[0, :1, :], 0.0))
        acc7 = acc7_ref[...]
        small7 = code_of(acc7, peaks[4], (1.0 + ramp_slope) / peaks[1], noise7_ref[...])
        acc8 = acc8_ref[...]
        small8 = code_of(acc8, peaks[5], (1.0 + ramp_slope) / peaks[2], noise8_ref[...])
        if small:
            resid7_ref[...] = acc7 - peaks[1] * small7
            resid8_ref[...] = acc8 - peaks[2] * small8
        code7[...] = mxu(eye(h1, BF16), small7.astype(BF16), 1, 1)
        code8[...] = jnp.zeros(code8.shape, F32)
        code8[:, :classes] = mxu(eye(h2, BF16), small8.astype(BF16), 1, 1)

    acc = acc6_ref[...]
    code = code_of(acc, peaks[3], (1.0 + ramp_slope) / peaks[0], noise6_ref[...])
    resid6_ref[...] = acc - peaks[0] * code
    code_ref[0, :rows6, :] = code.astype(BF16)
    half = table_ref[step]
    code_ref[0, rows6:, :] = jnp.zeros((rows7, h1), BF16)
    code_ref[0, rows6:, :h2] = code7[
        pl.ds(pl.multiple_of(half * rows7, 8), rows7), :
    ].astype(BF16)
    lead = (half % 2 == 0).astype(F32)
    code_ref[0, rows6 : rows6 + rows8, tail : tail + LANE] = (
        lead * code8[pl.ds(pl.multiple_of((half // 2) * rows8, 8), rows8), :]
    ).astype(BF16)


def code_call(sizes, small, table, stats, mine, acc6, noise6, acc7, noise7, acc8, noise8):
    ins, h1, h2, classes, rows6, rows7, rows8, tail = sizes
    block6 = pl.BlockSpec((rows6, h1), lambda i, t: (t[i], 0))
    out_shape = [
        jax.ShapeDtypeStruct((8, rows6 + rows7, h1), BF16),
        jax.ShapeDtypeStruct(acc6.shape, F32),
    ]
    out_specs = [pl.BlockSpec((1, rows6 + rows7, h1), lambda i, t: (i, 0, 0)), block6]
    if small:
        for acc in (acc7, acc8):
            out_shape.append(jax.ShapeDtypeStruct(acc.shape, F32))
            out_specs.append(full_spec(acc.shape))
    return call(
        functools.partial(code_kernel, sizes, small),
        grid_spec=pltpu.PrefetchScalarGridSpec(
            num_scalar_prefetch=1,
            grid=(8,),
            in_specs=[
                full_spec(stats.shape),
                pl.BlockSpec((1,) + mine.shape[1:], lambda i, t: (0, 0, 0)),
                block6,
                block6,
                full_spec(acc7.shape),
                full_spec(noise7.shape),
                full_spec(acc8.shape),
                full_spec(noise8.shape),
            ],
            out_specs=out_specs,
            scratch_shapes=[
                pltpu.VMEM((h1, h2), F32),
                pltpu.VMEM((h2, LANE), F32),
                pltpu.SMEM((6,), F32),
            ],
        ),
        out_shape=out_shape,
        input_output_aliases={3: 1},
        name="codes_sent" if small else "codes_kept",
    )(table, stats, mine, acc6, noise6, acc7, noise7, acc8, noise8)


def schulz_chain(gram, iterate):
    size = gram.shape[0]
    diagonal = eye(size, F32)
    norm = jnp.sqrt(jnp.sum(gram * diagonal)) + 1e-07
    inverse = 1.0 / norm
    gram = gram * (inverse * inverse)
    iterate = iterate * inverse

    def step(carry, last):
        gram, iterate = carry
        left = left_parts(gram)
        square = mxu(left, right_parts(gram))
        mixed = right_parts(coef_a * diagonal + coef_b * gram + coef_c * square)
        iterate = mxu(left_parts(iterate), mixed)
        if not last:
            gram = mxu(left_parts(mxu(left, mixed)), mixed)
        return gram, iterate

    return step, (gram, iterate)


def update_kernel(
    sizes,
    table_ref,
    core_ref,
    own_low,
    own_high,
    other_low,
    other_high,
    mine_ref,
    theirs_ref,
    w6_ref,
    w7_ref,
    w8_ref,
    new6_ref,
    new7_ref,
    new8_ref,
    low6_ref,
    low7_ref,
    low8_ref,
    mom6_ref,
    mom7_ref,
    mom8_ref,
    all6,
    all78,
):
    ins, h1, h2, classes, rows6, rows7, rows8, tail = sizes
    core = core_ref[0]

    for at, ref in enumerate((own_low, own_high, other_low, other_high)):
        for q in range(4):
            half = table_ref[at * 4 + q]
            all6[pl.ds(pl.multiple_of(half * rows6, 16), rows6), :] = ref[q, :rows6, :]
            all78[pl.ds(pl.multiple_of(half * rows7, 8), rows7), :] = ref[q, rows6:, :].astype(F32)
    gram6 = mxu(all6[...], all6[...], 0, 0)
    regions = all78[...].astype(BF16)
    gram78 = mxu(regions, regions, 0, 0)
    gram7 = gram78[:h2, :h2]
    gram8 = gram78[tail:, tail:]

    for at, ref in ((core, mine_ref), (1 - core, theirs_ref)):
        mom6_ref[pl.ds(pl.multiple_of(at * rows6, 8), rows6), :] = ref[0, :rows6, :]
        mom7_ref[pl.ds(pl.multiple_of(at * rows7, 8), rows7), :] = ref[
            0, rows6 : rows6 + rows7, :h2
        ]
    mom8 = jnp.where(
        core == 0,
        mine_ref[0, rows6 : rows6 + rows8, tail:],
        theirs_ref[0, rows6 : rows6 + rows8, tail:],
    )
    mom8_ref[...] = mom8[:, :classes]

    step6, carry6 = schulz_chain(gram6, mom6_ref[...])
    step7, carry7 = schulz_chain(gram7, mom7_ref[...])
    step8, carry8 = schulz_chain(gram8, mom8)

    for _ in range(NS_STEPS - 1):
        carry6 = step6(carry6, False)
        carry7 = step7(carry7, False)
        carry8 = step8(carry8, False)
    iterate6 = step6(carry6, True)[1]
    iterate7 = step7(carry7, True)[1]
    iterate8 = step8(carry8, True)[1][:, :classes]
    for iterate, w_ref, new_ref, low_ref in (
        (iterate6, w6_ref, new6_ref, low6_ref),
        (iterate7, w7_ref, new7_ref, low7_ref),
        (iterate8, w8_ref, new8_ref, low8_ref),
    ):
        master = w_ref[...]
        value = master - muon_rate * (iterate + decay_rate * master)
        new_ref[...] = value
        low_ref[...] = value.astype(BF16)


def paired_plan(
    features,
    labels,
    counts,
    weight6,
    weight7,
    weight8,
    moment6,
    moment7,
    moment8,
    resid6,
    resid7,
    resid8,
    noise6,
    noise7,
    noise8,
    biases,
    bias_first,
    bias_second,
):
    ins, h1 = resid6.shape
    h2, classes = resid8.shape
    rows6 = weight6.shape[0] // 2
    rows7 = weight7.shape[0] // 2
    rows8 = weight8.shape[0]
    tail = h1 - LANE
    sizes = (ins, h1, h2, classes, rows6, rows7, rows8, tail)
    devices = 32

    core = lax.axis_index("grp").astype(jnp.int32) % 2
    wide = lax.axis_index("wide").astype(jnp.int32)
    own = [position * 2 + core for position in places(wide, core)]
    other = [position * 2 + 1 - core for position in places(wide, 1 - core)]
    own_table = jnp.stack(own)
    other_table = jnp.stack(other)
    all_table = jnp.concatenate([own_table, other_table])

    halves = gather_halves(pack_weights(core, weight6, weight7, weight8))

    bias6 = biases[:h1].reshape(1, h1)
    bias7 = biases[h1 : h1 + h2].reshape(1, h2)
    bias8 = jnp.pad(biases[h1 + h2 :], (0, LANE - classes)).reshape(1, LANE)
    tile = 2 * LANE
    any_spec = pl.BlockSpec(memory_space=pl.ANY)
    smem_spec = pl.BlockSpec(memory_space=pltpu.SMEM)
    vmem_spec = pl.BlockSpec(memory_space=pltpu.VMEM)
    acc6, acc7, acc8, stats = call(
        functools.partial(worker_kernel, sizes, tile),
        in_specs=[smem_spec, smem_spec] + [vmem_spec] * 9 + [any_spec] + [vmem_spec] * 2,
        out_specs=[any_spec] + [vmem_spec] * 3,
        out_shape=[
            jax.ShapeDtypeStruct((ins, h1), F32),
            jax.ShapeDtypeStruct((h2, h1), F32),
            jax.ShapeDtypeStruct((classes, h2), F32),
            jax.ShapeDtypeStruct((devices, 8, LANE), F32),
        ],
        scratch_shapes=[
            pltpu.VMEM((ins, h1), BF16),
            pltpu.VMEM((h1, h2), F32),
            pltpu.VMEM((h2, LANE), F32),
            pltpu.VMEM((ins, h1), F32),
            pltpu.SemaphoreType.DMA((ins // tile,)),
            pltpu.SemaphoreType.DMA((ins // tile,)),
        ],
        name="worker",
    )(
        all_table,
        counts,
        *halves,
        features,
        labels.reshape(-1, 1),
        bias6,
        bias7,
        bias8,
        resid6,
        resid7.T,
        resid8.T,
    )

    all_stats = lax.all_to_all(stats, BOTH, 0, 0, tiled=True)

    sent, resid6_part, new_resid7, new_resid8 = code_call(
        sizes, True, other_table, all_stats, stats, acc6, noise6, acc7, noise7.T, acc8, noise8.T
    )
    kept, new_resid6 = code_call(
        sizes,
        False,
        own_table,
        all_stats,
        stats,
        resid6_part,
        noise6,
        acc7,
        noise7.T,
        acc8,
        noise8.T,
    )

    total = jnp.sum(all_stats, axis=0)
    peaks = jnp.max(all_stats[:, 0, :3], axis=0) + 1e-06
    loss_total = total[0, 3]
    image_total = total[0, 4]
    lanes6 = h1 // LANE
    bias_total = jnp.concatenate(
        [
            total[1 : 1 + lanes6].reshape(-1),
            total[1 + lanes6 : 3 + lanes6].reshape(-1)[:h2],
            total[3 + lanes6, :classes],
        ]
    )
    new_biases = adam_biases(biases, bias_first, bias_second, bias_total / image_total)

    got = lax.ppermute(sent, BOTH, grp_perm(1))
    part = kept.astype(F32)
    count = 8
    for phase in range(3):
        count = count // 2
        out = (part[count:] + got[count : 2 * count].astype(F32)).astype(BF16)
        next_got = lax.ppermute(out, BOTH, wide_perm(phase))
        part = part[:count] + got[:count].astype(F32)
        got = next_got
    mine = lax.optimization_barrier((part + got.astype(F32)).astype(BF16))
    theirs = lax.ppermute(mine, BOTH, grp_perm(2))
    code_sum = mine.astype(F32) + theirs.astype(F32)

    half6 = lax.dynamic_slice_in_dim(moment6, core * rows6, rows6, 0)
    half7 = lax.dynamic_slice_in_dim(moment7, core * rows7, rows7, 0)
    half8 = jnp.where(core == 0, moment8, 0.0)
    region = jnp.concatenate(
        [
            half7,
            jnp.zeros((rows7, tail - h2), F32),
            jnp.pad(half8, ((0, rows7 - rows8), (0, LANE - classes))),
        ],
        axis=1,
    )
    held = momentum_decay * jnp.concatenate([half6, region], axis=0)[None]
    rates = peaks / image_total
    row = lax.broadcasted_iota(jnp.int32, (1, rows6 + rows7, h1), 1)
    column = lax.broadcasted_iota(jnp.int32, (1, rows6 + rows7, h1), 2)
    rate = jnp.where(row < rows6, rates[0], jnp.where(column < h2, rates[1], rates[2]))
    moment = held + rate * code_sum
    moment_other = lax.ppermute(moment, BOTH, grp_perm(1))
    moments = gather_halves(moment.astype(BF16))

    updated = call(
        functools.partial(update_kernel, sizes),
        in_specs=[smem_spec] * 2 + [vmem_spec] * 9,
        out_specs=[vmem_spec] * 9,
        out_shape=[
            jax.ShapeDtypeStruct(weight6.shape, F32),
            jax.ShapeDtypeStruct(weight7.shape, F32),
            jax.ShapeDtypeStruct(weight8.shape, F32),
            jax.ShapeDtypeStruct(weight6.shape, BF16),
            jax.ShapeDtypeStruct(weight7.shape, BF16),
            jax.ShapeDtypeStruct(weight8.shape, BF16),
            jax.ShapeDtypeStruct(weight6.shape, F32),
            jax.ShapeDtypeStruct(weight7.shape, F32),
            jax.ShapeDtypeStruct(weight8.shape, F32),
        ],
        scratch_shapes=[pltpu.VMEM((ins, h1), BF16), pltpu.VMEM((16 * rows7, h1), F32)],
        name="update",
    )(all_table, core[None], *moments, moment, moment_other, weight6, weight7, weight8)

    return (
        *updated,
        new_resid6,
        new_resid7.T,
        new_resid8.T,
        *new_biases,
        loss_total,
        image_total,
    )


def on_device(*arrays):
    (ins, h1), (_, h2), (_, classes) = [array.shape for array in arrays[9:12]]
    rows6, rows7, rows8 = [array.shape[0] for array in arrays[3:6]]
    paired = (
        (lax.axis_size("grp"), lax.axis_size("wide")) == (4, 8)
        and rows6 % 32 == 0
        and rows7 % 16 == 0
        and rows8 % 8 == 0
        and rows8 <= rows7 // 2
        and h1 == 3 * LANE
        and h2 <= 2 * LANE
        and classes <= LANE
        and ins % (2 * LANE) == 0
    )
    return (paired_plan if paired else general_plan)(*arrays)


def solution(mesh):
    split_both = P(BOTH, None)
    split_wide = P("wide", None)
    return jax.shard_map(
        on_device,
        mesh=mesh,
        in_specs=(
            split_both,
            P(BOTH),
            P(BOTH),
            *[split_wide] * 6,
            *[split_both] * 6,
            P(),
            P(),
            P(),
        ),
        out_specs=(*[split_wide] * 9, *[split_both] * 3, P(), P(), P(), P(), P()),
        check_vma=False,
    )
```

time: 499 us -> 149 us (0.30); the launches traced: 491 us -> 148 us
  blocking collectives: 257 us -> 0 us
  matrix products: 96.6 us -> 0 us
  Pallas kernels: 0 us -> 37.1 us
  other arithmetic: 27.8 us -> 6.12 us
  between operations: 22.2 us -> 1.61 us
  starting transfers between devices: 0.21 us -> 18.7 us
  local copies, waits for them, and re-layouts: 30.8 us -> 16.1 us
  waiting for transfers between devices: 56 us -> 68.6 us
    all_gather x4 -> x0, blocking collectives: 127 us -> none  [the longest x1 32.3 us: on_device(): lax.all_gather(weight8.astype(jnp.bfloat16), 'wide', axis=0, tiled=True)]
    dot_general x53 -> x0, matrix products: 96.6 us -> none  [the longest x15 42.8 us: schulz_step(): return coef_a * iterate + jnp.dot(iterate, mixed, precision=highest)]
    ppermute x0 -> x16, waiting for transfers between devices: none -> 61 us  [the longest x3 18.3 us: paired_plan(): next_got = lax.ppermute(out, BOTH, wide_perm(phase))]
    psum x2 -> x0, blocking collectives: 52.8 us -> none  [the longest x1 41 us: on_device(): lax.psum((worker_loss, jnp.sum(row_mask), jnp.concatenate(bias_grads)), (...]
    pmax x1 -> x0, blocking collectives: 39.8 us -> none  [on_device(): lax.pmax((jnp.max(jnp.abs(clipped_list[0])), jnp.max(jnp.abs(clipped_list...]
    unnamed x1 -> x0, blocking collectives: 37.6 us -> none
    pallas_call x0 -> x5, Pallas kernels: none -> 37.1 us  [the longest x1 16.5 us: paired_plan(): call(functools.partial(update_kernel, sizes), in_specs=[smem_spec] * 2 +...]
    psum x1 -> x0, waiting for transfers between devices: 31.4 us -> none  [on_device(): code_sums = lax.psum((code_rows[0], code_rows[1], code_rows[2]), 'grp')]
  transfers between devices with their start and end apart: 5 -> 17, of which waited for: 2 -> 12; matrix products, arithmetic and copies ran while one was open for 9% -> 6% of each run, Pallas kernels for 0% -> 5%
where the time goes in v1:
time: 149 us; the launch traced here: 148 us
  waiting for transfers between devices  68.6 us (46%)
  Pallas kernels  37.1 us (25%)
  starting transfers between devices  18.7 us (13%)
  local copies, waits for them, and re-layouts  16.1 us (11%)
  other arithmetic  6.12 us (4%)
  between operations  1.61 us (1%)
    ppermute x3, waiting for transfers between devices, paired_plan(): next_got = lax.ppermute(out, BOTH, wide_perm(phase))  18.3 us
    pallas_call x1, Pallas kernels, paired_plan(): call(functools.partial(update_kernel, sizes), in_specs=[smem_spec] * 2 +...  16.5 us
    ppermute x2, waiting for transfers between devices, gather_halves(): third = lax.ppermute(four, BOTH, wide_perm(0))  15.8 us
    pallas_call x2, Pallas kernels, code_call(): call(functools.partial(code_kernel, sizes, small), grid_spec=pltpu.Prefet...  14.1 us
    ppermute x2, waiting for transfers between devices, gather_halves(): second = lax.ppermute(two, BOTH, wide_perm(1))  12.4 us
    ppermute x2, waiting for transfers between devices, gather_halves(): first = lax.ppermute(own, BOTH, wide_perm(2))  12 us
    unnamed x43, local copies, waits for them, and re-layouts  11.6 us
    all_to_all x1, waiting for transfers between devices, paired_plan(): all_stats = lax.all_to_all(stats, BOTH, 0, 0, tiled=True)  7.65 us
  transfers between devices with their start and end apart: 17, of which 12 were waited for; matrix products, arithmetic and copies ran while one was open for 6% of the time, Pallas kernels for 5%

profile of v1, /device:TPU:0, one launch (start us, length us, event | category | flops | bytes accessed | tf_op | source)
XLA Modules:
  0.0 148.3 jit_solution(4029743801679989740)
XLA Ops:
  0.7 1.1 copy-done.3
  1.7 0.8 copy-done.8
  2.5 0.7 copy-done.11
  3.4 4.0 %collective-permute-start = (bf16[1,168,384]{2,1,0:T(8,128)(2,1)S(1)}, bf16[1,168,384]{2,1,0:T(8,128)(2,1)S(1)}, u32[]{:S(2)}, u32[]{:S(2)}) collective-permute-start(bf16[1,168,384]{2,1,0:T(8,128)(2,1)S(1)} %pack_weights.1), channel_id=1, source_target_pairs={{0,4},{1,5},{2,6},{3,7},{4,0},{5,1},{6,2},{7,3},{8,12},{9,13},{10,... | collective-permute-start | bytes 387080 | tf_op jit(solution)/shard_map/ppermute | solution.py:211
  7.4 6.2 %collective-permute-done = bf16[1,168,384]{2,1,0:T(8,128)(2,1)S(1)} collective-permute-done((bf16[1,168,384]{2,1,0:T(8,128)(2,1)S(1)}, bf16[1,168,384]{2,1,0:T(8,128)(2,1)S(1)}, u32[]{:S(2)}, u32[]{:S(2)}) %collective-permute-start) | collective-permute-done | bytes 129056 | tf_op jit(solution)/shard_map/ppermute | solution.py:211
  13.7 0.8 collective-permute-start.1
  14.4 5.6 %collective-permute-done.1 = bf16[2,168,384]{2,1,0:T(8,128)(2,1)S(1)} collective-permute-done((bf16[2,168,384]{2,1,0:T(8,128)(2,1)S(1)}, bf16[2,168,384]{2,1,0:T(8,128)(2,1)S(1)}, u32[]{:S(2)}, u32[]{:S(2)}) %collective-permute-start.1) | collective-permute-done | bytes 258080 | tf_op jit(solution)/shard_map/ppermute | solution.py:213
  20.1 1.6 %collective-permute-start.2 = (bf16[4,168,384]{2,1,0:T(8,128)(2,1)S(1)}, bf16[4,168,384]{2,1,0:T(8,128)(2,1)S(1)}, u32[]{:S(2)}, u32[]{:S(2)}) collective-permute-start(bf16[4,168,384]{2,1,0:T(8,128)(2,1)S(1)} %pad_maximum_fusion.own_low), channel_id=1, source_target_pairs={{0,1},{1,0},{2,3},{3,2},{4,5},{5,4},{6,7},{7,6},{8,10},{9,11},{10,... | collective-permute-start | bytes 1548296 | tf_op jit(solution)/shard_map/ppermute | solution.py:215
  21.7 7.5 %collective-permute-done.2.own_high = bf16[4,168,384]{2,1,0:T(8,128)(2,1)S(1)} collective-permute-done((bf16[4,168,384]{2,1,0:T(8,128)(2,1)S(1)}, bf16[4,168,384]{2,1,0:T(8,128)(2,1)S(1)}, u32[]{:S(2)}, u32[]{:S(2)}) %collective-permute-start.2) | collective-permute-done | bytes 516128 | tf_op jit(solution)/shard_map/ppermute | solution.py:215
  29.3 0.7 slice.75
  30.0 0.7 slice.76
  30.7 0.8 slice.77
  32.1 0.8 copy.43.label_ref
  33.0 1.2 copy-done.6
  34.2 1.0 copy-done.7
  35.1 0.7 copy-done.13
  35.9 6.3 %worker.1 = (f32[2304,384]{1,0:T(8,128)}, f32[192,384]{1,0:T(8,128)S(1)}, f32[10,192]{1,0:T(8,128)S(1)}, f32[32,8,128]{2,1,0:T(8,128)}) custom-call(s32[16]{0:T(128)S(1)} %concatenate.38.table_ref, s32[1]{0:T(128)S(6)} %copy.50.count_ref, bf16[4,168,384]{2,1,0:T(8,128)(2,1)S(1)} %pad_maximum_fusion.own_low, ...), custom_call_target="tpu_custom_call" | custom-call | tf_op jit(solution)/shard_map/worker/pallas_call | solution.py:670
  42.2 5.9 %all-to-all-start = ((f32[32,8,128]{2,1,0:T(8,128)}), f32[32,8,128]{2,1,0:T(8,128)S(1)}, u32[]{:S(2)}, u32[]{:S(2)}) async-start(f32[32,8,128]{2,1,0:T(8,128)} %get-tuple-element.36.mine_ref), calls=%async_computation | async-start | bytes 262144 | tf_op jit(solution)/shard_map/all_to_all | solution.py:703
  48.2 7.7 %all-to-all-done.stats_ref = f32[32,8,128]{2,1,0:T(8,128)S(1)} async-done(((f32[32,8,128]{2,1,0:T(8,128)}), f32[32,8,128]{2,1,0:T(8,128)S(1)}, u32[]{:S(2)}, u32[]{:S(2)}) %all-to-all-start) | async-done | bytes 131104 | tf_op jit(solution)/shard_map/all_to_all | solution.py:703
  55.9 2.0 %copy-done.1 = s32[2304,384]{1,0:T(8,128)S(1)} copy-done((s32[2304,384]{1,0:T(8,128)S(1)}, s32[2304,384]{1,0:T(8,128)}, u32[]{:S(2)}) %copy-start.1) | copy-done | bytes 3538968
  57.9 7.1 %codes_sent.1 = (bf16[8,168,384]{2,1,0:T(8,128)(2,1)S(1)}, f32[2304,384]{1,0:T(8,128)}, f32[192,384]{1,0:T(8,128)}, f32[10,192]{1,0:T(8,128)}) custom-call(s32[8]{0:T(128)S(1)} %stack.71.table_ref, f32[32,8,128]{2,1,0:T(8,128)S(1)} %all-to-all-done.stats_ref, f32[32,8,128]{2,1,0:T(8,128)} %get-tuple-element.36.mine_ref, ...), custom_call_target="tpu_custom_call", output_to_operand_aliasing={{1}: (3, {})} | custom-call | tf_op jit(solution)/shard_map/codes_sent/pallas_call | solution.py:502
  65.4 2.0 %copy-done.2 = s32[2304,384]{1,0:T(8,128)S(1)} copy-done((s32[2304,384]{1,0:T(8,128)S(1)}, s32[2304,384]{1,0:T(8,128)}, u32[]{:S(2)}) %copy-start.2) | copy-done | bytes 3538968
  67.3 7.0 %codes_kept.1 = (bf16[8,168,384]{2,1,0:T(8,128)(2,1)S(1)}, f32[2304,384]{1,0:T(8,128)}) custom-call(s32[8]{0:T(128)S(1)} %stack.70.table_ref, f32[32,8,128]{2,1,0:T(8,128)S(1)} %all-to-all-done.stats_ref, f32[32,8,128]{2,1,0:T(8,128)} %get-tuple-element.36.mine_ref, f32[2304,384]{1,0:T(8,128)} %get-tuple-element.40.acc6_ref, ...), custom_call_target="tpu_custom_call", output_to_operand_aliasing={{1}: (3, {})} | custom-call | tf_op jit(solution)/shard_map/codes_kept/pallas_call | solution.py:502
  74.5 1.4 fusion
  76.1 1.3 collective-permute-start.6
  77.4 7.8 %collective-permute-done.6 = bf16[4,168,384]{2,1,0:T(8,128)(2,1)S(1)} collective-permute-done((bf16[4,168,384]{2,1,0:T(8,128)(2,1)S(1)}, bf16[4,168,384]{2,1,0:T(8,128)(2,1)S(1)}, u32[]{:S(2)}, u32[]{:S(2)}) %collective-permute-start.6) | collective-permute-done | bytes 516128 | tf_op jit(solution)/shard_map/ppermute | solution.py:742
  85.3 1.0 collective-permute-start.7
  86.3 0.6 fusion.12
  87.0 4.7 %collective-permute-done.7 = bf16[2,168,384]{2,1,0:T(8,128)(2,1)S(1)} collective-permute-done((bf16[2,168,384]{2,1,0:T(8,128)(2,1)S(1)}, bf16[2,168,384]{2,1,0:T(8,128)(2,1)S(1)}, u32[]{:S(2)}, u32[]{:S(2)}) %collective-permute-start.7) | collective-permute-done | bytes 258080 | tf_op jit(solution)/shard_map/ppermute | solution.py:742
  91.8 1.4 collective-permute-start.8
  93.2 0.6 add_divide_fusion
  93.9 5.7 %collective-permute-done.8 = bf16[1,168,384]{2,1,0:T(8,128)(2,1)S(1)} collective-permute-done((bf16[1,168,384]{2,1,0:T(8,128)(2,1)S(1)}, bf16[1,168,384]{2,1,0:T(8,128)(2,1)S(1)}, u32[]{:S(2)}, u32[]{:S(2)}) %collective-permute-start.8) | collective-permute-done | bytes 129056 | tf_op jit(solution)/shard_map/ppermute | solution.py:742
  99.6 1.0 collective-permute-start.9
  100.6 0.6 fusion.13
  101.2 1.3 fusion.8
  102.5 2.1 %collective-permute-done.9 = bf16[1,168,384]{2,1,0:T(8,128)(2,1)S(1)} collective-permute-done((bf16[1,168,384]{2,1,0:T(8,128)(2,1)S(1)}, bf16[1,168,384]{2,1,0:T(8,128)(2,1)S(1)}, u32[]{:S(2)}, u32[]{:S(2)}) %collective-permute-start.9) | collective-permute-done | bytes 129056 | tf_op jit(solution)/shard_map/ppermute | solution.py:746
  104.6 0.8 fusion.10
  105.5 5.8 %collective-permute-done.10 = bf16[1,168,384]{2,1,0:T(8,128)(2,1)S(1)} collective-permute-done((bf16[1,168,384]{2,1,0:T(8,128)(2,1)S(1)}, bf16[1,168,384]{2,1,0:T(8,128)(2,1)S(1)}, u32[]{:S(2)}, u32[]{:S(2)}) %collective-permute-start.10) | collective-permute-done | bytes 129056 | tf_op jit(solution)/shard_map/ppermute | solution.py:211
  111.4 6.8 %collective-permute-done.11 = bf16[2,168,384]{2,1,0:T(8,128)(2,1)S(1)} collective-permute-done((bf16[2,168,384]{2,1,0:T(8,128)(2,1)S(1)}, bf16[2,168,384]{2,1,0:T(8,128)(2,1)S(1)}, u32[]{:S(2)}, u32[]{:S(2)}) %collective-permute-start.11) | collective-permute-done | bytes 258080 | tf_op jit(solution)/shard_map/ppermute | solution.py:213
  118.3 0.8 collective-permute-start.12
  119.2 8.2 %collective-permute-done.12.own_high = bf16[4,168,384]{2,1,0:T(8,128)(2,1)S(1)} collective-permute-done((bf16[4,168,384]{2,1,0:T(8,128)(2,1)S(1)}, bf16[4,168,384]{2,1,0:T(8,128)(2,1)S(1)}, u32[]{:S(2)}, u32[]{:S(2)}) %collective-permute-start.12) | collective-permute-done | bytes 516128 | tf_op jit(solution)/shard_map/ppermute | solution.py:215
  127.4 0.5 collective-permute-start.15
  128.0 1.3 multiply_subtract_fusion
  129.3 0.4 collective-permute-done.15.theirs_ref
  129.7 16.5 %update.1 = (f32[288,384]{1,0:T(8,128)}, f32[48,192]{1,0:T(8,128)}, f32[24,10]{1,0:T(8,128)S(1)}, bf16[288,384]{1,0:T(8,128)(2,1)}, bf16[48,192]{1,0:T(8,128)(2,...) custom-call(s32[16]{0:T(128)S(1)} %concatenate.38.table_ref, ...), custom_call_target="tpu_custom_call" | custom-call | tf_op jit(solution)/shard_map/update/pallas_call | solution.py:769
  146.2 0.7 copy.45
  146.9 0.7 copy.46
  147.6 0.7 copy.47
  (70 shorter events, 1.7 us)
Async XLA Ops:
  0.7 64.7 %copy-start = (f32[288,384]{1,0:T(8,128)S(1)}, f32[288,384]{1,0:T(8,128)}, u32[]{:S(2)}) copy-start(f32[288,384]{1,0:T(8,128)} %param.24) | copy-start | bytes 1327108
  0.7 1.1 copy-start.3
  1.7 0.8 copy-start.8
  2.5 0.7 copy-start.11
  3.4 10.3 %collective-permute-start = (bf16[1,168,384]{2,1,0:T(8,128)(2,1)S(1)}, bf16[1,168,384]{2,1,0:T(8,128)(2,1)S(1)}, u32[]{:S(2)}, u32[]{:S(2)}) collective-permute-start(bf16[1,168,384]{2,1,0:T(8,128)(2,1)S(1)} %pack_weights.1), channel_id=1, source_target_pairs={{0,4},{1,5},{2,6},{3,7},{4,0},{5,1},{6,2},{7,3},{8,12},{9,13},{10,... | collective-permute-start | bytes 387080 | tf_op jit(solution)/shard_map/ppermute | solution.py:211
  13.7 6.4 %collective-permute-start.1 = (bf16[2,168,384]{2,1,0:T(8,128)(2,1)S(1)}, bf16[2,168,384]{2,1,0:T(8,128)(2,1)S(1)}, u32[]{:S(2)}, u32[]{:S(2)}) collective-permute-start(bf16[2,168,384]{2,1,0:T(8,128)(2,1)S(1)} %pad_maximum_fusion.2), channel_id=1, source_target_pairs={{0,2},{1,3},{2,0},{3,1},{4,6},{5,7},{6,4},{7,5},{8,9},{9,8},{10,11... | collective-permute-start | bytes 774152 | tf_op jit(solution)/shard_map/ppermute | solution.py:213
  20.1 9.2 %collective-permute-start.2 = (bf16[4,168,384]{2,1,0:T(8,128)(2,1)S(1)}, bf16[4,168,384]{2,1,0:T(8,128)(2,1)S(1)}, u32[]{:S(2)}, u32[]{:S(2)}) collective-permute-start(bf16[4,168,384]{2,1,0:T(8,128)(2,1)S(1)} %pad_maximum_fusion.own_low), channel_id=1, source_target_pairs={{0,1},{1,0},{2,3},{3,2},{4,5},{5,4},{6,7},{7,6},{8,10},{9,11},{10,... | collective-permute-start | bytes 1548296 | tf_op jit(solution)/shard_map/ppermute | solution.py:215
  21.7 11.3 %collective-permute-start.3 = (bf16[4,168,384]{2,1,0:T(8,128)(2,1)S(1)}, bf16[4,168,384]{2,1,0:T(8,128)(2,1)S(1)}, u32[]{:S(2)}, u32[]{:S(2)}) collective-permute-start(bf16[4,168,384]{2,1,0:T(8,128)(2,1)S(1)} %pad_maximum_fusion.own_low), channel_id=1, source_target_pairs={{0,8},{1,9},{2,10},{3,11},{4,12},{5,13},{6,14},{7,15},{8,0},{9,1},... | collective-permute-start | bytes 1548296 | tf_op jit(solution)/shard_map/ppermute | solution.py:216
  29.3 3.7 %collective-permute-start.4 = (bf16[4,168,384]{2,1,0:T(8,128)(2,1)S(1)}, bf16[4,168,384]{2,1,0:T(8,128)(2,1)S(1)}, u32[]{:S(2)}, u32[]{:S(2)}) collective-permute-start(bf16[4,168,384]{2,1,0:T(8,128)(2,1)S(1)} %collective-permute-done.2.own_high), channel_id=1, source_target_pairs={{0,8},{1,9},{2,10},{3,11},{4,12},{5,13},{6,14},{7,15},{8,0},{9,1},... | collective-permute-start | bytes 1548296 | tf_op jit(solution)/shard_map/ppermute | solution.py:217
  33.0 1.2 copy-start.6
  34.2 1.0 copy-start.7
  35.1 0.7 copy-start.13
  35.9 20.0 %copy-start.5 = (s32[384,192]{0,1:T(8,128)S(1)}, s32[384,192]{0,1:T(8,128)}, u32[]{:S(2)}) copy-start(s32[384,192]{0,1:T(8,128)} %param.31) | copy-start | bytes 884740
  35.9 20.0 %copy-start.10 = (s32[192,10]{0,1:T(8,128)S(1)}, s32[192,10]{0,1:T(8,128)}, u32[]{:S(2)}) copy-start(s32[192,10]{0,1:T(8,128)} %param.32) | copy-start | bytes 23044
  42.2 13.6 %all-to-all-start = ((f32[32,8,128]{2,1,0:T(8,128)}), f32[32,8,128]{2,1,0:T(8,128)S(1)}, u32[]{:S(2)}, u32[]{:S(2)}) async-start(f32[32,8,128]{2,1,0:T(8,128)} %get-tuple-element.36.mine_ref), calls=%async_computation | async-start | bytes 262144 | tf_op jit(solution)/shard_map/all_to_all | solution.py:703
  55.9 2.0 %copy-start.1 = (s32[2304,384]{1,0:T(8,128)S(1)}, s32[2304,384]{1,0:T(8,128)}, u32[]{:S(2)}) copy-start(s32[2304,384]{1,0:T(8,128)} %noise6_ref.3) | copy-start | bytes 10616836
  57.9 7.3 %copy-start.16 = (f32[24,10]{0,1:T(8,128)S(1)}, f32[24,10]{0,1:T(8,128)}, u32[]{:S(2)}) copy-start(f32[24,10]{0,1:T(8,128)} %param.26) | copy-start | bytes 2884
  65.0 9.6 %collective-permute-start.5 = (bf16[8,168,384]{2,1,0:T(8,128)(2,1)S(1)}, bf16[8,168,384]{2,1,0:T(8,128)(2,1)}, u32[]{:S(2)}, u32[]{:S(2)}) collective-permute-start(bf16[8,168,384]{2,1,0:T(8,128)(2,1)S(1)} %get-tuple-element.42), channel_id=1, source_target_pairs={{0,8},{1,9},{2,10},{3,11},{4,12},{5,13},{6,14},{7,15},{8,0},{9,1},... | collective-permute-start | bytes 3096584 | tf_op jit(solution)/shard_map/ppermute | solution.py:736
  65.3 2.0 %copy-start.2 = (s32[2304,384]{1,0:T(8,128)S(1)}, s32[2304,384]{1,0:T(8,128)}, u32[]{:S(2)}) copy-start(s32[2304,384]{1,0:T(8,128)} %noise6_ref.3) | copy-start | bytes 10616836
  74.4 3.0 %copy-start.15 = (f32[48,192]{1,0:T(8,128)S(1)}, f32[48,192]{1,0:T(8,128)}, u32[]{:S(2)}) copy-start(f32[48,192]{1,0:T(8,128)} %param.25) | copy-start | bytes 110596
  76.0 43.1 %copy-start.12 = (f32[24,10]{0,1:T(8,128)S(1)}, f32[24,10]{0,1:T(8,128)}, u32[]{:S(2)}) copy-start(f32[24,10]{0,1:T(8,128)} %param.23) | copy-start | bytes 2884
  76.0 52.0 %copy-start.14 = (f32[586]{0:T(1024)S(1)}, f32[586]{0:T(1024)}, u32[]{:S(2)}) copy-start(f32[586]{0:T(1024)} %param.33) | copy-start | bytes 7036
  76.0 51.9 %copy-start.17 = (f32[586]{0:T(1024)S(1)}, f32[586]{0:T(1024)}, u32[]{:S(2)}) copy-start(f32[586]{0:T(1024)} %param.34) | copy-start | bytes 7036
  76.0 51.9 %copy-start.18 = (f32[586]{0:T(1024)S(1)}, f32[586]{0:T(1024)}, u32[]{:S(2)}) copy-start(f32[586]{0:T(1024)} %param.35) | copy-start | bytes 7036
  76.0 53.7 %copy-start.4 = (f32[288,384]{1,0:T(8,128)S(1)}, f32[288,384]{1,0:T(8,128)}, u32[]{:S(2)}) copy-start(f32[288,384]{1,0:T(8,128)} %w6_ref.3) | copy-start | bytes 1327108
  76.0 53.7 %copy-start.9 = (f32[48,192]{1,0:T(8,128)S(1)}, f32[48,192]{1,0:T(8,128)}, u32[]{:S(2)}) copy-start(f32[48,192]{1,0:T(8,128)} %w7_ref.3) | copy-start | bytes 110596
  76.1 9.2 %collective-permute-start.6 = (bf16[4,168,384]{2,1,0:T(8,128)(2,1)S(1)}, bf16[4,168,384]{2,1,0:T(8,128)(2,1)S(1)}, u32[]{:S(2)}, u32[]{:S(2)}) collective-permute-start(bf16[4,168,384]{2,1,0:T(8,128)(2,1)S(1)} %get-tuple-element.94), channel_id=1, source_target_pairs={{0,1},{1,0},{2,3},{3,2},{4,5},{5,4},{6,7},{7,6},{8,10},{9,11},{10,... | collective-permute-start | bytes 1548296 | tf_op jit(solution)/shard_map/ppermute | solution.py:742
  85.3 6.4 %collective-permute-start.7 = (bf16[2,168,384]{2,1,0:T(8,128)(2,1)S(1)}, bf16[2,168,384]{2,1,0:T(8,128)(2,1)S(1)}, u32[]{:S(2)}, u32[]{:S(2)}) collective-permute-start(bf16[2,168,384]{2,1,0:T(8,128)(2,1)S(1)} %get-tuple-element.96), channel_id=1, source_target_pairs={{0,2},{1,3},{2,0},{3,1},{4,6},{5,7},{6,4},{7,5},{8,9},{9,8},{10,11... | collective-permute-start | bytes 774152 | tf_op jit(solution)/shard_map/ppermute | solution.py:742
  91.8 7.8 %collective-permute-start.8 = (bf16[1,168,384]{2,1,0:T(8,128)(2,1)S(1)}, bf16[1,168,384]{2,1,0:T(8,128)(2,1)S(1)}, u32[]{:S(2)}, u32[]{:S(2)}) collective-permute-start(bf16[1,168,384]{2,1,0:T(8,128)(2,1)S(1)} %fusion.2), channel_id=1, source_target_pairs={{0,4},{1,5},{2,6},{3,7},{4,0},{5,1},{6,2},{7,3},{8,12},{9,13},{10,... | collective-permute-start | bytes 387080 | tf_op jit(solution)/shard_map/ppermute | solution.py:742
  99.6 5.0 %collective-permute-start.9 = (bf16[1,168,384]{2,1,0:T(8,128)(2,1)S(1)}, bf16[1,168,384]{2,1,0:T(8,128)(2,1)S(1)}, u32[]{:S(2)}, u32[]{:S(2)}) collective-permute-start(bf16[1,168,384]{2,1,0:T(8,128)(2,1)S(1)} %fusion.4), channel_id=1, source_target_pairs={{0,16},{1,17},{2,18},{3,19},{4,20},{5,21},{6,22},{7,23},{8,24},{9,... | collective-permute-start | bytes 387080 | tf_op jit(solution)/shard_map/ppermute | solution.py:746
  105.4 5.9 %collective-permute-start.10 = (bf16[1,168,384]{2,1,0:T(8,128)(2,1)S(1)}, bf16[1,168,384]{2,1,0:T(8,128)(2,1)S(1)}, u32[]{:S(2)}, u32[]{:S(2)}) collective-permute-start(bf16[1,168,384]{2,1,0:T(8,128)(2,1)S(1)} %get-tuple-element.92), channel_id=1, source_target_pairs={{0,4},{1,5},{2,6},{3,7},{4,0},{5,1},{6,2},{7,3},{8,12},{9,13},{10,... | collective-permute-start | bytes 387080 | tf_op jit(solution)/shard_map/ppermute | solution.py:211
  111.3 6.9 %collective-permute-start.11 = (bf16[2,168,384]{2,1,0:T(8,128)(2,1)S(1)}, bf16[2,168,384]{2,1,0:T(8,128)(2,1)S(1)}, u32[]{:S(2)}, u32[]{:S(2)}) collective-permute-start(bf16[2,168,384]{2,1,0:T(8,128)(2,1)S(1)} %pad_maximum_fusion.3), channel_id=1, source_target_pairs={{0,2},{1,3},{2,0},{3,1},{4,6},{5,7},{6,4},{7,5},{8,9},{9,8},{10,11... | collective-permute-start | bytes 774152 | tf_op jit(solution)/shard_map/ppermute | solution.py:213
  118.3 9.2 %collective-permute-start.12 = (bf16[4,168,384]{2,1,0:T(8,128)(2,1)S(1)}, bf16[4,168,384]{2,1,0:T(8,128)(2,1)S(1)}, u32[]{:S(2)}, u32[]{:S(2)}) collective-permute-start(bf16[4,168,384]{2,1,0:T(8,128)(2,1)S(1)} %pad_maximum_fusion.1.own_low), channel_id=1, source_target_pairs={{0,1},{1,0},{2,3},{3,2},{4,5},{5,4},{6,7},{7,6},{8,10},{9,11},{10,... | collective-permute-start | bytes 1548296 | tf_op jit(solution)/shard_map/ppermute | solution.py:215
  119.2 10.5 %collective-permute-start.13 = (bf16[4,168,384]{2,1,0:T(8,128)(2,1)S(1)}, bf16[4,168,384]{2,1,0:T(8,128)(2,1)S(1)}, u32[]{:S(2)}, u32[]{:S(2)}) collective-permute-start(bf16[4,168,384]{2,1,0:T(8,128)(2,1)S(1)} %pad_maximum_fusion.1.own_low), channel_id=1, source_target_pairs={{0,8},{1,9},{2,10},{3,11},{4,12},{5,13},{6,14},{7,15},{8,0},{9,1},... | collective-permute-start | bytes 1548296 | tf_op jit(solution)/shard_map/ppermute | solution.py:216
  127.4 2.3 %collective-permute-start.14 = (bf16[4,168,384]{2,1,0:T(8,128)(2,1)S(1)}, bf16[4,168,384]{2,1,0:T(8,128)(2,1)S(1)}, u32[]{:S(2)}, u32[]{:S(2)}) collective-permute-start(bf16[4,168,384]{2,1,0:T(8,128)(2,1)S(1)} %collective-permute-done.12.own_high), channel_id=1, source_target_pairs={{0,8},{1,9},{2,10},{3,11},{4,12},{5,13},{6,14},{7,15},{8,0},{9,1},... | collective-permute-start | bytes 1548296 | tf_op jit(solution)/shard_map/ppermute | solution.py:217
  127.4 2.3 %collective-permute-start.15 = (f32[1,168,384]{2,1,0:T(8,128)S(1)}, f32[1,168,384]{2,1,0:T(8,128)S(1)}, u32[]{:S(2)}, u32[]{:S(2)}) collective-permute-start(f32[1,168,384]{2,1,0:T(8,128)S(1)} %get-tuple-element.93.mine_ref), channel_id=1, source_target_pairs={{0,8},{1,9},{2,10},{3,11},{4,12},{5,13},{6,14},{7,15},{8,0},{9,1},... | collective-permute-start | bytes 774152 | tf_op jit(solution)/shard_map/ppermute | solution.py:766

commit v2 on v0

v2 whole, which is shorter than its diff:
```python
import functools

import jax
import jax.numpy as jnp
from jax import lax
from jax.experimental import pallas as pl
from jax.experimental.pallas import tpu as pltpu
from jax.sharding import PartitionSpec as P

NS_STEPS = 5
ADAM_STEP = 10


highest = lax.Precision.HIGHEST
smoothing = 0.1
clip_width = 2.5
noise_levels = 1024.0
ramp_slope = 2.0
momentum_decay = 0.95
muon_rate = 0.6
decay_rate = 0.01
coef_a = 3.4445
coef_b = -4.775
coef_c = 2.0315
beta_first = 0.9
beta_second = 0.999
bias_rate = 0.05
adam_eps = 1e-08

F32 = jnp.float32
BF16 = jnp.bfloat16
LANE = 128
BOTH = ("grp", "wide")


def dithered_code(clipped, peak, noise):
    ratio = jnp.abs(clipped) / peak
    dither = (noise.astype(jnp.float32) + 0.5) / noise_levels
    return jnp.sign(clipped) * jnp.clip(ramp_slope * (ratio - dither) + ratio, 0.0, 1.0)


def gram_of(iterate):
    return jnp.dot(iterate.T, iterate, precision=highest)


def schulz_step(iterate, gram_matrix):
    mixed = coef_b * gram_matrix + coef_c * jnp.dot(gram_matrix, gram_matrix, precision=highest)
    return coef_a * iterate + jnp.dot(iterate, mixed, precision=highest)


def layer_forward(inputs_b, weight_b, bias_part):
    return jnp.dot(inputs_b, weight_b, preferred_element_type=jnp.float32) + bias_part


def layer_backward(inputs_b, weight_b, grad_pre):
    grad_low = grad_pre.astype(jnp.bfloat16)
    weight_grad = jnp.einsum("ri,ro->io", inputs_b, grad_low, preferred_element_type=jnp.float32)
    bias_grad = jnp.sum(grad_low.astype(jnp.float32), axis=0)
    grad_inputs = jnp.einsum("ro,io->ri", grad_low, weight_b, preferred_element_type=jnp.float32)
    return (weight_grad, bias_grad, grad_inputs)


def adam_biases(biases, bias_first, bias_second, bias_grad):
    first_new = beta_first * bias_first + (1.0 - beta_first) * bias_grad
    second_new = beta_second * bias_second + (1.0 - beta_second) * bias_grad * bias_grad
    first_hat = first_new / (1.0 - beta_first**ADAM_STEP)
    second_hat = second_new / (1.0 - beta_second**ADAM_STEP)
    biases_new = biases - bias_rate * (
        first_hat / (jnp.sqrt(second_hat) + adam_eps) + decay_rate * biases
    )
    return biases_new, first_new, second_new


def general_plan(
    features,
    labels,
    counts,
    weight6,
    weight7,
    weight8,
    moment6,
    moment7,
    moment8,
    resid6,
    resid7,
    resid8,
    noise6,
    noise7,
    noise8,
    biases,
    bias_first,
    bias_second,
):
    masters = (weight6, weight7, weight8)
    weights_b = [
        lax.all_gather(weight.astype(jnp.bfloat16), "wide", axis=0, tiled=True)
        for weight in masters
    ]
    widths = [weights_b[0].shape[1], weights_b[1].shape[1], weights_b[2].shape[1]]
    bias_parts = [
        biases[: widths[0]],
        biases[widths[0] : widths[0] + widths[1]],
        biases[widths[0] + widths[1] :],
    ]
    row_mask = (jnp.arange(features.shape[0]) < counts[0]).astype(jnp.float32)
    inputs_list = [features]
    gelu_backs = []
    logits = None
    for which_layer in range(3):
        pre_act = layer_forward(
            inputs_list[which_layer], weights_b[which_layer], bias_parts[which_layer]
        )
        if which_layer < 2:
            activ, gelu_back = jax.vjp(jax.nn.gelu, pre_act)
            inputs_list.append(activ.astype(jnp.bfloat16))
            gelu_backs.append(gelu_back)
        else:
            logits = pre_act
    logp = jax.nn.log_softmax(logits, axis=-1)
    onehot = (labels[:, None] == jnp.arange(widths[2])[None, :]).astype(jnp.float32)
    target = (1.0 - smoothing) * onehot + smoothing / widths[2]
    worker_loss = jnp.sum(-jnp.sum(target * logp, axis=-1) * row_mask)
    upstream = -target * row_mask[:, None]
    grad_pre = upstream - jnp.exp(logp) * jnp.sum(upstream, axis=-1, keepdims=True)
    weight_grads = [None, None, None]
    bias_grads = [None, None, None]
    for which_layer in (2, 1, 0):
        weight_grads[which_layer], bias_grads[which_layer], grad_inputs = layer_backward(
            inputs_list[which_layer], weights_b[which_layer], grad_pre
        )
        if which_layer > 0:
            grad_pre = gelu_backs[which_layer - 1](grad_inputs)[0]
    resids = (resid6, resid7, resid8)
    noises = (noise6, noise7, noise8)
    accs = [weight_grads[k] + resids[k] for k in range(3)]
    clipped_list = []
    for acc in accs:
        bound = clip_width * jnp.sqrt(jnp.mean(acc * acc))
        clipped_list.append(jnp.clip(acc, -bound, bound))
    peak_list = lax.pmax(tuple(jnp.max(jnp.abs(clipped)) for clipped in clipped_list), BOTH)
    peak_list = [p + 1e-06 for p in peak_list]
    code_list = [dithered_code(clipped_list[k], peak_list[k], noises[k]) for k in range(3)]
    new_resids = [accs[k] - peak_list[k] * code_list[k] for k in range(3)]
    loss_total, image_total, bias_total = lax.psum(
        (worker_loss, jnp.sum(row_mask), jnp.concatenate(bias_grads)), BOTH
    )
    code_rows = [
        lax.psum_scatter(code, "wide", scatter_dimension=0, tiled=True) for code in code_list
    ]
    code_sums = lax.psum(tuple(code_rows), "grp")
    moments = (moment6, moment7, moment8)
    new_moments = [
        momentum_decay * moments[k] + peak_list[k] * code_sums[k] / image_total for k in range(3)
    ]
    full_moments = [
        lax.all_gather(moment, "wide", axis=0, tiled=True) for moment in new_moments
    ]
    row_block = lax.axis_index("wide")
    iterates = []
    for k in range(3):
        whole = full_moments[k]
        iterate = whole / (jnp.sqrt(jnp.sum(whole * whole)) + 1e-07)
        for step_num in range(NS_STEPS):
            iterate = schulz_step(iterate, gram_of(iterate))
        row_count = new_moments[k].shape[0]
        iterates.append(lax.dynamic_slice_in_dim(iterate, row_block * row_count, row_count, 0))
    new_weights = [
        masters[k] - muon_rate * (iterates[k] + decay_rate * masters[k]) for k in range(3)
    ]
    new_biases = adam_biases(biases, bias_first, bias_second, bias_total / image_total)
    return (
        *new_weights,
        *[weight.astype(jnp.bfloat16) for weight in new_weights],
        *new_moments,
        *new_resids,
        *new_biases,
        loss_total,
        image_total,
    )


ORDERS = ((2, 1, 4), (1, 2, 4))


def wide_perm(phase):
    return [
        (g * 8 + w, g * 8 + (w ^ ORDERS[g % 2][phase])) for g in range(4) for w in range(8)
    ]


def grp_perm(bit):
    return [(g * 8 + w, (g ^ bit) * 8 + w) for g in range(4) for w in range(8)]


def swap(array, perm):
    return lax.ppermute(array, BOTH, perm)


def own_core():
    return lax.rem(lax.axis_index("grp"), 2)


def half_at(place, same_core):
    core = own_core() if same_core else 1 - own_core()
    masks = [
        sum(order[phase] for phase in range(3) if place & (4 >> phase)) for order in ORDERS
    ]
    return 2 * (lax.axis_index("wide") ^ jnp.where(core == 0, masks[0], masks[1])) + core


def dims(contract_left, contract_right):
    return (((contract_left,), (contract_right,)), ((), ()))


def mxu(left, right, contract_left=1, contract_right=0):
    return lax.dot_general(
        left, right, dims(contract_left, contract_right), preferred_element_type=F32
    )


def split(value):
    high = value.astype(BF16)
    return high, (value - high.astype(F32)).astype(BF16)


def left_parts(value):
    high, rest = split(value)
    return jnp.concatenate([high, high, rest], axis=1)


def right_parts(value):
    high, rest = split(value)
    return jnp.concatenate([high, rest, high], axis=0)


def shifted_eye(rows, cols, shift, dtype):
    at = lax.broadcasted_iota(jnp.int32, (rows, cols), 0) + shift
    return (at == lax.broadcasted_iota(jnp.int32, (rows, cols), 1)).astype(dtype)


def upright(flat, shift, dtype=BF16):
    return mxu(flat.astype(BF16), shifted_eye(flat.shape[0], 2 * LANE, shift, BF16), 0, 0)


def fold(region):
    n = region.shape[0] // 3
    third = jnp.concatenate([region[2 * n :, :LANE], region[2 * n :, LANE:]], axis=0)
    return jnp.concatenate([region[: 2 * n], third], axis=1)


def unfold(folded):
    n = folded.shape[0] // 2
    last = jnp.concatenate([folded[:n, 2 * LANE :], folded[n:, 2 * LANE :]], axis=1)
    return jnp.concatenate([folded[:, : 2 * LANE], last], axis=0)


HBM = pl.BlockSpec(memory_space=pltpu.HBM)
SMEM = pl.BlockSpec(memory_space=pltpu.SMEM)
VMEM = pl.BlockSpec(memory_space=pltpu.VMEM)
RESULT = pl.BlockSpec(memory_space=pltpu.VMEM)


def shape_of(shape, dtype=F32):
    return jax.ShapeDtypeStruct(shape, dtype)


MICROS = {"passed_near": 0.6, "passed_last": 20.0}


def placed(shape, spec):
    if spec is HBM:
        return pltpu.HBM(shape.shape, shape.dtype)
    return pltpu.VMEM(shape.shape, shape.dtype) if spec is VMEM else shape


def call(kernel, name, in_specs, out_specs, out_shape, scratch=(), megabytes=4, aliases=None):
    many = isinstance(out_shape, list)
    shapes = [
        placed(shape, spec)
        for shape, spec in zip(
            out_shape if many else [out_shape], out_specs if many else [out_specs]
        )
    ]
    kernel_call = pl.pallas_call(
        kernel,
        in_specs=in_specs,
        out_specs=out_specs,
        out_shape=shapes if many else shapes[0],
        scratch_shapes=list(scratch),
        compiler_params=pltpu.CompilerParams(vmem_limit_bytes=megabytes * 1024 * 1024),
        cost_estimate=pl.CostEstimate(
            flops=int(MICROS.get(name, 0.0) * 1.15e9), bytes_accessed=0, transcendentals=0
        ),
        input_output_aliases=aliases or {},
        name=name,
    )

    def run(*arrays):
        return kernel_call(
            *[
                pltpu.with_memory_space_constraint(array, pltpu.HBM) if spec is HBM else array
                for array, spec in zip(arrays, in_specs)
            ]
        )

    return run


def pack_kernel(w6_ref, w7_ref, w8_ref, out_ref, half6, half7, all8, sems):
    core = own_core()
    rows6, rows7 = half6.shape[0], half7.shape[0]
    copies = [
        pltpu.make_async_copy(
            w6_ref.at[pl.ds(pl.multiple_of(core * rows6, 8), rows6)], half6, sems.at[0]
        ),
        pltpu.make_async_copy(
            w7_ref.at[pl.ds(pl.multiple_of(core * rows7, 8), rows7)], half7, sems.at[1]
        ),
        pltpu.make_async_copy(w8_ref, all8, sems.at[2]),
    ]
    for copy in copies:
        copy.start()
    for copy in copies:
        copy.wait()
    out_ref[0, :rows6, :] = half6[...].astype(BF16)
    h2 = half7.shape[1]
    lead = (core == 0).astype(F32)
    region = upright(all8[...], h2) * lead + jnp.concatenate(
        [half7[...], jnp.zeros((rows7, 2 * LANE - h2), F32)], axis=1
    )
    out_ref[0, rows6:, :] = fold(region).astype(BF16)


def pack_weights(weight6, weight7, weight8):
    rows6, h1 = weight6.shape[0] // 2, weight6.shape[1]
    rows7, h2 = weight7.shape[0] // 2, weight7.shape[1]
    return call(
        pack_kernel,
        "pack_weights",
        [HBM] * 3,
        VMEM,
        shape_of((1, rows6 + rows7 * 2 // 3, h1), BF16),
        [
            pltpu.VMEM((rows6, h1), F32),
            pltpu.VMEM((rows7, h2), F32),
            pltpu.VMEM(weight8.shape[::-1], F32),
            pltpu.SemaphoreType.DMA((3,)),
        ],
    )(weight6, weight7, weight8.T)


def stage_kernel(count, after_ref, images_ref, *refs):
    ins, outs, token_ref, sems = refs[:count], refs[count:-2], refs[-2], refs[-1]
    copies = [
        pltpu.make_async_copy(
            source, target if len(source.shape) == len(target.shape) else target.at[0], sems.at[k]
        )
        for k, (source, target) in enumerate(zip(ins, outs))
    ]
    for copy in copies:
        copy.start()
    token_ref[...] = jnp.full(token_ref.shape, images_ref[0], jnp.int32)
    for copy in copies:
        copy.wait()


def stage(after, counts, *arrays):
    count = len(arrays)
    shapes = [(1,) * (2 - array.ndim) + array.shape for array in arrays]
    return call(
        functools.partial(stage_kernel, count),
        "stage",
        [VMEM, SMEM] + [HBM] * count,
        [VMEM] * (count + 1),
        [shape_of(shape, array.dtype) for shape, array in zip(shapes, arrays)]
        + [shape_of((1, LANE), jnp.int32)],
        [pltpu.SemaphoreType.DMA((count,))],
    )(after, counts, *arrays)


def add_kernel(picks, size, *refs):
    for k in range(size):
        total = None
        for ref, pick in zip(refs, picks):
            part = ref[pick + k].astype(F32)
            total = part if total is None else total + part
        refs[-1][k] = total.astype(BF16)


def add(picks, arrays, size, after=(), name="add"):
    shape = shape_of((size,) + arrays[0].shape[1:], BF16)
    specs = [VMEM] * len(arrays) + [spec for spec, _ in after]
    return call(functools.partial(add_kernel, picks, size), name, specs, VMEM, shape)(
        *arrays, *[array for _, array in after]
    )


def pass_kernel(in_ref, *refs):
    refs[-1][...] = in_ref[...]


def passed(array, after, name="passed"):
    specs = [VMEM] * (1 + len(after))
    shape = shape_of(array.shape, array.dtype)
    return call(pass_kernel, name, specs, VMEM, shape)(array, *after)


def first_join_kernel(own_ref, far_ref, mid_ref, *refs):
    trio_ref, again_ref = refs[-2:]
    for k, ref in enumerate((own_ref, far_ref, mid_ref)):
        trio_ref[k] = ref[0]
    again_ref[...] = far_ref[...]


def relay_kernel(trio_ref, one_ref, out_ref):
    count = trio_ref.shape[0]
    out_ref[:count] = trio_ref[...]
    out_ref[count:] = one_ref[...]


def relay(trio, one):
    shape = shape_of((trio.shape[0] + one.shape[0],) + one.shape[1:], one.dtype)
    return call(relay_kernel, "relay", [VMEM] * 2, VMEM, shape)(trio, one)


def gather_halves(own, after=(), work=None):
    far = swap(own, wide_perm(2))
    mid = swap(own, wide_perm(1))
    trio, far = call(
        first_join_kernel,
        "first_join",
        [VMEM] * 3 + [spec for spec, _ in after],
        [VMEM] * 2,
        [shape_of((3,) + own.shape[1:], BF16), shape_of(own.shape, BF16)],
    )(own, far, mid, *[array for _, array in after])
    one3 = swap(far, wide_perm(1))
    trio4 = swap(trio, wide_perm(0))
    one7 = swap(one3, wide_perm(0))
    four, done = (relay(trio, one3), None) if work is None else work(trio, one3)
    trio4 = passed(trio4, (four,))
    one7 = passed(one7, done[:3] if done else (), "passed_last")
    mine = (four, trio4, one7)
    return (*mine, *[swap(part, grp_perm(1)) for part in mine]), done


def gelu_pair(pre):
    slope = 0.7978845608028654
    inner = slope * (pre + 0.044715 * pre * pre * pre)
    t = jnp.tanh(inner)
    value = 0.5 * pre * (1.0 + t)
    back = 0.5 * (1.0 + t) + 0.5 * pre * (1.0 - t * t) * slope * (1.0 + 3 * 0.044715 * pre * pre)
    return value, back


def place_all(sizes, refs, all6, all7, all8):
    ins, h1, h2, classes, rows6, rows7, rows8 = sizes
    for at in range(16):
        place = at % 8
        ref, q = refs[3 * (at // 8) + (0, 0, 0, 0, 1, 1, 1, 2)[place]], place % 4 % (4 - place // 4)
        half = half_at(place, at < 8)
        all6[pl.ds(pl.multiple_of(half * rows6, 16), rows6), :] = ref[q, :rows6, :]
        region = unfold(ref[q, rows6:, :].astype(F32))
        all7[pl.ds(pl.multiple_of(half * rows7, 8), rows7), :] = region

        @pl.when(half % 2 == 0)
        def _():
            row = pl.multiple_of((half // 2) * rows8, 8)
            all8[pl.ds(row, rows8), :] = region[:rows8, LANE:]


def worker_kernel(sizes, tile, *refs):
    ins, h1, h2, classes, rows6, rows7, rows8 = sizes
    halves, refs = refs[:6], refs[6:]
    count_ref, feat_ref, label_ref, bias_ref, resid6_ref, resid7_ref, resid8_ref = refs[:7]
    acc6_ref, acc7_ref, acc8_ref, stats_ref, w6, w7, w8 = refs[7:]
    first = h2 - LANE

    place_all(sizes, halves, w6, w7, w8)
    w7_low = w7[:, :h2].astype(BF16)
    w8_low = w8[...].astype(BF16)

    rows = feat_ref.shape[0]
    row_mask = (lax.broadcasted_iota(jnp.int32, (rows, 1), 0) < count_ref[:, :1]).astype(F32)
    lanes = lax.broadcasted_iota(jnp.int32, (rows, LANE), 1) - first
    valid = (lanes >= 0) & (lanes < classes)
    labels = jnp.sum(
        jnp.where(shifted_eye(rows, rows, 0, jnp.bool_), label_ref[...], 0), axis=1, keepdims=True
    )
    bias8 = jnp.concatenate(
        [bias_ref[:, h1 + LANE :], jnp.zeros((1, LANE - first - classes), F32)], axis=1
    )

    pre6 = mxu(feat_ref[...], w6[...]) + bias_ref[:, :h1]
    act6, back6 = gelu_pair(pre6)
    act6 = act6.astype(BF16)
    pre7 = mxu(act6, w7_low) + bias_ref[:, h1 : h1 + h2]
    act7, back7 = gelu_pair(pre7)
    act7 = act7.astype(BF16)
    logits = jnp.where(valid, mxu(act7, w8_low) + bias8, -1e30)
    shifted = logits - jnp.max(logits, axis=1, keepdims=True)
    logp = shifted - jnp.log(jnp.sum(jnp.exp(shifted), axis=1, keepdims=True))
    onehot = (labels == lanes).astype(F32)
    target = jnp.where(valid, (1.0 - smoothing) * onehot + smoothing / classes, 0.0)
    loss = jnp.sum(-jnp.sum(target * jnp.where(valid, logp, 0.0), axis=1, keepdims=True) * row_mask)
    weight = jnp.sum(target, axis=1, keepdims=True)
    dlogits = (row_mask * (jnp.exp(logp) * weight - target)).astype(BF16)
    dpre7 = (mxu(dlogits, w8_low, 1, 1) * back7).astype(BF16)
    dpre6 = (mxu(dpre7, w7_low, 1, 1) * back6).astype(BF16)

    square6 = jnp.zeros((8, h1), F32)
    most6 = jnp.zeros((8, h1), F32)
    for t in range(ins // tile):
        part = slice(t * tile, (t + 1) * tile)
        acc = resid6_ref[part, :] + mxu(feat_ref[:, part], dpre6, 0, 0)
        acc6_ref[part, :] = acc
        square6 = square6 + jnp.sum((acc * acc).reshape(tile // 8, 8, h1), axis=0)
        most6 = jnp.maximum(most6, jnp.max(jnp.abs(acc).reshape(tile // 8, 8, h1), axis=0))
    acc7 = mxu(dpre7, act6, 0, 0) + resid7_ref[...]
    acc7_ref[...] = acc7
    acc8 = mxu(dlogits, act7, 0, 0)[first : first + classes, :] + resid8_ref[...]
    acc8_ref[...] = acc8

    bound6 = clip_width * jnp.sqrt(jnp.sum(square6) * (1.0 / (ins * h1)))
    bound7 = clip_width * jnp.sqrt(jnp.sum(acc7 * acc7) * (1.0 / (h1 * h2)))
    bound8 = clip_width * jnp.sqrt(jnp.sum(acc8 * acc8) * (1.0 / (h2 * classes)))
    peak6 = jnp.minimum(jnp.max(most6), bound6)
    peak7 = jnp.minimum(jnp.max(jnp.abs(acc7)), bound7)
    peak8 = jnp.minimum(jnp.max(jnp.abs(acc8)), bound8)
    lane = lax.broadcasted_iota(jnp.int32, (1, LANE), 1) - (first + classes)
    tail = jnp.zeros((1, LANE), F32)
    count = count_ref[:, :1].astype(F32)
    for k, value in enumerate((peak6, peak7, peak8, loss, count, bound6, bound7, bound8)):
        tail = jnp.where(lane == k, value, tail)
    db6 = jnp.sum(dpre6.astype(F32), axis=0, keepdims=True)
    db7 = jnp.sum(dpre7.astype(F32), axis=0, keepdims=True)
    db8 = jnp.sum(dlogits.astype(F32), axis=0, keepdims=True)
    db7 = jnp.concatenate([db7, jnp.zeros((1, 2 * LANE - h2), F32)], axis=1)
    row = jnp.concatenate([db6, db7[:, :LANE], db7[:, LANE:] + db8 + tail], axis=1)
    stats_ref[...] = jnp.broadcast_to(row[None], stats_ref.shape)


def code_of(acc, bound, scale, noise):
    ramp = jnp.minimum(jnp.abs(acc), bound) * scale - (
        noise.astype(F32) * (ramp_slope / noise_levels) + 0.5 * ramp_slope / noise_levels
    )
    ramp = jnp.clip(ramp, 0.0, 1.0)
    return jnp.where(acc < 0, -ramp, ramp)


def lane_of(row_ref, k):
    return row_ref[0:1, k : k + 1]


def write_codes(sizes, places, same_core, head, acc6_ref, noise6_ref, code7, code8, out):
    ins, h1, h2, classes, rows6, rows7, rows8 = sizes
    peak, bound = lane_of(head, 0), lane_of(head, 3)
    scale = (1.0 + ramp_slope) / peak
    for at, place in enumerate(places):
        half = half_at(place, same_core)
        part = pl.ds(pl.multiple_of(half * rows6, 8), rows6)
        code = code_of(acc6_ref[part, :], bound, scale, noise6_ref[part, :])
        out[at, :rows6, :] = code.astype(BF16)
        region = code7[pl.ds(pl.multiple_of(half * rows7, 8), rows7), :]
        lead = (half % 2 == 0).astype(F32)
        region = region + lead * code8[pl.ds(pl.multiple_of((half // 2) * rows8, 8), rows8), :]
        out[at, rows6:, :] = fold(region).astype(BF16)


def first_codes_kernel(sizes, places, stats_ref, mine_ref, acc6_ref, noise6_ref, *refs):
    ins, h1, h2, classes, rows6, rows7, rows8 = sizes
    acc7_ref, noise7_ref, acc8_ref, noise8_ref, out_ref, head_ref, code7, code8 = refs
    at = h1 + h2 + classes
    most = jnp.max(stats_ref[:, :, at : at + 3], axis=0) + 1e-06
    images = jnp.sum(stats_ref[:, :, at + 4 : at + 5], axis=0)
    lane = lax.broadcasted_iota(jnp.int32, (1, LANE), 1)
    head = jnp.zeros((1, LANE), F32)
    for k in range(3):
        head = jnp.where(lane == k, most[:, k : k + 1], head)
        head = jnp.where(lane == 3 + k, mine_ref[0, :, at + 5 + k : at + 6 + k], head)
        head = jnp.where(lane == 6 + k, most[:, k : k + 1] / images, head)
    head_ref[...] = head
    ramp = 1.0 + ramp_slope
    small7 = code_of(acc7_ref[...], lane_of(head, 4), ramp / lane_of(head, 1), noise7_ref[...])
    small8 = code_of(acc8_ref[...], lane_of(head, 5), ramp / lane_of(head, 2), noise8_ref[...])
    code7[...] = upright(small7, 0)
    code8[...] = upright(small8, h2)
    write_codes(sizes, places, False, head, acc6_ref, noise6_ref, code7, code8, out_ref)


def codes_kernel(sizes, places, same_core, head_ref, acc6, noise6, code7, code8, *refs):
    write_codes(sizes, places, same_core, head_ref, acc6, noise6, code7, code8, refs[-1])


def resid_of(head, layer, acc, noise):
    peak = lane_of(head, layer)
    return acc - peak * code_of(acc, lane_of(head, 3 + layer), (1.0 + ramp_slope) / peak, noise)


def resid_kernel(tile, start, after_ref, head_ref, acc6_ref, noise6_ref, *refs):
    out_ref, hold, sems = refs[-3:]
    head = head_ref[...]
    copies = []
    for t in range(hold.shape[0] // tile):
        here, there = pl.ds(t * tile, tile), pl.ds(start + t * tile, tile)
        hold[here, :] = resid_of(head, 0, acc6_ref[there, :], noise6_ref[there, :])
        copies.append(pltpu.make_async_copy(hold.at[here], out_ref.at[there], sems.at[t]))
        copies[-1].start()
    for copy in copies:
        copy.wait()


def new_resid6_part(start, rows, after, head, acc6, noise6, before=None):
    tile = 3 * LANE
    ins = [after, head, acc6, noise6] + ([] if before is None else [before])
    return call(
        functools.partial(resid_kernel, tile, start),
        "new_resid",
        [VMEM] * 4 + [HBM] * (len(ins) - 4),
        HBM,
        shape_of(acc6.shape),
        [pltpu.VMEM((rows, acc6.shape[1]), F32), pltpu.SemaphoreType.DMA((rows // tile,))],
        megabytes=8,
        aliases={} if before is None else {4: 0},
    )(*ins)


def small_resids_kernel(after_ref, head_ref, acc7_ref, noise7_ref, acc8_ref, noise8_ref, *outs):
    head = head_ref[...]
    outs[0][...] = resid_of(head, 1, acc7_ref[...], noise7_ref[...])
    outs[1][...] = resid_of(head, 2, acc8_ref[...], noise8_ref[...])


def totals_kernel(after_ref, stats_ref, bias_ref, first_ref, second_ref, *refs):
    outs, loss_ref, images_ref, rows, sems = refs[:3], refs[3], refs[4], refs[5:8], refs[8]
    width = bias_ref.shape[1]
    total = jnp.sum(stats_ref[...], axis=0)
    images = total[:, width + 4 : width + 5]
    loss_ref[...] = total[:, width + 3 : width + 4]
    images_ref[...] = images
    rows[0][...], rows[1][...], rows[2][...] = adam_biases(
        bias_ref[...], first_ref[...], second_ref[...], total[:, :width] / images
    )
    copies = [
        pltpu.make_async_copy(row.at[0], out, sems.at[k])
        for k, (row, out) in enumerate(zip(rows, outs))
    ]
    for copy in copies:
        copy.start()
    for copy in copies:
        copy.wait()


def hold_kernel(after_ref, m6_ref, m7_ref, m8_ref, out_ref, half7, all8, sems):
    core = own_core()
    rows7, h2 = half7.shape
    rows6 = out_ref.shape[1] - rows7 * 2 // 3
    copies = [
        pltpu.make_async_copy(
            m6_ref.at[pl.ds(pl.multiple_of(core * rows6, 8), rows6)],
            out_ref.at[0, pl.ds(0, rows6)],
            sems.at[0],
        ),
        pltpu.make_async_copy(
            m7_ref.at[pl.ds(pl.multiple_of(core * rows7, 8), rows7)], half7, sems.at[1]
        ),
        pltpu.make_async_copy(m8_ref, all8, sems.at[2]),
    ]
    for copy in copies:
        copy.start()
    for copy in copies:
        copy.wait()
    lead = (core == 0).astype(F32)
    tall = jnp.zeros((rows7, 2 * LANE), F32)
    parts = all8[...]
    for _ in range(3):
        high = parts.astype(BF16)
        tall = tall + upright(high, h2)
        parts = parts - high.astype(F32)
    region = tall * lead + jnp.concatenate(
        [half7[...], jnp.zeros((rows7, 2 * LANE - h2), F32)], axis=1
    )
    out_ref[0, rows6:, :] = fold(region)


def hold_moments(after, moment6, moment7, moment8):
    rows6, h1 = moment6.shape[0] // 2, moment6.shape[1]
    rows7, h2 = moment7.shape[0] // 2, moment7.shape[1]
    return call(
        hold_kernel,
        "hold_moments",
        [VMEM] + [HBM] * 3,
        VMEM,
        shape_of((1, rows6 + rows7 * 2 // 3, h1)),
        [
            pltpu.VMEM((rows7, h2), F32),
            pltpu.VMEM(moment8.shape[::-1], F32),
            pltpu.SemaphoreType.DMA((3,)),
        ],
    )(after, moment6, moment7, moment8.T)


def moment_kernel(sizes, head_ref, held_ref, mine_ref, theirs_ref, out_ref, low_ref):
    ins, h1, h2, classes, rows6, rows7, rows8 = sizes
    codes = mine_ref[0].astype(F32) + theirs_ref[0].astype(F32)
    moment6 = momentum_decay * held_ref[0, :rows6] + lane_of(head_ref, 6) * codes[:rows6]
    column = lax.broadcasted_iota(jnp.int32, (rows7, 2 * LANE), 1)
    rate = fold(jnp.where(column < h2, lane_of(head_ref, 7), lane_of(head_ref, 8)))
    region = momentum_decay * held_ref[0, rows6:] + rate * codes[rows6:]
    out_ref[0, :rows6] = moment6
    out_ref[0, rows6:] = region
    low_ref[0, :rows6] = moment6.astype(BF16)
    low_ref[0, rows6:] = region.astype(BF16)


def schulz_chains(grams, iterates):
    diagonals = [shifted_eye(gram.shape[0], gram.shape[0], 0, F32) for gram in grams]
    for number in range(NS_STEPS):
        lefts = [left_parts(gram) for gram in grams]
        squares = [mxu(left, right_parts(gram)) for left, gram in zip(lefts, grams)]
        mixed = [
            right_parts(coef_a * diagonal + coef_b * gram + coef_c * square)
            for diagonal, gram, square in zip(diagonals, grams, squares)
        ]
        rows = [left_parts(iterate) for iterate in iterates]
        if number == NS_STEPS - 1:
            return [mxu(row, right) for row, right in zip(rows, mixed)]
        both = [
            mxu(jnp.concatenate([left, row], axis=0), right)
            for left, row, right in zip(lefts, rows, mixed)
        ]
        iterates = [value[gram.shape[0] :] for value, gram in zip(both, grams)]
        grams = [
            mxu(left_parts(value[: gram.shape[0]]), right)
            for value, gram, right in zip(both, grams, mixed)
        ]


def grams_of(sizes, ref):
    rows6 = sizes[4]
    places = range(ref.shape[0])
    block = jnp.concatenate([ref[k, :rows6, :] for k in places], axis=0)
    region = [unfold(ref[k, rows6:, :].astype(F32)) for k in places]
    region = jnp.concatenate(region, axis=0).astype(BF16)
    return mxu(block, block, 0, 0), mxu(region, region, 0, 0)


def early_kernel(sizes, trio_ref, one_ref, moment_ref, four_ref, out6_ref, out78_ref, again_ref):
    relay_kernel(trio_ref, one_ref, four_ref)
    again_ref[...] = moment_ref[...]
    out6_ref[...], out78_ref[...] = grams_of(sizes, four_ref)


def late_kernel(sizes, own6_ref, own78_ref, trio_ref, one_ref, theirs_ref, trio2_ref, *outs):
    trio6, trio78 = grams_of(sizes, trio_ref)
    one6, one78 = grams_of(sizes, one_ref)
    outs[0][...] = own6_ref[...] + trio6 + one6
    outs[1][...] = own78_ref[...] + trio78 + one78
    four6, four78 = grams_of(sizes, theirs_ref)
    trio6, trio78 = grams_of(sizes, trio2_ref)
    outs[2][...] = four6 + trio6
    outs[3][...] = four78 + trio78


def momenta_kernel(sizes, mine_ref, theirs_ref, *refs):
    ins, h1, h2, classes, rows6, rows7, rows8 = sizes
    out6_ref, out7_ref, out8_ref, near6_ref, near78_ref, stage7, sems = refs
    core = own_core()
    copies = []
    region8 = None
    for k, (at, ref) in enumerate(((core, mine_ref), (1 - core, theirs_ref))):
        part = pl.ds(pl.multiple_of(at * rows6, 8), rows6)
        near6_ref[part, :] = ref[0, :rows6, :]
        copies.append(
            pltpu.make_async_copy(ref.at[0, pl.ds(0, rows6)], out6_ref.at[part], sems.at[k])
        )
        copies[-1].start()
        region = unfold(ref[0, rows6:, :])
        near78_ref[pl.ds(pl.multiple_of(at * rows7, 8), rows7), :] = region
        region8 = region if region8 is None else jnp.where(core == 0, region8, region)
    column = lax.broadcasted_iota(jnp.int32, (2 * rows7, 2 * LANE), 1)
    near78_ref[: 2 * rows7, :] = jnp.where(column < h2, near78_ref[: 2 * rows7, :], 0.0)
    near78_ref[2 * rows7 :, :] = jnp.where(column[:rows8] < h2, 0.0, region8[:rows8])
    stage7[...] = near78_ref[: 2 * rows7, :h2]
    copies.append(pltpu.make_async_copy(stage7, out7_ref, sems.at[2]))
    copies[-1].start()
    out8_ref[...] = turned(sizes, near78_ref[2 * rows7 :, LANE:])
    for copy in copies:
        copy.wait()


def turned(sizes, rows):
    ins, h1, h2, classes, rows6, rows7, rows8 = sizes
    square = jnp.concatenate([rows, jnp.zeros((LANE - rows8, LANE), F32)], axis=0)
    return square.T[h2 - LANE : h2 - LANE + classes, :rows8]


def update_kernel(sizes, own6, own78, other6, other78, one7_ref, *refs):
    ins, h1, h2, classes, rows6, rows7, rows8 = sizes
    near6_ref, near78_ref, w6_ref, w7_ref, w8_ref, *outs = refs
    new6_ref, new7_ref, new8_ref, low6_ref, low7_ref, low8_ref = outs
    last6, last78 = grams_of(sizes, one7_ref)
    gram6 = own6[...] + (other6[...] + last6)
    gram7 = own78[...] + (other78[...] + last78)

    size = 2 * LANE
    is7_row = lax.broadcasted_iota(jnp.int32, (size, size), 0) < h2
    is7_col = lax.broadcasted_iota(jnp.int32, (size, size), 1) < h2
    diagonal = shifted_eye(size, size, 0, F32)
    inverse6 = 1.0 / (jnp.sqrt(jnp.sum(gram6 * shifted_eye(h1, h1, 0, F32))) + 1e-07)
    trace7 = jnp.sum(jnp.where(is7_col, gram7 * diagonal, 0.0))
    trace8 = jnp.sum(jnp.where(is7_col, 0.0, gram7 * diagonal))
    inverse7 = 1.0 / (jnp.sqrt(trace7) + 1e-07)
    inverse8 = 1.0 / (jnp.sqrt(trace8) + 1e-07)
    inverse = jnp.where(is7_col[:1], inverse7, inverse8)
    gram7 = jnp.where(is7_row == is7_col, gram7 * (inverse * inverse), 0.0)
    iterate6, iterate7 = schulz_chains(
        [gram6 * (inverse6 * inverse6), gram7],
        [near6_ref[...] * inverse6, near78_ref[...] * inverse],
    )
    for iterate, w_ref, new_ref, low_ref in (
        (iterate6, w6_ref, new6_ref, low6_ref),
        (iterate7[: 2 * rows7, :h2], w7_ref, new7_ref, low7_ref),
        (turned(sizes, iterate7[2 * rows7 :, LANE:]), w8_ref, new8_ref, low8_ref),
    ):
        master = w_ref[...]
        value = master - muon_rate * (iterate + decay_rate * master)
        new_ref[...] = value
        low_ref[...] = value.astype(BF16)


def paired_plan(
    features,
    labels,
    counts,
    weight6,
    weight7,
    weight8,
    moment6,
    moment7,
    moment8,
    resid6,
    resid7,
    resid8,
    noise6,
    noise7,
    noise8,
    biases,
    bias_first,
    bias_second,
):
    ins, h1 = resid6.shape
    h2, classes = resid8.shape
    rows6 = weight6.shape[0] // 2
    rows7 = weight7.shape[0] // 2
    rows8 = weight8.shape[0]
    sizes = (ins, h1, h2, classes, rows6, rows7, rows8)
    devices = 32
    half = (rows6 + rows7 * 2 // 3, h1)

    packed = pack_weights(weight6, weight7, weight8)
    staged = stage(
        packed,
        counts,
        features,
        labels,
        biases,
        bias_first,
        bias_second,
        resid6,
        resid7.T,
        resid8.T,
        noise6,
        noise7.T,
        noise8.T,
    )
    features, labels, *bias_rows = staged[:5]
    resid6, resid7, resid8, noise6, noise7, noise8, count_row = staged[5:]
    halves, _ = gather_halves(packed, [(VMEM, count_row)])

    tile = 2 * LANE
    lanes = h1 + 2 * LANE
    acc6, acc7, acc8, stats = call(
        functools.partial(worker_kernel, sizes, tile),
        "worker",
        [VMEM] * 13,
        [VMEM] * 4,
        [
            shape_of((ins, h1)),
            shape_of((h2, h1)),
            shape_of((classes, h2)),
            shape_of((devices, 1, lanes)),
        ],
        [
            pltpu.VMEM((ins, h1), BF16),
            pltpu.VMEM((h1, 2 * LANE), F32),
            pltpu.VMEM((h2, LANE), F32),
        ],
        megabytes=16,
    )(*halves, count_row, features, labels, bias_rows[0], resid6, resid7, resid8)

    all_stats = lax.all_to_all(stats, BOTH, 0, 0, tiled=True)

    def halves_of(count):
        return shape_of((count,) + half, BF16)

    sent7, head, code7, code8 = call(
        functools.partial(first_codes_kernel, sizes, (7,)),
        "codes_first",
        [VMEM] * 8,
        [VMEM] * 4,
        [
            halves_of(1),
            shape_of((1, LANE)),
            shape_of((h1, 2 * LANE)),
            shape_of((h2, 2 * LANE)),
        ],
    )(all_stats, stats, acc6, noise6, acc7, noise7, acc8, noise8)

    def codes(places, same_core, after=()):
        return call(
            functools.partial(codes_kernel, sizes, places, same_core),
            "codes",
            [VMEM] * (5 + len(after)),
            VMEM,
            halves_of(len(places)),
        )(head, acc6, noise6, code7, code8, *after)

    got7 = swap(sent7, grp_perm(1))
    kept7 = codes((7,), True)
    sent456 = codes((4, 5, 6), False, (kept7,))
    got456 = swap(sent456, grp_perm(1))
    out7 = add((0, 0), (kept7, got7), 1, [(VMEM, sent456)])
    near7 = swap(out7, wide_perm(0))
    kept456 = codes((4, 5, 6), True, (out7,))
    out56 = add((1, 1), (kept456, got456), 2)
    near56 = swap(out56, wide_perm(0))
    near4 = swap(add((0, 0), (kept456, got456), 1), wide_perm(0))
    got3 = swap(codes((3,), False, (out56,)), grp_perm(1))
    far3 = add((0, 0, 0), (codes((3,), True, (out56,)), got3, near7), 1)
    near56 = passed(near56, (far3,), "passed_near")
    got012 = swap(codes((0, 1, 2), False, (far3,)), grp_perm(1))
    kept012 = codes((0, 1, 2), True, (far3,))
    totals = call(
        totals_kernel,
        "totals",
        [VMEM] * 5,
        [HBM] * 3 + [RESULT] * 2,
        [shape_of(biases.shape)] * 3 + [shape_of((1, 1))] * 2,
        [pltpu.VMEM((1, biases.shape[0]), F32)] * 3 + [pltpu.SemaphoreType.DMA((3,))],
    )(far3, all_stats, *bias_rows)
    flat = totals[:3]
    far3 = swap(far3, wide_perm(1))
    far2 = add((2, 2, 1), (kept012, got012, near56), 1, name="add_far2")
    far2 = swap(far2, wide_perm(1))
    last = add((1, 1, 0, 0), (kept012, got012, near56, far3), 1, [(HBM, row) for row in flat])
    new_resid6 = new_resid6_part(0, ins // 2, last, head, acc6, noise6)
    last = swap(last, wide_perm(2))
    mine = add((0,) * 5, (kept012, got012, near4, far2, last), 1, [(HBM, new_resid6)])
    held = hold_moments(mine, moment6, moment7, moment8)
    theirs = swap(mine, grp_perm(2))

    moment, moment_low = call(
        functools.partial(moment_kernel, sizes),
        "moment",
        [VMEM] * 4,
        [VMEM] * 2,
        [shape_of((1,) + half), shape_of((1,) + half, BF16)],
    )(head, held, mine, theirs)
    new_resid6 = new_resid6_part(
        ins // 2, ins // 2, moment_low, head, acc6, noise6, new_resid6
    )
    new_resid7, new_resid8 = call(
        small_resids_kernel,
        "small_resids",
        [VMEM] * 6,
        [RESULT] * 2,
        [shape_of(acc7.shape), shape_of(acc8.shape)],
    )(moment_low, head, acc7, noise7, acc8, noise8)
    grams = [shape_of((h1, h1)), shape_of((2 * LANE, 2 * LANE))]

    def beside_last(trio, one3):
        four, *early, again = call(
            functools.partial(early_kernel, sizes),
            "early_grams",
            [VMEM] * 3,
            [VMEM] * 4,
            [halves_of(4), *grams, shape_of((1,) + half)],
            megabytes=8,
        )(trio, one3, moment)
        momenta = call(
            functools.partial(momenta_kernel, sizes),
            "momenta",
            [VMEM] * 2,
            [HBM, HBM, RESULT, VMEM, VMEM],
            [
                shape_of(moment6.shape),
                shape_of(moment7.shape),
                shape_of(moment8.shape[::-1]),
                shape_of(moment6.shape),
                shape_of((2 * rows7 + rows8, 2 * LANE)),
            ],
            [pltpu.VMEM(moment7.shape, F32), pltpu.SemaphoreType.DMA((3,))],
        )(again, swap(again, grp_perm(1)))
        return four, [momenta[3], *early, *momenta]

    moments, done = gather_halves(
        moment_low, [(HBM, new_resid6), (HBM, new_resid8)], beside_last
    )
    early, (mom6, mom7, mom8, near6, near78) = done[1:3], done[3:]
    late = call(
        functools.partial(late_kernel, sizes),
        "late_grams",
        [VMEM] * 6,
        [VMEM] * 4,
        grams * 2,
        megabytes=8,
    )(*early, *moments[1:5])

    updated = call(
        functools.partial(update_kernel, sizes),
        "update",
        [VMEM] * 10,
        [RESULT] * 6,
        [
            shape_of(weight6.shape),
            shape_of(weight7.shape),
            shape_of(weight8.shape[::-1]),
            shape_of(weight6.shape, BF16),
            shape_of(weight7.shape, BF16),
            shape_of(weight8.shape[::-1], BF16),
        ],
        megabytes=16,
    )(*late, moments[5], near6, near78, weight6, weight7, weight8.T)
    new6, new7, new8, low6, low7, low8 = updated
    return (
        new6,
        new7,
        new8.T,
        low6,
        low7,
        low8.T,
        mom6,
        mom7,
        mom8.T,
        new_resid6,
        new_resid7.T,
        new_resid8.T,
        *flat,
        *[array.reshape(()) for array in totals[3:]],
    )


def on_device(*arrays):
    (ins, h1), (_, h2), (_, classes) = [array.shape for array in arrays[9:12]]
    rows6, rows7, rows8 = [array.shape[0] for array in arrays[3:6]]
    paired = (
        (lax.axis_size("grp"), lax.axis_size("wide")) == (4, 8)
        and h1 == 3 * LANE
        and LANE < h2 < 2 * LANE
        and h2 + classes <= 2 * LANE
        and rows6 % 32 == 0
        and rows7 == rows8 * 2
        and rows8 % 24 == 0
        and ins % (2 * LANE) == 0
        and 16 * rows7 // 2 == h1
    )
    return (paired_plan if paired else general_plan)(*arrays)


def solution(mesh):
    split_both = P(BOTH, None)
    split_wide = P("wide", None)
    return jax.shard_map(
        on_device,
        mesh=mesh,
        in_specs=(
            split_both,
            P(BOTH),
            P(BOTH),
            *[split_wide] * 6,
            *[split_both] * 6,
            P(),
            P(),
            P(),
        ),
        out_specs=(*[split_wide] * 9, *[split_both] * 3, P(), P(), P(), P(), P()),
        check_vma=False,
    )
```

time: 499 us -> 101 us (0.20); the launches traced: 491 us -> 101 us
  blocking collectives: 257 us -> 12.2 us
  matrix products: 96.6 us -> 0 us
  Pallas kernels: 0 us -> 34.4 us
  local copies, waits for them, and re-layouts: 30.8 us -> 0.01 us
  other arithmetic: 27.8 us -> 0 us
  waiting for transfers between devices: 56 us -> 31.9 us
  starting transfers between devices: 0.21 us -> 20.8 us
  between operations: 22.2 us -> 1.61 us
    all_gather x4 -> x0, blocking collectives: 127 us -> none  [the longest x1 32.3 us: on_device(): lax.all_gather(weight8.astype(jnp.bfloat16), 'wide', axis=0, tiled=True)]
    dot_general x53 -> x0, matrix products: 96.6 us -> none  [the longest x15 42.8 us: schulz_step(): return coef_a * iterate + jnp.dot(iterate, mixed, precision=highest)]
    psum x2 -> x0, blocking collectives: 52.8 us -> none  [the longest x1 41 us: on_device(): lax.psum((worker_loss, jnp.sum(row_mask), jnp.concatenate(bias_grads)), (...]
    pmax x1 -> x0, blocking collectives: 39.8 us -> none  [on_device(): lax.pmax((jnp.max(jnp.abs(clipped_list[0])), jnp.max(jnp.abs(clipped_list...]
    unnamed x1 -> x0, blocking collectives: 37.6 us -> none
    pallas_call x0 -> x36, Pallas kernels: none -> 34.4 us  [run(): kernel_call(*[pltpu.with_memory_space_constraint(array, pltpu.HBM) if spe...]
    ppermute x0 -> x28, waiting for transfers between devices: none -> 31.9 us  [swap(): return lax.ppermute(array, BOTH, perm)]
    psum x1 -> x0, waiting for transfers between devices: 31.4 us -> none  [on_device(): code_sums = lax.psum((code_rows[0], code_rows[1], code_rows[2]), 'grp')]
  transfers between devices with their start and end apart: 5 -> 28, of which waited for: 2 -> 13; matrix products, arithmetic and copies ran while one was open for 9% -> 0% of each run, Pallas kernels for 0% -> 16%
where the time goes in v2:
time: 101 us
  Pallas kernels  34.4 us (34%)
  waiting for transfers between devices  31.9 us (32%)
  starting transfers between devices  20.8 us (21%)
  blocking collectives  12.2 us (12%)
  between operations  1.61 us (2%)
    pallas_call x36, Pallas kernels, run(): kernel_call(*[pltpu.with_memory_space_constraint(array, pltpu.HBM) if spe...  34.4 us
    ppermute x28, waiting for transfers between devices, swap(): return lax.ppermute(array, BOTH, perm)  31.9 us
    ppermute x28, starting transfers between devices, swap(): return lax.ppermute(array, BOTH, perm)  20.8 us
    all_to_all x1, blocking collectives, paired_plan(): all_stats = lax.all_to_all(stats, BOTH, 0, 0, tiled=True)  12.2 us
  transfers between devices with their start and end apart: 28, of which 13 were waited for; matrix products, arithmetic and copies ran while one was open for 0% of the time, Pallas kernels for 16%

profile of v2, /device:TPU:0, one launch (start us, length us, event | category | flops | bytes accessed | tf_op | source)
XLA Modules:
  0.0 100.9 jit_solution(9244102639962680646)
XLA Ops:
  0.7 1.2 %pack_weights.1.after_ref.own_ref = bf16[1,160,384]{2,1,0:T(8,128)(2,1)S(1)} custom-call(f32[288,384]{1,0:T(8,128)} %refs_2_.3, f32[48,192]{1,0:T(8,128)} %refs_3_.3, f32[10,24]{1,0:T(8,128)} %bitcast.13), custom_call_target="tpu_custom_call" | custom-call | tf_op jit(solution)/shard_map/pack_weights/pallas_call | solution.py:299
  1.8 4.1 %collective-permute-start = (bf16[1,160,384]{2,1,0:T(8,128)(2,1)S(1)}, bf16[1,160,384]{2,1,0:T(8,128)(2,1)S(1)}, u32[]{:S(2)}, u32[]{:S(2)}) collective-permute-start(bf16[1,160,384]{2,1,0:T(8,128)(2,1)S(1)} %pack_weights.1.after_ref.own_ref), channel_id=1, source_target_pairs={{0,4},{1,5},{2,6},{3,7},{4,0},{5,1},{6,2},{7,3},{8,12},{9,13},{10,... | collective-permute-start | bytes 368648 | tf_op jit(solution)/shard_map/ppermute | solution.py:196
  5.9 1.5 %collective-permute-start.1 = (bf16[1,160,384]{2,1,0:T(8,128)(2,1)S(1)}, bf16[1,160,384]{2,1,0:T(8,128)(2,1)S(1)}, u32[]{:S(2)}, u32[]{:S(2)}) collective-permute-start(bf16[1,160,384]{2,1,0:T(8,128)(2,1)S(1)} %pack_weights.1.after_ref.own_ref), channel_id=1, source_target_pairs={{0,1},{1,0},{2,3},{3,2},{4,5},{5,4},{6,7},{7,6},{8,10},{9,11},{10,... | collective-permute-start | bytes 368648 | tf_op jit(solution)/shard_map/ppermute | solution.py:196
  8.1 3.6 %stage.1 = (bf16[192,2304]{1,0:T(8,128)(2,1)S(1)}, s32[1,192]{1,0:T(1,128)S(1)}, f32[1,586]{1,0:T(1,128)S(1)}, f32[1,586]{1,0:T(1,128)S(1)}, f32[1,586]{1,0:T(1,...) custom-call(bf16[1,160,384]{2,1,0:T(8,128)(2,1)S(1)} %pack_weights.1, ...), custom_call_target="tpu_custom_call" | custom-call | tf_op jit(solution)/shard_map/stage/pallas_call | solution.py:299
  11.9 1.5 %collective-permute-start.3 = (bf16[3,160,384]{2,1,0:T(8,128)(2,1)S(1)}, bf16[3,160,384]{2,1,0:T(8,128)(2,1)S(1)}, u32[]{:S(2)}, u32[]{:S(2)}) collective-permute-start(bf16[3,160,384]{2,1,0:T(8,128)(2,1)S(1)} %get-tuple-element.70.trio_ref), channel_id=1, source_target_pairs={{0,2},{1,3},{2,0},{3,1},{4,6},{5,7},{6,4},{7,5},{8,9},{9,8},{10,11... | collective-permute-start | bytes 1105928 | tf_op jit(solution)/shard_map/ppermute | solution.py:196
  13.4 0.8 collective-permute-start.2
  14.2 4.9 %collective-permute-done.2.one_ref = bf16[1,160,384]{2,1,0:T(8,128)(2,1)S(1)} collective-permute-done((bf16[1,160,384]{2,1,0:T(8,128)(2,1)S(1)}, bf16[1,160,384]{2,1,0:T(8,128)(2,1)S(1)}, u32[]{:S(2)}, u32[]{:S(2)}) %collective-permute-start.2) | collective-permute-done | bytes 122912 | tf_op jit(solution)/shard_map/ppermute | solution.py:196
  19.1 1.2 %collective-permute-start.4 = (bf16[1,160,384]{2,1,0:T(8,128)(2,1)S(1)}, bf16[1,160,384]{2,1,0:T(8,128)(2,1)S(1)}, u32[]{:S(2)}, u32[]{:S(2)}) collective-permute-start(bf16[1,160,384]{2,1,0:T(8,128)(2,1)S(1)} %collective-permute-done.2.one_ref), channel_id=1, source_target_pairs={{0,2},{1,3},{2,0},{3,1},{4,6},{5,7},{6,4},{7,5},{8,9},{9,8},{10,11... | collective-permute-start | bytes 368648 | tf_op jit(solution)/shard_map/ppermute | solution.py:196
  20.5 0.5 collective-permute-start.6
  21.0 2.9 %collective-permute-done.4.in_ref = bf16[1,160,384]{2,1,0:T(8,128)(2,1)S(1)} collective-permute-done((bf16[1,160,384]{2,1,0:T(8,128)(2,1)S(1)}, bf16[1,160,384]{2,1,0:T(8,128)(2,1)S(1)}, u32[]{:S(2)}, u32[]{:S(2)}) %collective-permute-start.4) | collective-permute-done | bytes 122912 | tf_op jit(solution)/shard_map/ppermute | solution.py:196
  24.1 1.3 %collective-permute-done.7.refs_5_ = bf16[1,160,384]{2,1,0:T(8,128)(2,1)S(1)} collective-permute-done((bf16[1,160,384]{2,1,0:T(8,128)(2,1)S(1)}, bf16[1,160,384]{2,1,0:T(8,128)(2,1)S(1)}, u32[]{:S(2)}, u32[]{:S(2)}) %collective-permute-start.7) | collective-permute-done | bytes 122912 | tf_op jit(solution)/shard_map/ppermute | solution.py:196
  25.4 2.9 %worker.1 = (f32[2304,384]{1,0:T(8,128)S(1)}, f32[192,384]{1,0:T(8,128)S(1)}, f32[10,192]{1,0:T(8,128)S(1)}, f32[32,1,640]{2,1,0:T(1,128)S(1)}) custom-call(bf16[4,160,384]{2,1,0:T(8,128)(2,1)S(1)} %relay.1.refs_0_, bf16[3,160,384]{2,1,0:T(8,128)(2,1)S(1)} %passed.2.refs_1_, bf16[1,160,384]{2,1,0:T(8,128)(2,1)S(1)} %passed_last.2.refs_2_, ...), custom_call_target="tpu_custom_call" | custom-call | tf_op jit(solution)/shard_map/worker/pallas_call | solution.py:299
  28.3 12.2 %all_to_all.5.stats_ref = f32[32,1,640]{2,1,0:T(1,128)S(1)} all-to-all(f32[32,1,640]{2,1,0:T(1,128)S(1)} %get-tuple-element.78.mine_ref), channel_id=1, replica_groups=mesh['grp'=4,'wide'=8] {'grp','wide'}, dimensions={0} | all-to-all | bytes 163840 | tf_op jit(solution)/shard_map/all_to_all | solution.py:901
  40.5 0.6 codes_first.1
  41.3 0.4 codes.8.refs_2_
  41.9 0.4 collective-permute-start.8
  42.3 1.4 %collective-permute-done.8.refs_1_ = bf16[1,160,384]{2,1,0:T(8,128)(2,1)S(1)} collective-permute-done((bf16[1,160,384]{2,1,0:T(8,128)(2,1)S(1)}, bf16[1,160,384]{2,1,0:T(8,128)(2,1)S(1)}, u32[]{:S(2)}, u32[]{:S(2)}) %collective-permute-start.8) | collective-permute-done | bytes 122912 | tf_op jit(solution)/shard_map/ppermute | solution.py:196
  43.7 0.4 codes.9.refs_0_
  44.1 0.6 collective-permute-start.11
  45.3 3.7 %collective-permute-done.11.refs_2_ = bf16[1,160,384]{2,1,0:T(8,128)(2,1)S(1)} collective-permute-done((bf16[1,160,384]{2,1,0:T(8,128)(2,1)S(1)}, bf16[1,160,384]{2,1,0:T(8,128)(2,1)S(1)}, u32[]{:S(2)}, u32[]{:S(2)}) %collective-permute-start.11) | collective-permute-done | bytes 122912 | tf_op jit(solution)/shard_map/ppermute | solution.py:196
  49.1 0.4 codes.13
  49.6 0.6 collective-permute-start.14
  50.2 0.9 collective-permute-start.16
  51.2 1.5 %collective-permute-start.13 = (bf16[1,160,384]{2,1,0:T(8,128)(2,1)S(1)}, bf16[1,160,384]{2,1,0:T(8,128)(2,1)S(1)}, u32[]{:S(2)}, u32[]{:S(2)}) collective-permute-start(bf16[1,160,384]{2,1,0:T(8,128)(2,1)S(1)} %add.9), channel_id=1, source_target_pairs={{0,2},{1,3},{2,0},{3,1},{4,6},{5,7},{6,4},{7,5},{8,9},{9,8},{10,11... | collective-permute-start | bytes 368648 | tf_op jit(solution)/shard_map/ppermute | solution.py:196
  52.6 0.4 codes.12.refs_0_
  53.1 1.3 %totals.1 = (f32[586]{0:T(1024)}, f32[586]{0:T(1024)}, f32[586]{0:T(1024)}, f32[1,1]{1,0:T(1,128)}, f32[1,1]{1,0:T(1,128)}) custom-call(bf16[1,160,384]{2,1,0:T(8,128)(2,1)S(1)} %add.8.refs_0_.after_ref, f32[32,1,640]{2,1,0:T(1,128)S(1)} %all_to_all.5.stats_ref, f32[1,586]{1,0:T(1,128)S(1)} %get-tuple-element.74.refs_9_.bias_ref, ...), custom_call_target="tpu_custom_call" | custom-call | tf_op jit(solution)/shard_map/totals/pallas_call | solution.py:299
  54.3 2.9 %collective-permute-done.14.in_ref = bf16[2,160,384]{2,1,0:T(8,128)(2,1)S(1)} collective-permute-done((bf16[2,160,384]{2,1,0:T(8,128)(2,1)S(1)}, bf16[2,160,384]{2,1,0:T(8,128)(2,1)S(1)}, u32[]{:S(2)}, u32[]{:S(2)}) %collective-permute-start.14) | collective-permute-done | bytes 245792 | tf_op jit(solution)/shard_map/ppermute | solution.py:196
  57.3 0.5 collective-permute-start.17
  57.9 0.9 collective-permute-start.15
  58.8 2.4 %new_resid.2.refs_5_.refs_0_ = f32[2304,384]{1,0:T(8,128)} custom-call(bf16[1,160,384]{2,1,0:T(8,128)(2,1)S(1)} %add.10.after_ref, f32[1,128]{1,0:T(1,128)S(1)} %get-tuple-element.85.head_ref, f32[2304,384]{1,0:T(8,128)S(1)} %get-tuple-element.79.acc6_ref.acc6, s32[2304,384]{1,0:T(8,128)S(1)} %get-tuple-element.80.noise6_ref.noise6), custom_call_target="tpu_custom_call" | custom-call | tf_op jit(solution)/shard_map/new_resid/pallas_call | solution.py:299
  61.2 3.8 %collective-permute-done.17.refs_4_ = bf16[1,160,384]{2,1,0:T(8,128)(2,1)S(1)} collective-permute-done((bf16[1,160,384]{2,1,0:T(8,128)(2,1)S(1)}, bf16[1,160,384]{2,1,0:T(8,128)(2,1)S(1)}, u32[]{:S(2)}, u32[]{:S(2)}) %collective-permute-start.17) | collective-permute-done | bytes 122912 | tf_op jit(solution)/shard_map/ppermute | solution.py:196
  65.1 0.6 collective-permute-start.18
  65.7 1.2 %hold_moments.1.held_ref = f32[1,160,384]{2,1,0:T(8,128)S(1)} custom-call(bf16[1,160,384]{2,1,0:T(8,128)(2,1)S(1)} %add.11.after_ref.mine_ref, f32[288,384]{1,0:T(8,128)} %m6_ref.1, f32[48,192]{1,0:T(8,128)} %m7_ref.1, f32[10,24]{1,0:T(8,128)} %bitcast.20), custom_call_target="tpu_custom_call" | custom-call | tf_op jit(solution)/shard_map/hold_moments/pallas_call | solution.py:299
  66.9 3.1 %collective-permute-done.18.theirs_ref = bf16[1,160,384]{2,1,0:T(8,128)(2,1)S(1)} collective-permute-done((bf16[1,160,384]{2,1,0:T(8,128)(2,1)S(1)}, bf16[1,160,384]{2,1,0:T(8,128)(2,1)S(1)}, u32[]{:S(2)}, u32[]{:S(2)}) %collective-permute-start.18) | collective-permute-done | bytes 122912 | tf_op jit(solution)/shard_map/ppermute | solution.py:196
  70.1 0.4 collective-permute-start.19
  70.5 0.8 collective-permute-start.20
  71.4 1.0 small_resids.1
  72.3 2.4 %new_resid.3.refs_0_ = f32[2304,384]{1,0:T(8,128)} custom-call(bf16[1,160,384]{2,1,0:T(8,128)(2,1)S(1)} %get-tuple-element.94.after_ref.own_ref, f32[1,128]{1,0:T(1,128)S(1)} %get-tuple-element.85.head_ref, f32[2304,384]{1,0:T(8,128)S(1)} %get-tuple-element.79.acc6_ref.acc6, ...), custom_call_target="tpu_custom_call", output_to_operand_aliasing={{}: (4, {})} | custom-call | tf_op jit(solution)/shard_map/new_resid/pallas_call | solution.py:299
  74.8 2.1 %collective-permute-done.19.far_ref = bf16[1,160,384]{2,1,0:T(8,128)(2,1)S(1)} collective-permute-done((bf16[1,160,384]{2,1,0:T(8,128)(2,1)S(1)}, bf16[1,160,384]{2,1,0:T(8,128)(2,1)S(1)}, u32[]{:S(2)}, u32[]{:S(2)}) %collective-permute-start.19) | collective-permute-done | bytes 122912 | tf_op jit(solution)/shard_map/ppermute | solution.py:196
  76.9 1.2 %collective-permute-start.21 = (bf16[1,160,384]{2,1,0:T(8,128)(2,1)S(1)}, bf16[1,160,384]{2,1,0:T(8,128)(2,1)S(1)}, u32[]{:S(2)}, u32[]{:S(2)}) collective-permute-start(bf16[1,160,384]{2,1,0:T(8,128)(2,1)S(1)} %get-tuple-element.97), channel_id=1, source_target_pairs={{0,1},{1,0},{2,3},{3,2},{4,5},{5,4},{6,7},{7,6},{8,10},{9,11},{10,... | collective-permute-start | bytes 368648 | tf_op jit(solution)/shard_map/ppermute | solution.py:196
  78.2 3.7 %collective-permute-done.21.one_ref = bf16[1,160,384]{2,1,0:T(8,128)(2,1)S(1)} collective-permute-done((bf16[1,160,384]{2,1,0:T(8,128)(2,1)S(1)}, bf16[1,160,384]{2,1,0:T(8,128)(2,1)S(1)}, u32[]{:S(2)}, u32[]{:S(2)}) %collective-permute-start.21) | collective-permute-done | bytes 122912 | tf_op jit(solution)/shard_map/ppermute | solution.py:196
  81.9 0.5 early_grams.1
  82.5 1.4 %collective-permute-start.23 = (bf16[1,160,384]{2,1,0:T(8,128)(2,1)S(1)}, bf16[1,160,384]{2,1,0:T(8,128)(2,1)S(1)}, u32[]{:S(2)}, u32[]{:S(2)}) collective-permute-start(bf16[1,160,384]{2,1,0:T(8,128)(2,1)S(1)} %collective-permute-done.21.one_ref), channel_id=1, source_target_pairs={{0,2},{1,3},{2,0},{3,1},{4,6},{5,7},{6,4},{7,5},{8,9},{9,8},{10,11... | collective-permute-start | bytes 368648 | tf_op jit(solution)/shard_map/ppermute | solution.py:196
  83.9 1.7 %collective-permute-done.22.in_ref = bf16[3,160,384]{2,1,0:T(8,128)(2,1)S(1)} collective-permute-done((bf16[3,160,384]{2,1,0:T(8,128)(2,1)S(1)}, bf16[3,160,384]{2,1,0:T(8,128)(2,1)S(1)}, u32[]{:S(2)}, u32[]{:S(2)}) %collective-permute-start.22) | collective-permute-done | bytes 368672 | tf_op jit(solution)/shard_map/ppermute | solution.py:196
  85.8 1.4 %momenta.1 = (f32[288,384]{1,0:T(8,128)}, f32[48,192]{1,0:T(8,128)}, f32[10,24]{1,0:T(8,128)}, f32[288,384]{1,0:T(8,128)S(1)}, f32[72,256]{1,0:T(8,128)S(1)}) custom-call(f32[1,160,384]{2,1,0:T(8,128)S(1)} %get-tuple-element.102.mine_ref, f32[1,160,384]{2,1,0:T(8,128)S(1)} %collective-permute-done.24.theirs_ref), custom_call_target="tpu_custom_call" | custom-call | tf_op jit(solution)/shard_map/momenta/pallas_call | solution.py:299
  87.5 0.4 collective-permute-start.27
  87.8 1.1 %late_grams.1 = (f32[384,384]{1,0:T(8,128)S(1)}, f32[256,256]{1,0:T(8,128)S(1)}, f32[384,384]{1,0:T(8,128)S(1)}, f32[256,256]{1,0:T(8,128)S(1)}) custom-call(f32[384,384]{1,0:T(8,128)S(1)} %get-tuple-element.99.refs_1_.own6_ref, f32[256,256]{1,0:T(8,128)S(1)} %get-tuple-element.100.refs_2_.own78_ref, bf16[3,160,384]{2,1,0:T(8,128)(2,1)S(1)} %passed.3.trio_ref, ...), custom_call_target="tpu_custom_call" | custom-call | tf_op jit(solution)/shard_map/late_grams/pallas_call | solution.py:299
  89.0 11.9 %update.1 = (f32[288,384]{1,0:T(8,128)}, f32[48,192]{1,0:T(8,128)}, f32[10,24]{1,0:T(8,128)}, bf16[288,384]{1,0:T(8,128)(2,1)}, bf16[48,192]{1,0:T(8,128)(2,1)}, /*index=5*/bf16[10,24]{1,0:T(8,128)(2,1)}) custom-call(f32[384,384]{1,0:T(8,128)S(1)} %get-tuple-element.104.own6, f32[256,256]{1,0:T(8,128)S(1)} %get-tuple-element.105.own78, ...), custom_call_target="tpu_custom_call" | custom-call | tf_op jit(solution)/shard_map/update/pallas_call | solution.py:299
  (51 shorter events, 2.5 us)
Async XLA Ops:
  1.8 10.1 %collective-permute-start = (bf16[1,160,384]{2,1,0:T(8,128)(2,1)S(1)}, bf16[1,160,384]{2,1,0:T(8,128)(2,1)S(1)}, u32[]{:S(2)}, u32[]{:S(2)}) collective-permute-start(bf16[1,160,384]{2,1,0:T(8,128)(2,1)S(1)} %pack_weights.1.after_ref.own_ref), channel_id=1, source_target_pairs={{0,4},{1,5},{2,6},{3,7},{4,0},{5,1},{6,2},{7,3},{8,12},{9,13},{10,... | collective-permute-start | bytes 368648 | tf_op jit(solution)/shard_map/ppermute | solution.py:196
  5.9 6.0 %collective-permute-start.1 = (bf16[1,160,384]{2,1,0:T(8,128)(2,1)S(1)}, bf16[1,160,384]{2,1,0:T(8,128)(2,1)S(1)}, u32[]{:S(2)}, u32[]{:S(2)}) collective-permute-start(bf16[1,160,384]{2,1,0:T(8,128)(2,1)S(1)} %pack_weights.1.after_ref.own_ref), channel_id=1, source_target_pairs={{0,1},{1,0},{2,3},{3,2},{4,5},{5,4},{6,7},{7,6},{8,10},{9,11},{10,... | collective-permute-start | bytes 368648 | tf_op jit(solution)/shard_map/ppermute | solution.py:196
  11.9 8.5 %collective-permute-start.3 = (bf16[3,160,384]{2,1,0:T(8,128)(2,1)S(1)}, bf16[3,160,384]{2,1,0:T(8,128)(2,1)S(1)}, u32[]{:S(2)}, u32[]{:S(2)}) collective-permute-start(bf16[3,160,384]{2,1,0:T(8,128)(2,1)S(1)} %get-tuple-element.70.trio_ref), channel_id=1, source_target_pairs={{0,2},{1,3},{2,0},{3,1},{4,6},{5,7},{6,4},{7,5},{8,9},{9,8},{10,11... | collective-permute-start | bytes 1105928 | tf_op jit(solution)/shard_map/ppermute | solution.py:196
  13.4 5.6 %collective-permute-start.2 = (bf16[1,160,384]{2,1,0:T(8,128)(2,1)S(1)}, bf16[1,160,384]{2,1,0:T(8,128)(2,1)S(1)}, u32[]{:S(2)}, u32[]{:S(2)}) collective-permute-start(bf16[1,160,384]{2,1,0:T(8,128)(2,1)S(1)} %get-tuple-element.71), channel_id=1, source_target_pairs={{0,1},{1,0},{2,3},{3,2},{4,5},{5,4},{6,7},{7,6},{8,10},{9,11},{10,... | collective-permute-start | bytes 368648 | tf_op jit(solution)/shard_map/ppermute | solution.py:196
  19.1 4.9 %collective-permute-start.4 = (bf16[1,160,384]{2,1,0:T(8,128)(2,1)S(1)}, bf16[1,160,384]{2,1,0:T(8,128)(2,1)S(1)}, u32[]{:S(2)}, u32[]{:S(2)}) collective-permute-start(bf16[1,160,384]{2,1,0:T(8,128)(2,1)S(1)} %collective-permute-done.2.one_ref), channel_id=1, source_target_pairs={{0,2},{1,3},{2,0},{3,1},{4,6},{5,7},{6,4},{7,5},{8,9},{9,8},{10,11... | collective-permute-start | bytes 368648 | tf_op jit(solution)/shard_map/ppermute | solution.py:196
  20.3 5.0 %collective-permute-start.5 = (bf16[4,160,384]{2,1,0:T(8,128)(2,1)S(1)}, bf16[4,160,384]{2,1,0:T(8,128)(2,1)S(1)}, u32[]{:S(2)}, u32[]{:S(2)}) collective-permute-start(bf16[4,160,384]{2,1,0:T(8,128)(2,1)S(1)} %relay.1.refs_0_), channel_id=1, source_target_pairs={{0,8},{1,9},{2,10},{3,11},{4,12},{5,13},{6,14},{7,15},{8,0},{9,1},... | collective-permute-start | bytes 1474568 | tf_op jit(solution)/shard_map/ppermute | solution.py:196
  20.5 4.9 %collective-permute-start.6 = (bf16[3,160,384]{2,1,0:T(8,128)(2,1)S(1)}, bf16[3,160,384]{2,1,0:T(8,128)(2,1)S(1)}, u32[]{:S(2)}, u32[]{:S(2)}) collective-permute-start(bf16[3,160,384]{2,1,0:T(8,128)(2,1)S(1)} %passed.2.refs_1_), channel_id=1, source_target_pairs={{0,8},{1,9},{2,10},{3,11},{4,12},{5,13},{6,14},{7,15},{8,0},{9,1},... | collective-permute-start | bytes 1105928 | tf_op jit(solution)/shard_map/ppermute | solution.py:196
  24.0 1.4 %collective-permute-start.7 = (bf16[1,160,384]{2,1,0:T(8,128)(2,1)S(1)}, bf16[1,160,384]{2,1,0:T(8,128)(2,1)S(1)}, u32[]{:S(2)}, u32[]{:S(2)}) collective-permute-start(bf16[1,160,384]{2,1,0:T(8,128)(2,1)S(1)} %passed_last.2.refs_2_), channel_id=1, source_target_pairs={{0,8},{1,9},{2,10},{3,11},{4,12},{5,13},{6,14},{7,15},{8,0},{9,1},... | collective-permute-start | bytes 368648 | tf_op jit(solution)/shard_map/ppermute | solution.py:196
  41.7 3.0 %collective-permute-start.9 = (bf16[3,160,384]{2,1,0:T(8,128)(2,1)S(1)}, bf16[3,160,384]{2,1,0:T(8,128)(2,1)S(1)}, u32[]{:S(2)}, u32[]{:S(2)}) collective-permute-start(bf16[3,160,384]{2,1,0:T(8,128)(2,1)S(1)} %codes.8.refs_2_), channel_id=1, source_target_pairs={{0,8},{1,9},{2,10},{3,11},{4,12},{5,13},{6,14},{7,15},{8,0},{9,1},... | collective-permute-start | bytes 1105928 | tf_op jit(solution)/shard_map/ppermute | solution.py:196
  41.9 1.7 %collective-permute-start.8 = (bf16[1,160,384]{2,1,0:T(8,128)(2,1)S(1)}, bf16[1,160,384]{2,1,0:T(8,128)(2,1)S(1)}, u32[]{:S(2)}, u32[]{:S(2)}) collective-permute-start(bf16[1,160,384]{2,1,0:T(8,128)(2,1)S(1)} %get-tuple-element.88), channel_id=1, source_target_pairs={{0,8},{1,9},{2,10},{3,11},{4,12},{5,13},{6,14},{7,15},{8,0},{9,1},... | collective-permute-start | bytes 368648 | tf_op jit(solution)/shard_map/ppermute | solution.py:196
  44.1 4.9 %collective-permute-start.11 = (bf16[1,160,384]{2,1,0:T(8,128)(2,1)S(1)}, bf16[1,160,384]{2,1,0:T(8,128)(2,1)S(1)}, u32[]{:S(2)}, u32[]{:S(2)}) collective-permute-start(bf16[1,160,384]{2,1,0:T(8,128)(2,1)S(1)} %add.6.refs_0_), channel_id=1, source_target_pairs={{0,2},{1,3},{2,0},{3,1},{4,6},{5,7},{6,4},{7,5},{8,9},{9,8},{10,11... | collective-permute-start | bytes 368648 | tf_op jit(solution)/shard_map/ppermute | solution.py:196
  44.9 4.1 %collective-permute-start.10 = (bf16[1,160,384]{2,1,0:T(8,128)(2,1)S(1)}, bf16[1,160,384]{2,1,0:T(8,128)(2,1)S(1)}, u32[]{:S(2)}, u32[]{:S(2)}) collective-permute-start(bf16[1,160,384]{2,1,0:T(8,128)(2,1)S(1)} %codes.11), channel_id=1, source_target_pairs={{0,8},{1,9},{2,10},{3,11},{4,12},{5,13},{6,14},{7,15},{8,0},{9,1},... | collective-permute-start | bytes 368648 | tf_op jit(solution)/shard_map/ppermute | solution.py:196
  49.5 7.7 %collective-permute-start.12 = (bf16[3,160,384]{2,1,0:T(8,128)(2,1)S(1)}, bf16[3,160,384]{2,1,0:T(8,128)(2,1)S(1)}, u32[]{:S(2)}, u32[]{:S(2)}) collective-permute-start(bf16[3,160,384]{2,1,0:T(8,128)(2,1)S(1)} %codes.13), channel_id=1, source_target_pairs={{0,8},{1,9},{2,10},{3,11},{4,12},{5,13},{6,14},{7,15},{8,0},{9,1},... | collective-permute-start | bytes 1105928 | tf_op jit(solution)/shard_map/ppermute | solution.py:196
  49.6 7.6 %collective-permute-start.14 = (bf16[2,160,384]{2,1,0:T(8,128)(2,1)S(1)}, bf16[2,160,384]{2,1,0:T(8,128)(2,1)S(1)}, u32[]{:S(2)}, u32[]{:S(2)}) collective-permute-start(bf16[2,160,384]{2,1,0:T(8,128)(2,1)S(1)} %add.7.refs_0_), channel_id=1, source_target_pairs={{0,2},{1,3},{2,0},{3,1},{4,6},{5,7},{6,4},{7,5},{8,9},{9,8},{10,11... | collective-permute-start | bytes 737288 | tf_op jit(solution)/shard_map/ppermute | solution.py:196
  50.2 7.0 %collective-permute-start.16 = (bf16[1,160,384]{2,1,0:T(8,128)(2,1)S(1)}, bf16[1,160,384]{2,1,0:T(8,128)(2,1)S(1)}, u32[]{:S(2)}, u32[]{:S(2)}) collective-permute-start(bf16[1,160,384]{2,1,0:T(8,128)(2,1)S(1)} %add.8.refs_0_.after_ref), channel_id=1, source_target_pairs={{0,1},{1,0},{2,3},{3,2},{4,5},{5,4},{6,7},{7,6},{8,10},{9,11},{10,... | collective-permute-start | bytes 368648 | tf_op jit(solution)/shard_map/ppermute | solution.py:196
  51.2 10.0 %collective-permute-start.13 = (bf16[1,160,384]{2,1,0:T(8,128)(2,1)S(1)}, bf16[1,160,384]{2,1,0:T(8,128)(2,1)S(1)}, u32[]{:S(2)}, u32[]{:S(2)}) collective-permute-start(bf16[1,160,384]{2,1,0:T(8,128)(2,1)S(1)} %add.9), channel_id=1, source_target_pairs={{0,2},{1,3},{2,0},{3,1},{4,6},{5,7},{6,4},{7,5},{8,9},{9,8},{10,11... | collective-permute-start | bytes 368648 | tf_op jit(solution)/shard_map/ppermute | solution.py:196
  57.3 7.7 %collective-permute-start.17 = (bf16[1,160,384]{2,1,0:T(8,128)(2,1)S(1)}, bf16[1,160,384]{2,1,0:T(8,128)(2,1)S(1)}, u32[]{:S(2)}, u32[]{:S(2)}) collective-permute-start(bf16[1,160,384]{2,1,0:T(8,128)(2,1)S(1)} %add.10.after_ref), channel_id=1, source_target_pairs={{0,4},{1,5},{2,6},{3,7},{4,0},{5,1},{6,2},{7,3},{8,12},{9,13},{10,... | collective-permute-start | bytes 368648 | tf_op jit(solution)/shard_map/ppermute | solution.py:196
  57.9 7.1 %collective-permute-start.15 = (bf16[1,160,384]{2,1,0:T(8,128)(2,1)S(1)}, bf16[1,160,384]{2,1,0:T(8,128)(2,1)S(1)}, u32[]{:S(2)}, u32[]{:S(2)}) collective-permute-start(bf16[1,160,384]{2,1,0:T(8,128)(2,1)S(1)} %add_far2.1), channel_id=1, source_target_pairs={{0,1},{1,0},{2,3},{3,2},{4,5},{5,4},{6,7},{7,6},{8,10},{9,11},{10,... | collective-permute-start | bytes 368648 | tf_op jit(solution)/shard_map/ppermute | solution.py:196
  65.1 4.9 %collective-permute-start.18 = (bf16[1,160,384]{2,1,0:T(8,128)(2,1)S(1)}, bf16[1,160,384]{2,1,0:T(8,128)(2,1)S(1)}, u32[]{:S(2)}, u32[]{:S(2)}) collective-permute-start(bf16[1,160,384]{2,1,0:T(8,128)(2,1)S(1)} %add.11.after_ref.mine_ref), channel_id=1, source_target_pairs={{0,16},{1,17},{2,18},{3,19},{4,20},{5,21},{6,22},{7,23},{8,24},{9,... | collective-permute-start | bytes 368648 | tf_op jit(solution)/shard_map/ppermute | solution.py:196
  70.1 6.8 %collective-permute-start.19 = (bf16[1,160,384]{2,1,0:T(8,128)(2,1)S(1)}, bf16[1,160,384]{2,1,0:T(8,128)(2,1)S(1)}, u32[]{:S(2)}, u32[]{:S(2)}) collective-permute-start(bf16[1,160,384]{2,1,0:T(8,128)(2,1)S(1)} %get-tuple-element.94.after_ref.own_ref), channel_id=1, source_target_pairs={{0,4},{1,5},{2,6},{3,7},{4,0},{5,1},{6,2},{7,3},{8,12},{9,13},{10,... | collective-permute-start | bytes 368648 | tf_op jit(solution)/shard_map/ppermute | solution.py:196
  70.5 6.4 %collective-permute-start.20 = (bf16[1,160,384]{2,1,0:T(8,128)(2,1)S(1)}, bf16[1,160,384]{2,1,0:T(8,128)(2,1)S(1)}, u32[]{:S(2)}, u32[]{:S(2)}) collective-permute-start(bf16[1,160,384]{2,1,0:T(8,128)(2,1)S(1)} %get-tuple-element.94.after_ref.own_ref), channel_id=1, source_target_pairs={{0,1},{1,0},{2,3},{3,2},{4,5},{5,4},{6,7},{7,6},{8,10},{9,11},{10,... | collective-permute-start | bytes 368648 | tf_op jit(solution)/shard_map/ppermute | solution.py:196
  76.9 4.9 %collective-permute-start.21 = (bf16[1,160,384]{2,1,0:T(8,128)(2,1)S(1)}, bf16[1,160,384]{2,1,0:T(8,128)(2,1)S(1)}, u32[]{:S(2)}, u32[]{:S(2)}) collective-permute-start(bf16[1,160,384]{2,1,0:T(8,128)(2,1)S(1)} %get-tuple-element.97), channel_id=1, source_target_pairs={{0,1},{1,0},{2,3},{3,2},{4,5},{5,4},{6,7},{7,6},{8,10},{9,11},{10,... | collective-permute-start | bytes 368648 | tf_op jit(solution)/shard_map/ppermute | solution.py:196
  78.2 7.5 %collective-permute-start.22 = (bf16[3,160,384]{2,1,0:T(8,128)(2,1)S(1)}, bf16[3,160,384]{2,1,0:T(8,128)(2,1)S(1)}, u32[]{:S(2)}, u32[]{:S(2)}) collective-permute-start(bf16[3,160,384]{2,1,0:T(8,128)(2,1)S(1)} %get-tuple-element.96.trio_ref), channel_id=1, source_target_pairs={{0,2},{1,3},{2,0},{3,1},{4,6},{5,7},{6,4},{7,5},{8,9},{9,8},{10,11... | collective-permute-start | bytes 1105928 | tf_op jit(solution)/shard_map/ppermute | solution.py:196
  82.4 3.4 %collective-permute-start.24 = (f32[1,160,384]{2,1,0:T(8,128)S(1)}, f32[1,160,384]{2,1,0:T(8,128)S(1)}, u32[]{:S(2)}, u32[]{:S(2)}) collective-permute-start(f32[1,160,384]{2,1,0:T(8,128)S(1)} %get-tuple-element.102.mine_ref), channel_id=1, source_target_pairs={{0,8},{1,9},{2,10},{3,11},{4,12},{5,13},{6,14},{7,15},{8,0},{9,1},... | collective-permute-start | bytes 737288 | tf_op jit(solution)/shard_map/ppermute | solution.py:196
  82.5 4.9 %collective-permute-start.23 = (bf16[1,160,384]{2,1,0:T(8,128)(2,1)S(1)}, bf16[1,160,384]{2,1,0:T(8,128)(2,1)S(1)}, u32[]{:S(2)}, u32[]{:S(2)}) collective-permute-start(bf16[1,160,384]{2,1,0:T(8,128)(2,1)S(1)} %collective-permute-done.21.one_ref), channel_id=1, source_target_pairs={{0,2},{1,3},{2,0},{3,1},{4,6},{5,7},{6,4},{7,5},{8,9},{9,8},{10,11... | collective-permute-start | bytes 368648 | tf_op jit(solution)/shard_map/ppermute | solution.py:196
  83.9 3.9 %collective-permute-start.25 = (bf16[4,160,384]{2,1,0:T(8,128)(2,1)S(1)}, bf16[4,160,384]{2,1,0:T(8,128)(2,1)S(1)}, u32[]{:S(2)}, u32[]{:S(2)}) collective-permute-start(bf16[4,160,384]{2,1,0:T(8,128)(2,1)S(1)} %get-tuple-element.101.refs_0_), channel_id=1, source_target_pairs={{0,8},{1,9},{2,10},{3,11},{4,12},{5,13},{6,14},{7,15},{8,0},{9,1},... | collective-permute-start | bytes 1474568 | tf_op jit(solution)/shard_map/ppermute | solution.py:196
  85.7 2.1 %collective-permute-start.26 = (bf16[3,160,384]{2,1,0:T(8,128)(2,1)S(1)}, bf16[3,160,384]{2,1,0:T(8,128)(2,1)S(1)}, u32[]{:S(2)}, u32[]{:S(2)}) collective-permute-start(bf16[3,160,384]{2,1,0:T(8,128)(2,1)S(1)} %passed.3.trio_ref), channel_id=1, source_target_pairs={{0,8},{1,9},{2,10},{3,11},{4,12},{5,13},{6,14},{7,15},{8,0},{9,1},... | collective-permute-start | bytes 1105928 | tf_op jit(solution)/shard_map/ppermute | solution.py:196
  87.4 1.5 %copy-start = (f32[288,384]{1,0:T(8,128)S(1)}, f32[288,384]{1,0:T(8,128)}, u32[]{:S(2)}) copy-start(f32[288,384]{1,0:T(8,128)} %refs_2_.3) | copy-start | bytes 1327108
  87.4 1.5 %copy-start.1 = (f32[48,192]{1,0:T(8,128)S(1)}, f32[48,192]{1,0:T(8,128)}, u32[]{:S(2)}) copy-start(f32[48,192]{1,0:T(8,128)} %refs_3_.3) | copy-start | bytes 110596
  87.4 1.6 %copy-start.2 = (f32[24,10]{0,1:T(8,128)S(1)}, f32[24,10]{0,1:T(8,128)}, u32[]{:S(2)}) copy-start(f32[24,10]{0,1:T(8,128)} %param.23) | copy-start | bytes 2884
  87.5 1.5 %collective-permute-start.27 = (bf16[1,160,384]{2,1,0:T(8,128)(2,1)S(1)}, bf16[1,160,384]{2,1,0:T(8,128)(2,1)S(1)}, u32[]{:S(2)}, u32[]{:S(2)}) collective-permute-start(bf16[1,160,384]{2,1,0:T(8,128)(2,1)S(1)} %passed_last.3.one_ref), channel_id=1, source_target_pairs={{0,8},{1,9},{2,10},{3,11},{4,12},{5,13},{6,14},{7,15},{8,0},{9,1},... | collective-permute-start | bytes 368648 | tf_op jit(solution)/shard_map/ppermute | solution.py:196

commit v3 on v2

--- a/solution.py
+++ b/solution.py
@@ -264,7 +264,7 @@
     return jax.ShapeDtypeStruct(shape, dtype)
 
 
-MICROS = {"passed_near": 0.6, "passed_last": 20.0}
+MICROS = {"passed_last": 20.0}
 
 
 def placed(shape, spec):
@@ -412,15 +412,20 @@
     again_ref[...] = far_ref[...]
 
 
-def relay_kernel(trio_ref, one_ref, out_ref):
+def relay_kernel(trio_ref, one_ref, *refs):
+    outs = refs[len(refs) // 2 :]
     count = trio_ref.shape[0]
-    out_ref[:count] = trio_ref[...]
-    out_ref[count:] = one_ref[...]
-
-
-def relay(trio, one):
-    shape = shape_of((trio.shape[0] + one.shape[0],) + one.shape[1:], one.dtype)
-    return call(relay_kernel, "relay", [VMEM] * 2, VMEM, shape)(trio, one)
+    outs[0][:count] = trio_ref[...]
+    outs[0][count:] = one_ref[...]
+    if len(refs) > 1:
+        outs[1][...] = refs[0][...]
+
+
+def relay(trio, one, beside=()):
+    joined = shape_of((trio.shape[0] + one.shape[0],) + one.shape[1:], one.dtype)
+    shapes = [joined] + [shape_of(array.shape, array.dtype) for array in beside]
+    ins = [trio, one, *beside]
+    return call(relay_kernel, "relay", [VMEM] * len(ins), [VMEM] * len(shapes), shapes)(*ins)
 
 
 def gather_halves(own, after=(), work=None):
@@ -433,12 +438,12 @@
         [VMEM] * 2,
         [shape_of((3,) + own.shape[1:], BF16), shape_of(own.shape, BF16)],
     )(own, far, mid, *[array for _, array in after])
+    trio4 = swap(trio, wide_perm(0))
     one3 = swap(far, wide_perm(1))
-    trio4 = swap(trio, wide_perm(0))
     one7 = swap(one3, wide_perm(0))
-    four, done = (relay(trio, one3), None) if work is None else work(trio, one3)
+    four, done = (relay(trio, one3)[0], None) if work is None else work(trio, one3)
     trio4 = passed(trio4, (four,))
-    one7 = passed(one7, done[:3] if done else (), "passed_last")
+    one7 = passed(one7, done[:3] if done else (four,), "passed_last")
     mine = (four, trio4, one7)
     return (*mine, *[swap(part, grp_perm(1)) for part in mine]), done
 
@@ -744,9 +749,7 @@
     return mxu(block, block, 0, 0), mxu(region, region, 0, 0)
 
 
-def early_kernel(sizes, trio_ref, one_ref, moment_ref, four_ref, out6_ref, out78_ref, again_ref):
-    relay_kernel(trio_ref, one_ref, four_ref)
-    again_ref[...] = moment_ref[...]
+def early_kernel(sizes, four_ref, out6_ref, out78_ref):
     out6_ref[...], out78_ref[...] = grams_of(sizes, four_ref)
 
 
@@ -926,20 +929,15 @@
         )(head, acc6, noise6, code7, code8, *after)
 
     got7 = swap(sent7, grp_perm(1))
-    kept7 = codes((7,), True)
-    sent456 = codes((4, 5, 6), False, (kept7,))
-    got456 = swap(sent456, grp_perm(1))
-    out7 = add((0, 0), (kept7, got7), 1, [(VMEM, sent456)])
+    out7 = add((0, 0), (codes((7,), True), got7), 1)
     near7 = swap(out7, wide_perm(0))
-    kept456 = codes((4, 5, 6), True, (out7,))
-    out56 = add((1, 1), (kept456, got456), 2)
-    near56 = swap(out56, wide_perm(0))
-    near4 = swap(add((0, 0), (kept456, got456), 1), wide_perm(0))
-    got3 = swap(codes((3,), False, (out56,)), grp_perm(1))
-    far3 = add((0, 0, 0), (codes((3,), True, (out56,)), got3, near7), 1)
+    rest = tuple(range(7))
+    got = swap(codes(rest, False, (out7,)), grp_perm(1))
+    kept = codes(rest, True, (out7,))
+    near56 = swap(add((5, 5), (kept, got), 2), wide_perm(0))
+    near4 = swap(add((4, 4), (kept, got), 1), wide_perm(0))
+    far3 = add((3, 3, 0), (kept, got, near7), 1)
     near56 = passed(near56, (far3,), "passed_near")
-    got012 = swap(codes((0, 1, 2), False, (far3,)), grp_perm(1))
-    kept012 = codes((0, 1, 2), True, (far3,))
     totals = call(
         totals_kernel,
         "totals",
@@ -950,12 +948,12 @@
     )(far3, all_stats, *bias_rows)
     flat = totals[:3]
     far3 = swap(far3, wide_perm(1))
-    far2 = add((2, 2, 1), (kept012, got012, near56), 1, name="add_far2")
+    far2 = add((2, 2, 1), (kept, got, near56), 1, name="add_far2")
     far2 = swap(far2, wide_perm(1))
-    last = add((1, 1, 0, 0), (kept012, got012, near56, far3), 1, [(HBM, row) for row in flat])
+    last = add((1, 1, 0, 0), (kept, got, near56, far3), 1, [(HBM, row) for row in flat])
     new_resid6 = new_resid6_part(0, ins // 2, last, head, acc6, noise6)
     last = swap(last, wide_perm(2))
-    mine = add((0,) * 5, (kept012, got012, near4, far2, last), 1, [(HBM, new_resid6)])
+    mine = add((0,) * 5, (kept, got, near4, far2, last), 1, [(HBM, new_resid6)])
     held = hold_moments(mine, moment6, moment7, moment8)
     theirs = swap(mine, grp_perm(2))
 
@@ -979,14 +977,15 @@
     grams = [shape_of((h1, h1)), shape_of((2 * LANE, 2 * LANE))]
 
     def beside_last(trio, one3):
-        four, *early, again = call(
+        four, again = relay(trio, one3, (moment,))
+        early = call(
             functools.partial(early_kernel, sizes),
             "early_grams",
-            [VMEM] * 3,
-            [VMEM] * 4,
-            [halves_of(4), *grams, shape_of((1,) + half)],
+            [VMEM],
+            [VMEM] * 2,
+            grams,
             megabytes=8,
-        )(trio, one3, moment)
+        )(four)
         momenta = call(
             functools.partial(momenta_kernel, sizes),
             "momenta",

time: 101 us -> 98.3 us (0.973)
  waiting for transfers between devices: 31.9 us -> 29.8 us
    ppermute x28 -> x26, waiting for transfers between devices: 31.9 us -> 29.8 us  [swap(): return lax.ppermute(array, BOTH, perm)]
    ppermute x28 -> x26, starting transfers between devices: 20.8 us -> 20.2 us  [swap(): return lax.ppermute(array, BOTH, perm)]
    pallas_call x36 -> x33, Pallas kernels: 34.4 us -> 34.3 us  [run(): kernel_call(*[pltpu.with_memory_space_constraint(array, pltpu.HBM) if spe...]
  transfers between devices with their start and end apart: 28 -> 26, of which waited for: 13 -> 15; matrix products, arithmetic and copies ran while one was open for 0% -> 0% of each run, Pallas kernels for 16% -> 17%
where the time goes in v3:
time: 98.3 us; the launch traced here: 98.1 us
  Pallas kernels  34.3 us (35%)
  waiting for transfers between devices  29.8 us (30%)
  starting transfers between devices  20.2 us (21%)
  blocking collectives  12.2 us (12%)
  between operations  1.61 us (2%)
    pallas_call x33, Pallas kernels, run(): kernel_call(*[pltpu.with_memory_space_constraint(array, pltpu.HBM) if spe...  34.3 us
    ppermute x26, waiting for transfers between devices, swap(): return lax.ppermute(array, BOTH, perm)  29.8 us
    ppermute x26, starting transfers between devices, swap(): return lax.ppermute(array, BOTH, perm)  20.2 us
    all_to_all x1, blocking collectives, paired_plan(): all_stats = lax.all_to_all(stats, BOTH, 0, 0, tiled=True)  12.2 us
  transfers between devices with their start and end apart: 26, of which 15 were waited for; matrix products, arithmetic and copies ran while one was open for 0% of the time, Pallas kernels for 17%

profile of v3, /device:TPU:0, one launch (start us, length us, event | category | flops | bytes accessed | tf_op | source)
XLA Modules:
  0.0 98.1 jit_solution(13303411433273114342)
XLA Ops:
  0.7 1.2 %pack_weights.1.after_ref.own_ref = bf16[1,160,384]{2,1,0:T(8,128)(2,1)S(1)} custom-call(f32[288,384]{1,0:T(8,128)} %refs_2_.3, f32[48,192]{1,0:T(8,128)} %refs_3_.3, f32[10,24]{1,0:T(8,128)} %bitcast.13), custom_call_target="tpu_custom_call" | custom-call | tf_op jit(solution)/shard_map/pack_weights/pallas_call | solution.py:299
  1.8 4.1 %collective-permute-start = (bf16[1,160,384]{2,1,0:T(8,128)(2,1)S(1)}, bf16[1,160,384]{2,1,0:T(8,128)(2,1)S(1)}, u32[]{:S(2)}, u32[]{:S(2)}) collective-permute-start(bf16[1,160,384]{2,1,0:T(8,128)(2,1)S(1)} %pack_weights.1.after_ref.own_ref), channel_id=1, source_target_pairs={{0,4},{1,5},{2,6},{3,7},{4,0},{5,1},{6,2},{7,3},{8,12},{9,13},{10,... | collective-permute-start | bytes 368648 | tf_op jit(solution)/shard_map/ppermute | solution.py:196
  5.9 1.5 %collective-permute-start.1 = (bf16[1,160,384]{2,1,0:T(8,128)(2,1)S(1)}, bf16[1,160,384]{2,1,0:T(8,128)(2,1)S(1)}, u32[]{:S(2)}, u32[]{:S(2)}) collective-permute-start(bf16[1,160,384]{2,1,0:T(8,128)(2,1)S(1)} %pack_weights.1.after_ref.own_ref), channel_id=1, source_target_pairs={{0,1},{1,0},{2,3},{3,2},{4,5},{5,4},{6,7},{7,6},{8,10},{9,11},{10,... | collective-permute-start | bytes 368648 | tf_op jit(solution)/shard_map/ppermute | solution.py:196
  8.1 3.6 %stage.1 = (bf16[192,2304]{1,0:T(8,128)(2,1)S(1)}, s32[1,192]{1,0:T(1,128)S(1)}, f32[1,586]{1,0:T(1,128)S(1)}, f32[1,586]{1,0:T(1,128)S(1)}, f32[1,586]{1,0:T(1,...) custom-call(bf16[1,160,384]{2,1,0:T(8,128)(2,1)S(1)} %pack_weights.1, ...), custom_call_target="tpu_custom_call" | custom-call | tf_op jit(solution)/shard_map/stage/pallas_call | solution.py:299
  11.9 1.5 %collective-permute-start.3 = (bf16[3,160,384]{2,1,0:T(8,128)(2,1)S(1)}, bf16[3,160,384]{2,1,0:T(8,128)(2,1)S(1)}, u32[]{:S(2)}, u32[]{:S(2)}) collective-permute-start(bf16[3,160,384]{2,1,0:T(8,128)(2,1)S(1)} %get-tuple-element.70.trio_ref), channel_id=1, source_target_pairs={{0,2},{1,3},{2,0},{3,1},{4,6},{5,7},{6,4},{7,5},{8,9},{9,8},{10,11... | collective-permute-start | bytes 1105928 | tf_op jit(solution)/shard_map/ppermute | solution.py:196
  13.4 0.8 collective-permute-start.2
  14.2 4.9 %collective-permute-done.2.one_ref = bf16[1,160,384]{2,1,0:T(8,128)(2,1)S(1)} collective-permute-done((bf16[1,160,384]{2,1,0:T(8,128)(2,1)S(1)}, bf16[1,160,384]{2,1,0:T(8,128)(2,1)S(1)}, u32[]{:S(2)}, u32[]{:S(2)}) %collective-permute-start.2) | collective-permute-done | bytes 122912 | tf_op jit(solution)/shard_map/ppermute | solution.py:196
  19.1 1.2 %collective-permute-start.4 = (bf16[1,160,384]{2,1,0:T(8,128)(2,1)S(1)}, bf16[1,160,384]{2,1,0:T(8,128)(2,1)S(1)}, u32[]{:S(2)}, u32[]{:S(2)}) collective-permute-start(bf16[1,160,384]{2,1,0:T(8,128)(2,1)S(1)} %collective-permute-done.2.one_ref), channel_id=1, source_target_pairs={{0,2},{1,3},{2,0},{3,1},{4,6},{5,7},{6,4},{7,5},{8,9},{9,8},{10,11... | collective-permute-start | bytes 368648 | tf_op jit(solution)/shard_map/ppermute | solution.py:196
  20.5 0.5 collective-permute-start.6
  21.0 2.9 %collective-permute-done.4.in_ref = bf16[1,160,384]{2,1,0:T(8,128)(2,1)S(1)} collective-permute-done((bf16[1,160,384]{2,1,0:T(8,128)(2,1)S(1)}, bf16[1,160,384]{2,1,0:T(8,128)(2,1)S(1)}, u32[]{:S(2)}, u32[]{:S(2)}) %collective-permute-start.4) | collective-permute-done | bytes 122912 | tf_op jit(solution)/shard_map/ppermute | solution.py:196
  24.1 1.3 %collective-permute-done.7.refs_5_ = bf16[1,160,384]{2,1,0:T(8,128)(2,1)S(1)} collective-permute-done((bf16[1,160,384]{2,1,0:T(8,128)(2,1)S(1)}, bf16[1,160,384]{2,1,0:T(8,128)(2,1)S(1)}, u32[]{:S(2)}, u32[]{:S(2)}) %collective-permute-start.7) | collective-permute-done | bytes 122912 | tf_op jit(solution)/shard_map/ppermute | solution.py:196
  25.4 2.9 %worker.1 = (f32[2304,384]{1,0:T(8,128)S(1)}, f32[192,384]{1,0:T(8,128)S(1)}, f32[10,192]{1,0:T(8,128)S(1)}, f32[32,1,640]{2,1,0:T(1,128)S(1)}) custom-call(bf16[4,160,384]{2,1,0:T(8,128)(2,1)S(1)} %relay.2.refs_0_, bf16[3,160,384]{2,1,0:T(8,128)(2,1)S(1)} %passed.2.refs_1_, bf16[1,160,384]{2,1,0:T(8,128)(2,1)S(1)} %passed_last.2.refs_2_, ...), custom_call_target="tpu_custom_call" | custom-call | tf_op jit(solution)/shard_map/worker/pallas_call | solution.py:299
  28.3 12.2 %all_to_all.5.stats_ref = f32[32,1,640]{2,1,0:T(1,128)S(1)} all-to-all(f32[32,1,640]{2,1,0:T(1,128)S(1)} %get-tuple-element.78.mine_ref), channel_id=1, replica_groups=mesh['grp'=4,'wide'=8] {'grp','wide'}, dimensions={0} | all-to-all | bytes 163840 | tf_op jit(solution)/shard_map/all_to_all | solution.py:904
  40.5 0.6 codes_first.1
  41.5 1.1 %collective-permute-done.8.refs_1_ = bf16[1,160,384]{2,1,0:T(8,128)(2,1)S(1)} collective-permute-done((bf16[1,160,384]{2,1,0:T(8,128)(2,1)S(1)}, bf16[1,160,384]{2,1,0:T(8,128)(2,1)S(1)}, u32[]{:S(2)}, u32[]{:S(2)}) %collective-permute-start.8) | collective-permute-done | bytes 122912 | tf_op jit(solution)/shard_map/ppermute | solution.py:196
  42.6 0.9 codes.5
  43.7 0.9 codes.4.refs_0_
  44.6 0.6 collective-permute-start.12
  45.2 0.7 collective-permute-done.9.refs_1_
  46.0 0.8 collective-permute-start.11
  46.9 2.7 %collective-permute-done.12.refs_2_ = bf16[1,160,384]{2,1,0:T(8,128)(2,1)S(1)} collective-permute-done((bf16[1,160,384]{2,1,0:T(8,128)(2,1)S(1)}, bf16[1,160,384]{2,1,0:T(8,128)(2,1)S(1)}, u32[]{:S(2)}, u32[]{:S(2)}) %collective-permute-start.12) | collective-permute-done | bytes 122912 | tf_op jit(solution)/shard_map/ppermute | solution.py:196
  49.6 0.9 collective-permute-start.14
  50.6 0.7 collective-permute-start.10
  51.3 1.3 %totals.1 = (f32[586]{0:T(1024)}, f32[586]{0:T(1024)}, f32[586]{0:T(1024)}, f32[1,1]{1,0:T(1,128)}, f32[1,1]{1,0:T(1,128)}) custom-call(bf16[1,160,384]{2,1,0:T(8,128)(2,1)S(1)} %add.9.refs_0_.after_ref, f32[32,1,640]{2,1,0:T(1,128)S(1)} %all_to_all.5.stats_ref, f32[1,586]{1,0:T(1,128)S(1)} %get-tuple-element.74.refs_9_.bias_ref, ...), custom_call_target="tpu_custom_call" | custom-call | tf_op jit(solution)/shard_map/totals/pallas_call | solution.py:299
  52.7 2.0 %collective-permute-done.14.refs_3_ = bf16[1,160,384]{2,1,0:T(8,128)(2,1)S(1)} collective-permute-done((bf16[1,160,384]{2,1,0:T(8,128)(2,1)S(1)}, bf16[1,160,384]{2,1,0:T(8,128)(2,1)S(1)}, u32[]{:S(2)}, u32[]{:S(2)}) %collective-permute-start.14) | collective-permute-done | bytes 122912 | tf_op jit(solution)/shard_map/ppermute | solution.py:196
  54.9 1.0 collective-permute-start.15
  55.9 1.1 %collective-permute-start.13 = (bf16[1,160,384]{2,1,0:T(8,128)(2,1)S(1)}, bf16[1,160,384]{2,1,0:T(8,128)(2,1)S(1)}, u32[]{:S(2)}, u32[]{:S(2)}) collective-permute-start(bf16[1,160,384]{2,1,0:T(8,128)(2,1)S(1)} %add_far2.1), channel_id=1, source_target_pairs={{0,1},{1,0},{2,3},{3,2},{4,5},{5,4},{6,7},{7,6},{8,10},{9,11},{10,... | collective-permute-start | bytes 368648 | tf_op jit(solution)/shard_map/ppermute | solution.py:196
  57.0 2.4 %new_resid.2.refs_5_.refs_0_ = f32[2304,384]{1,0:T(8,128)} custom-call(bf16[1,160,384]{2,1,0:T(8,128)(2,1)S(1)} %add.10.after_ref, f32[1,128]{1,0:T(1,128)S(1)} %get-tuple-element.85.head_ref, f32[2304,384]{1,0:T(8,128)S(1)} %get-tuple-element.79.acc6_ref.acc6, s32[2304,384]{1,0:T(8,128)S(1)} %get-tuple-element.80.noise6_ref.noise6), custom_call_target="tpu_custom_call" | custom-call | tf_op jit(solution)/shard_map/new_resid/pallas_call | solution.py:299
  59.4 3.2 %collective-permute-done.15.refs_4_ = bf16[1,160,384]{2,1,0:T(8,128)(2,1)S(1)} collective-permute-done((bf16[1,160,384]{2,1,0:T(8,128)(2,1)S(1)}, bf16[1,160,384]{2,1,0:T(8,128)(2,1)S(1)}, u32[]{:S(2)}, u32[]{:S(2)}) %collective-permute-start.15) | collective-permute-done | bytes 122912 | tf_op jit(solution)/shard_map/ppermute | solution.py:196
  62.7 0.8 collective-permute-start.16
  63.5 1.2 %hold_moments.1.held_ref = f32[1,160,384]{2,1,0:T(8,128)S(1)} custom-call(bf16[1,160,384]{2,1,0:T(8,128)(2,1)S(1)} %add.11.after_ref.mine_ref, f32[288,384]{1,0:T(8,128)} %m6_ref.1, f32[48,192]{1,0:T(8,128)} %m7_ref.1, f32[10,24]{1,0:T(8,128)} %bitcast.20), custom_call_target="tpu_custom_call" | custom-call | tf_op jit(solution)/shard_map/hold_moments/pallas_call | solution.py:299
  64.7 3.0 %collective-permute-done.16.theirs_ref = bf16[1,160,384]{2,1,0:T(8,128)(2,1)S(1)} collective-permute-done((bf16[1,160,384]{2,1,0:T(8,128)(2,1)S(1)}, bf16[1,160,384]{2,1,0:T(8,128)(2,1)S(1)}, u32[]{:S(2)}, u32[]{:S(2)}) %collective-permute-start.16) | collective-permute-done | bytes 122912 | tf_op jit(solution)/shard_map/ppermute | solution.py:196
  67.8 0.3 collective-permute-start.17
  68.1 1.0 collective-permute-start.18
  69.0 1.0 small_resids.1
  70.0 2.4 %new_resid.3.refs_0_ = f32[2304,384]{1,0:T(8,128)} custom-call(bf16[1,160,384]{2,1,0:T(8,128)(2,1)S(1)} %get-tuple-element.94.after_ref.own_ref, f32[1,128]{1,0:T(1,128)S(1)} %get-tuple-element.85.head_ref, f32[2304,384]{1,0:T(8,128)S(1)} %get-tuple-element.79.acc6_ref.acc6, ...), custom_call_target="tpu_custom_call", output_to_operand_aliasing={{}: (4, {})} | custom-call | tf_op jit(solution)/shard_map/new_resid/pallas_call | solution.py:299
  72.4 2.2 %collective-permute-done.17.far_ref = bf16[1,160,384]{2,1,0:T(8,128)(2,1)S(1)} collective-permute-done((bf16[1,160,384]{2,1,0:T(8,128)(2,1)S(1)}, bf16[1,160,384]{2,1,0:T(8,128)(2,1)S(1)}, u32[]{:S(2)}, u32[]{:S(2)}) %collective-permute-start.17) | collective-permute-done | bytes 122912 | tf_op jit(solution)/shard_map/ppermute | solution.py:196
  74.6 0.5 collective-permute-start.19
  75.1 0.3 collective-permute-start.20
  75.4 4.2 %collective-permute-done.19.one_ref = bf16[1,160,384]{2,1,0:T(8,128)(2,1)S(1)} collective-permute-done((bf16[1,160,384]{2,1,0:T(8,128)(2,1)S(1)}, bf16[1,160,384]{2,1,0:T(8,128)(2,1)S(1)}, u32[]{:S(2)}, u32[]{:S(2)}) %collective-permute-start.19) | collective-permute-done | bytes 122912 | tf_op jit(solution)/shard_map/ppermute | solution.py:196
  79.7 1.4 %collective-permute-start.21 = (bf16[1,160,384]{2,1,0:T(8,128)(2,1)S(1)}, bf16[1,160,384]{2,1,0:T(8,128)(2,1)S(1)}, u32[]{:S(2)}, u32[]{:S(2)}) collective-permute-start(bf16[1,160,384]{2,1,0:T(8,128)(2,1)S(1)} %collective-permute-done.19.one_ref), channel_id=1, source_target_pairs={{0,2},{1,3},{2,0},{3,1},{4,6},{5,7},{6,4},{7,5},{8,9},{9,8},{10,11... | collective-permute-start | bytes 368648 | tf_op jit(solution)/shard_map/ppermute | solution.py:196
  81.1 0.5 early_grams.1
  81.7 1.4 %momenta.1 = (f32[288,384]{1,0:T(8,128)}, f32[48,192]{1,0:T(8,128)}, f32[10,24]{1,0:T(8,128)}, f32[288,384]{1,0:T(8,128)S(1)}, f32[72,256]{1,0:T(8,128)S(1)}) custom-call(f32[1,160,384]{2,1,0:T(8,128)S(1)} %get-tuple-element.102.mine_ref, f32[1,160,384]{2,1,0:T(8,128)S(1)} %collective-permute-done.22.theirs_ref), custom_call_target="tpu_custom_call" | custom-call | tf_op jit(solution)/shard_map/momenta/pallas_call | solution.py:299
  83.2 0.5 collective-permute-start.24
  83.7 0.9 collective-permute-done.21.in_ref
  84.8 0.3 collective-permute-done.24.trio2_ref
  85.0 1.1 %late_grams.1 = (f32[384,384]{1,0:T(8,128)S(1)}, f32[256,256]{1,0:T(8,128)S(1)}, f32[384,384]{1,0:T(8,128)S(1)}, f32[256,256]{1,0:T(8,128)S(1)}) custom-call(f32[384,384]{1,0:T(8,128)S(1)} %get-tuple-element.100.refs_1_.own6_ref, f32[256,256]{1,0:T(8,128)S(1)} %get-tuple-element.101.refs_2_.own78_ref, bf16[3,160,384]{2,1,0:T(8,128)(2,1)S(1)} %passed.3.trio_ref, ...), custom_call_target="tpu_custom_call" | custom-call | tf_op jit(solution)/shard_map/late_grams/pallas_call | solution.py:299
  86.2 11.9 %update.1 = (f32[288,384]{1,0:T(8,128)}, f32[48,192]{1,0:T(8,128)}, f32[10,24]{1,0:T(8,128)}, bf16[288,384]{1,0:T(8,128)(2,1)}, bf16[48,192]{1,0:T(8,128)(2,1)}, /*index=5*/bf16[10,24]{1,0:T(8,128)(2,1)}) custom-call(f32[384,384]{1,0:T(8,128)S(1)} %get-tuple-element.104.own6, f32[256,256]{1,0:T(8,128)S(1)} %get-tuple-element.105.own78, ...), custom_call_target="tpu_custom_call" | custom-call | tf_op jit(solution)/shard_map/update/pallas_call | solution.py:299
  (44 shorter events, 2.1 us)
Async XLA Ops:
  1.8 10.1 %collective-permute-start = (bf16[1,160,384]{2,1,0:T(8,128)(2,1)S(1)}, bf16[1,160,384]{2,1,0:T(8,128)(2,1)S(1)}, u32[]{:S(2)}, u32[]{:S(2)}) collective-permute-start(bf16[1,160,384]{2,1,0:T(8,128)(2,1)S(1)} %pack_weights.1.after_ref.own_ref), channel_id=1, source_target_pairs={{0,4},{1,5},{2,6},{3,7},{4,0},{5,1},{6,2},{7,3},{8,12},{9,13},{10,... | collective-permute-start | bytes 368648 | tf_op jit(solution)/shard_map/ppermute | solution.py:196
  5.9 6.0 %collective-permute-start.1 = (bf16[1,160,384]{2,1,0:T(8,128)(2,1)S(1)}, bf16[1,160,384]{2,1,0:T(8,128)(2,1)S(1)}, u32[]{:S(2)}, u32[]{:S(2)}) collective-permute-start(bf16[1,160,384]{2,1,0:T(8,128)(2,1)S(1)} %pack_weights.1.after_ref.own_ref), channel_id=1, source_target_pairs={{0,1},{1,0},{2,3},{3,2},{4,5},{5,4},{6,7},{7,6},{8,10},{9,11},{10,... | collective-permute-start | bytes 368648 | tf_op jit(solution)/shard_map/ppermute | solution.py:196
  11.9 8.5 %collective-permute-start.3 = (bf16[3,160,384]{2,1,0:T(8,128)(2,1)S(1)}, bf16[3,160,384]{2,1,0:T(8,128)(2,1)S(1)}, u32[]{:S(2)}, u32[]{:S(2)}) collective-permute-start(bf16[3,160,384]{2,1,0:T(8,128)(2,1)S(1)} %get-tuple-element.70.trio_ref), channel_id=1, source_target_pairs={{0,2},{1,3},{2,0},{3,1},{4,6},{5,7},{6,4},{7,5},{8,9},{9,8},{10,11... | collective-permute-start | bytes 1105928 | tf_op jit(solution)/shard_map/ppermute | solution.py:196
  13.4 5.6 %collective-permute-start.2 = (bf16[1,160,384]{2,1,0:T(8,128)(2,1)S(1)}, bf16[1,160,384]{2,1,0:T(8,128)(2,1)S(1)}, u32[]{:S(2)}, u32[]{:S(2)}) collective-permute-start(bf16[1,160,384]{2,1,0:T(8,128)(2,1)S(1)} %get-tuple-element.71), channel_id=1, source_target_pairs={{0,1},{1,0},{2,3},{3,2},{4,5},{5,4},{6,7},{7,6},{8,10},{9,11},{10,... | collective-permute-start | bytes 368648 | tf_op jit(solution)/shard_map/ppermute | solution.py:196
  19.1 4.9 %collective-permute-start.4 = (bf16[1,160,384]{2,1,0:T(8,128)(2,1)S(1)}, bf16[1,160,384]{2,1,0:T(8,128)(2,1)S(1)}, u32[]{:S(2)}, u32[]{:S(2)}) collective-permute-start(bf16[1,160,384]{2,1,0:T(8,128)(2,1)S(1)} %collective-permute-done.2.one_ref), channel_id=1, source_target_pairs={{0,2},{1,3},{2,0},{3,1},{4,6},{5,7},{6,4},{7,5},{8,9},{9,8},{10,11... | collective-permute-start | bytes 368648 | tf_op jit(solution)/shard_map/ppermute | solution.py:196
  20.3 5.0 %collective-permute-start.5 = (bf16[4,160,384]{2,1,0:T(8,128)(2,1)S(1)}, bf16[4,160,384]{2,1,0:T(8,128)(2,1)S(1)}, u32[]{:S(2)}, u32[]{:S(2)}) collective-permute-start(bf16[4,160,384]{2,1,0:T(8,128)(2,1)S(1)} %relay.2.refs_0_), channel_id=1, source_target_pairs={{0,8},{1,9},{2,10},{3,11},{4,12},{5,13},{6,14},{7,15},{8,0},{9,1},... | collective-permute-start | bytes 1474568 | tf_op jit(solution)/shard_map/ppermute | solution.py:196
  20.5 4.9 %collective-permute-start.6 = (bf16[3,160,384]{2,1,0:T(8,128)(2,1)S(1)}, bf16[3,160,384]{2,1,0:T(8,128)(2,1)S(1)}, u32[]{:S(2)}, u32[]{:S(2)}) collective-permute-start(bf16[3,160,384]{2,1,0:T(8,128)(2,1)S(1)} %passed.2.refs_1_), channel_id=1, source_target_pairs={{0,8},{1,9},{2,10},{3,11},{4,12},{5,13},{6,14},{7,15},{8,0},{9,1},... | collective-permute-start | bytes 1105928 | tf_op jit(solution)/shard_map/ppermute | solution.py:196
  24.0 1.4 %collective-permute-start.7 = (bf16[1,160,384]{2,1,0:T(8,128)(2,1)S(1)}, bf16[1,160,384]{2,1,0:T(8,128)(2,1)S(1)}, u32[]{:S(2)}, u32[]{:S(2)}) collective-permute-start(bf16[1,160,384]{2,1,0:T(8,128)(2,1)S(1)} %passed_last.2.refs_2_), channel_id=1, source_target_pairs={{0,8},{1,9},{2,10},{3,11},{4,12},{5,13},{6,14},{7,15},{8,0},{9,1},... | collective-permute-start | bytes 368648 | tf_op jit(solution)/shard_map/ppermute | solution.py:196
  41.2 1.4 %collective-permute-start.8 = (bf16[1,160,384]{2,1,0:T(8,128)(2,1)S(1)}, bf16[1,160,384]{2,1,0:T(8,128)(2,1)S(1)}, u32[]{:S(2)}, u32[]{:S(2)}) collective-permute-start(bf16[1,160,384]{2,1,0:T(8,128)(2,1)S(1)} %get-tuple-element.88), channel_id=1, source_target_pairs={{0,8},{1,9},{2,10},{3,11},{4,12},{5,13},{6,14},{7,15},{8,0},{9,1},... | collective-permute-start | bytes 368648 | tf_op jit(solution)/shard_map/ppermute | solution.py:196
  43.5 2.5 %collective-permute-start.9 = (bf16[7,160,384]{2,1,0:T(8,128)(2,1)S(1)}, bf16[7,160,384]{2,1,0:T(8,128)(2,1)S(1)}, u32[]{:S(2)}, u32[]{:S(2)}) collective-permute-start(bf16[7,160,384]{2,1,0:T(8,128)(2,1)S(1)} %codes.5), channel_id=1, source_target_pairs={{0,8},{1,9},{2,10},{3,11},{4,12},{5,13},{6,14},{7,15},{8,0},{9,1},... | collective-permute-start | bytes 2580488 | tf_op jit(solution)/shard_map/ppermute | solution.py:196
  44.6 4.9 %collective-permute-start.12 = (bf16[1,160,384]{2,1,0:T(8,128)(2,1)S(1)}, bf16[1,160,384]{2,1,0:T(8,128)(2,1)S(1)}, u32[]{:S(2)}, u32[]{:S(2)}) collective-permute-start(bf16[1,160,384]{2,1,0:T(8,128)(2,1)S(1)} %add.6.refs_0_), channel_id=1, source_target_pairs={{0,2},{1,3},{2,0},{3,1},{4,6},{5,7},{6,4},{7,5},{8,9},{9,8},{10,11... | collective-permute-start | bytes 368648 | tf_op jit(solution)/shard_map/ppermute | solution.py:196
  46.0 6.7 %collective-permute-start.11 = (bf16[2,160,384]{2,1,0:T(8,128)(2,1)S(1)}, bf16[2,160,384]{2,1,0:T(8,128)(2,1)S(1)}, u32[]{:S(2)}, u32[]{:S(2)}) collective-permute-start(bf16[2,160,384]{2,1,0:T(8,128)(2,1)S(1)} %add.8), channel_id=1, source_target_pairs={{0,2},{1,3},{2,0},{3,1},{4,6},{5,7},{6,4},{7,5},{8,9},{9,8},{10,11... | collective-permute-start | bytes 737288 | tf_op jit(solution)/shard_map/ppermute | solution.py:196
  49.6 5.1 %collective-permute-start.14 = (bf16[1,160,384]{2,1,0:T(8,128)(2,1)S(1)}, bf16[1,160,384]{2,1,0:T(8,128)(2,1)S(1)}, u32[]{:S(2)}, u32[]{:S(2)}) collective-permute-start(bf16[1,160,384]{2,1,0:T(8,128)(2,1)S(1)} %add.9.refs_0_.after_ref), channel_id=1, source_target_pairs={{0,1},{1,0},{2,3},{3,2},{4,5},{5,4},{6,7},{7,6},{8,10},{9,11},{10,... | collective-permute-start | bytes 368648 | tf_op jit(solution)/shard_map/ppermute | solution.py:196
  50.6 8.8 %collective-permute-start.10 = (bf16[1,160,384]{2,1,0:T(8,128)(2,1)S(1)}, bf16[1,160,384]{2,1,0:T(8,128)(2,1)S(1)}, u32[]{:S(2)}, u32[]{:S(2)}) collective-permute-start(bf16[1,160,384]{2,1,0:T(8,128)(2,1)S(1)} %add.7), channel_id=1, source_target_pairs={{0,2},{1,3},{2,0},{3,1},{4,6},{5,7},{6,4},{7,5},{8,9},{9,8},{10,11... | collective-permute-start | bytes 368648 | tf_op jit(solution)/shard_map/ppermute | solution.py:196
  54.9 7.8 %collective-permute-start.15 = (bf16[1,160,384]{2,1,0:T(8,128)(2,1)S(1)}, bf16[1,160,384]{2,1,0:T(8,128)(2,1)S(1)}, u32[]{:S(2)}, u32[]{:S(2)}) collective-permute-start(bf16[1,160,384]{2,1,0:T(8,128)(2,1)S(1)} %add.10.after_ref), channel_id=1, source_target_pairs={{0,4},{1,5},{2,6},{3,7},{4,0},{5,1},{6,2},{7,3},{8,12},{9,13},{10,... | collective-permute-start | bytes 368648 | tf_op jit(solution)/shard_map/ppermute | solution.py:196
  55.9 6.7 %collective-permute-start.13 = (bf16[1,160,384]{2,1,0:T(8,128)(2,1)S(1)}, bf16[1,160,384]{2,1,0:T(8,128)(2,1)S(1)}, u32[]{:S(2)}, u32[]{:S(2)}) collective-permute-start(bf16[1,160,384]{2,1,0:T(8,128)(2,1)S(1)} %add_far2.1), channel_id=1, source_target_pairs={{0,1},{1,0},{2,3},{3,2},{4,5},{5,4},{6,7},{7,6},{8,10},{9,11},{10,... | collective-permute-start | bytes 368648 | tf_op jit(solution)/shard_map/ppermute | solution.py:196
  62.7 4.9 %collective-permute-start.16 = (bf16[1,160,384]{2,1,0:T(8,128)(2,1)S(1)}, bf16[1,160,384]{2,1,0:T(8,128)(2,1)S(1)}, u32[]{:S(2)}, u32[]{:S(2)}) collective-permute-start(bf16[1,160,384]{2,1,0:T(8,128)(2,1)S(1)} %add.11.after_ref.mine_ref), channel_id=1, source_target_pairs={{0,16},{1,17},{2,18},{3,19},{4,20},{5,21},{6,22},{7,23},{8,24},{9,... | collective-permute-start | bytes 368648 | tf_op jit(solution)/shard_map/ppermute | solution.py:196
  67.8 6.8 %collective-permute-start.17 = (bf16[1,160,384]{2,1,0:T(8,128)(2,1)S(1)}, bf16[1,160,384]{2,1,0:T(8,128)(2,1)S(1)}, u32[]{:S(2)}, u32[]{:S(2)}) collective-permute-start(bf16[1,160,384]{2,1,0:T(8,128)(2,1)S(1)} %get-tuple-element.94.after_ref.own_ref), channel_id=1, source_target_pairs={{0,4},{1,5},{2,6},{3,7},{4,0},{5,1},{6,2},{7,3},{8,12},{9,13},{10,... | collective-permute-start | bytes 368648 | tf_op jit(solution)/shard_map/ppermute | solution.py:196
  68.1 6.5 %collective-permute-start.18 = (bf16[1,160,384]{2,1,0:T(8,128)(2,1)S(1)}, bf16[1,160,384]{2,1,0:T(8,128)(2,1)S(1)}, u32[]{:S(2)}, u32[]{:S(2)}) collective-permute-start(bf16[1,160,384]{2,1,0:T(8,128)(2,1)S(1)} %get-tuple-element.94.after_ref.own_ref), channel_id=1, source_target_pairs={{0,1},{1,0},{2,3},{3,2},{4,5},{5,4},{6,7},{7,6},{8,10},{9,11},{10,... | collective-permute-start | bytes 368648 | tf_op jit(solution)/shard_map/ppermute | solution.py:196
  74.6 4.9 %collective-permute-start.19 = (bf16[1,160,384]{2,1,0:T(8,128)(2,1)S(1)}, bf16[1,160,384]{2,1,0:T(8,128)(2,1)S(1)}, u32[]{:S(2)}, u32[]{:S(2)}) collective-permute-start(bf16[1,160,384]{2,1,0:T(8,128)(2,1)S(1)} %get-tuple-element.97), channel_id=1, source_target_pairs={{0,1},{1,0},{2,3},{3,2},{4,5},{5,4},{6,7},{7,6},{8,10},{9,11},{10,... | collective-permute-start | bytes 368648 | tf_op jit(solution)/shard_map/ppermute | solution.py:196
  75.1 8.0 %collective-permute-start.20 = (bf16[3,160,384]{2,1,0:T(8,128)(2,1)S(1)}, bf16[3,160,384]{2,1,0:T(8,128)(2,1)S(1)}, u32[]{:S(2)}, u32[]{:S(2)}) collective-permute-start(bf16[3,160,384]{2,1,0:T(8,128)(2,1)S(1)} %get-tuple-element.96.trio_ref), channel_id=1, source_target_pairs={{0,2},{1,3},{2,0},{3,1},{4,6},{5,7},{6,4},{7,5},{8,9},{9,8},{10,11... | collective-permute-start | bytes 1105928 | tf_op jit(solution)/shard_map/ppermute | solution.py:196
  79.6 2.1 %collective-permute-start.22 = (f32[1,160,384]{2,1,0:T(8,128)S(1)}, f32[1,160,384]{2,1,0:T(8,128)S(1)}, u32[]{:S(2)}, u32[]{:S(2)}) collective-permute-start(f32[1,160,384]{2,1,0:T(8,128)S(1)} %get-tuple-element.102.mine_ref), channel_id=1, source_target_pairs={{0,8},{1,9},{2,10},{3,11},{4,12},{5,13},{6,14},{7,15},{8,0},{9,1},... | collective-permute-start | bytes 737288 | tf_op jit(solution)/shard_map/ppermute | solution.py:196
  79.7 4.9 %collective-permute-start.21 = (bf16[1,160,384]{2,1,0:T(8,128)(2,1)S(1)}, bf16[1,160,384]{2,1,0:T(8,128)(2,1)S(1)}, u32[]{:S(2)}, u32[]{:S(2)}) collective-permute-start(bf16[1,160,384]{2,1,0:T(8,128)(2,1)S(1)} %collective-permute-done.19.one_ref), channel_id=1, source_target_pairs={{0,2},{1,3},{2,0},{3,1},{4,6},{5,7},{6,4},{7,5},{8,9},{9,8},{10,11... | collective-permute-start | bytes 368648 | tf_op jit(solution)/shard_map/ppermute | solution.py:196
  81.6 3.1 %collective-permute-start.23 = (bf16[4,160,384]{2,1,0:T(8,128)(2,1)S(1)}, bf16[4,160,384]{2,1,0:T(8,128)(2,1)S(1)}, u32[]{:S(2)}, u32[]{:S(2)}) collective-permute-start(bf16[4,160,384]{2,1,0:T(8,128)(2,1)S(1)} %get-tuple-element.99.four_ref.refs_0_), channel_id=1, source_target_pairs={{0,8},{1,9},{2,10},{3,11},{4,12},{5,13},{6,14},{7,15},{8,0},{9,1},... | collective-permute-start | bytes 1474568 | tf_op jit(solution)/shard_map/ppermute | solution.py:196
  83.2 1.9 %collective-permute-start.24 = (bf16[3,160,384]{2,1,0:T(8,128)(2,1)S(1)}, bf16[3,160,384]{2,1,0:T(8,128)(2,1)S(1)}, u32[]{:S(2)}, u32[]{:S(2)}) collective-permute-start(bf16[3,160,384]{2,1,0:T(8,128)(2,1)S(1)} %passed.3.trio_ref), channel_id=1, source_target_pairs={{0,8},{1,9},{2,10},{3,11},{4,12},{5,13},{6,14},{7,15},{8,0},{9,1},... | collective-permute-start | bytes 1105928 | tf_op jit(solution)/shard_map/ppermute | solution.py:196
  84.7 1.5 %copy-start = (f32[288,384]{1,0:T(8,128)S(1)}, f32[288,384]{1,0:T(8,128)}, u32[]{:S(2)}) copy-start(f32[288,384]{1,0:T(8,128)} %refs_2_.3) | copy-start | bytes 1327108
  84.7 1.5 %copy-start.1 = (f32[48,192]{1,0:T(8,128)S(1)}, f32[48,192]{1,0:T(8,128)}, u32[]{:S(2)}) copy-start(f32[48,192]{1,0:T(8,128)} %refs_3_.3) | copy-start | bytes 110596
  84.7 1.5 %copy-start.2 = (f32[24,10]{0,1:T(8,128)S(1)}, f32[24,10]{0,1:T(8,128)}, u32[]{:S(2)}) copy-start(f32[24,10]{0,1:T(8,128)} %param.23) | copy-start | bytes 2884
  84.7 1.5 %collective-permute-start.25 = (bf16[1,160,384]{2,1,0:T(8,128)(2,1)S(1)}, bf16[1,160,384]{2,1,0:T(8,128)(2,1)S(1)}, u32[]{:S(2)}, u32[]{:S(2)}) collective-permute-start(bf16[1,160,384]{2,1,0:T(8,128)(2,1)S(1)} %passed_last.3.one_ref), channel_id=1, source_target_pairs={{0,8},{1,9},{2,10},{3,11},{4,12},{5,13},{6,14},{7,15},{8,0},{9,1},... | collective-permute-start | bytes 368648 | tf_op jit(solution)/shard_map/ppermute | solution.py:196

commit v4 on v3

--- a/solution.py
+++ b/solution.py
@@ -182,10 +182,17 @@
 ORDERS = ((2, 1, 4), (1, 2, 4))
 
 
+def half_of(grp, wide):
+    return (grp + wide + (wide >> 1)) & 1
+
+
 def wide_perm(phase):
-    return [
-        (g * 8 + w, g * 8 + (w ^ ORDERS[g % 2][phase])) for g in range(4) for w in range(8)
-    ]
+    pairs = []
+    for g in range(4):
+        for w in range(8):
+            bit = ORDERS[half_of(g, w)][phase]
+            pairs.append((g * 8 + w, (g ^ (bit < 4)) * 8 + (w ^ bit)))
+    return pairs
 
 
 def grp_perm(bit):
@@ -196,12 +203,12 @@
     return lax.ppermute(array, BOTH, perm)
 
 
-def own_core():
-    return lax.rem(lax.axis_index("grp"), 2)
+def own_half():
+    return half_of(lax.axis_index("grp"), lax.axis_index("wide"))
 
 
 def half_at(place, same_core):
-    core = own_core() if same_core else 1 - own_core()
+    core = own_half() if same_core else 1 - own_half()
     masks = [
         sum(order[phase] for phase in range(3) if place & (4 >> phase)) for order in ORDERS
     ]
@@ -264,7 +271,7 @@
     return jax.ShapeDtypeStruct(shape, dtype)
 
 
-MICROS = {"passed_last": 20.0}
+MICROS = {"passed": 5.0, "passed_last": 20.0, "passed_one": 20.0, "add_far3": 20.0}
 
 
 def placed(shape, spec):
@@ -307,7 +314,7 @@
 
 
 def pack_kernel(w6_ref, w7_ref, w8_ref, out_ref, half6, half7, all8, sems):
-    core = own_core()
+    core = own_half()
     rows6, rows7 = half6.shape[0], half7.shape[0]
     copies = [
         pltpu.make_async_copy(
@@ -440,12 +447,15 @@
     )(own, far, mid, *[array for _, array in after])
     trio4 = swap(trio, wide_perm(0))
     one3 = swap(far, wide_perm(1))
+    one3 = passed(one3, (), "passed_one")
     one7 = swap(one3, wide_perm(0))
-    four, done = (relay(trio, one3)[0], None) if work is None else work(trio, one3)
+    four, begun = (relay(trio, one3)[0], None) if work is None else work(trio, one3)
     trio4 = passed(trio4, (four,))
-    one7 = passed(one7, done[:3] if done else (four,), "passed_last")
-    mine = (four, trio4, one7)
-    return (*mine, *[swap(part, grp_perm(1)) for part in mine]), done
+    other_four = swap(four, grp_perm(1))
+    done = (four,) if work is None else begun(trio4, other_four)
+    one7 = passed(one7, done[:3], "passed_last")
+    others = (other_four, swap(trio4, grp_perm(1)), swap(one7, grp_perm(1)))
+    return (four, trio4, one7, *others), done
 
 
 def gelu_pair(pre):
@@ -656,7 +666,7 @@
 
 
 def hold_kernel(after_ref, m6_ref, m7_ref, m8_ref, out_ref, half7, all8, sems):
-    core = own_core()
+    core = own_half()
     rows7, h2 = half7.shape
     rows6 = out_ref.shape[1] - rows7 * 2 // 3
     copies = [
@@ -717,11 +727,15 @@
     low_ref[0, rows6:] = region.astype(BF16)
 
 
-def schulz_chains(grams, iterates):
+def schulz_chains(grams, iterates, inverses):
     diagonals = [shifted_eye(gram.shape[0], gram.shape[0], 0, F32) for gram in grams]
     for number in range(NS_STEPS):
         lefts = [left_parts(gram) for gram in grams]
         squares = [mxu(left, right_parts(gram)) for left, gram in zip(lefts, grams)]
+        if number == 0:
+            scales = [inverse * inverse for inverse in inverses]
+            squares = [square * (scale * scale) for square, scale in zip(squares, scales)]
+            grams = [gram * scale for gram, scale in zip(grams, scales)]
         mixed = [
             right_parts(coef_a * diagonal + coef_b * gram + coef_c * square)
             for diagonal, gram, square in zip(diagonals, grams, squares)
@@ -734,10 +748,11 @@
             for left, row, right in zip(lefts, rows, mixed)
         ]
         iterates = [value[gram.shape[0] :] for value, gram in zip(both, grams)]
-        grams = [
-            mxu(left_parts(value[: gram.shape[0]]), right)
-            for value, gram, right in zip(both, grams, mixed)
-        ]
+        products = [value[: gram.shape[0]] for value, gram in zip(both, grams)]
+        if number == 0:
+            iterates = [iterate * inverse for iterate, inverse in zip(iterates, inverses)]
+            products = [product * scale for product, scale in zip(products, scales)]
+        grams = [mxu(left_parts(product), right) for product, right in zip(products, mixed)]
 
 
 def grams_of(sizes, ref):
@@ -753,21 +768,26 @@
     out6_ref[...], out78_ref[...] = grams_of(sizes, four_ref)
 
 
-def late_kernel(sizes, own6_ref, own78_ref, trio_ref, one_ref, theirs_ref, trio2_ref, *outs):
+def middle_kernel(sizes, own6_ref, own78_ref, trio_ref, theirs_ref, *outs):
     trio6, trio78 = grams_of(sizes, trio_ref)
+    outs[0][...] = own6_ref[...] + trio6
+    outs[1][...] = own78_ref[...] + trio78
+    outs[2][...], outs[3][...] = grams_of(sizes, theirs_ref)
+
+
+def late_kernel(sizes, own6_ref, own78_ref, other6_ref, other78_ref, one_ref, trio_ref, *outs):
     one6, one78 = grams_of(sizes, one_ref)
-    outs[0][...] = own6_ref[...] + trio6 + one6
-    outs[1][...] = own78_ref[...] + trio78 + one78
-    four6, four78 = grams_of(sizes, theirs_ref)
-    trio6, trio78 = grams_of(sizes, trio2_ref)
-    outs[2][...] = four6 + trio6
-    outs[3][...] = four78 + trio78
+    outs[0][...] = own6_ref[...] + one6
+    outs[1][...] = own78_ref[...] + one78
+    trio6, trio78 = grams_of(sizes, trio_ref)
+    outs[2][...] = other6_ref[...] + trio6
+    outs[3][...] = other78_ref[...] + trio78
 
 
 def momenta_kernel(sizes, mine_ref, theirs_ref, *refs):
     ins, h1, h2, classes, rows6, rows7, rows8 = sizes
     out6_ref, out7_ref, out8_ref, near6_ref, near78_ref, stage7, sems = refs
-    core = own_core()
+    core = own_half()
     copies = []
     region8 = None
     for k, (at, ref) in enumerate(((core, mine_ref), (1 - core, theirs_ref))):
@@ -815,10 +835,9 @@
     inverse7 = 1.0 / (jnp.sqrt(trace7) + 1e-07)
     inverse8 = 1.0 / (jnp.sqrt(trace8) + 1e-07)
     inverse = jnp.where(is7_col[:1], inverse7, inverse8)
-    gram7 = jnp.where(is7_row == is7_col, gram7 * (inverse * inverse), 0.0)
+    gram7 = jnp.where(is7_row == is7_col, gram7, 0.0)
     iterate6, iterate7 = schulz_chains(
-        [gram6 * (inverse6 * inverse6), gram7],
-        [near6_ref[...] * inverse6, near78_ref[...] * inverse],
+        [gram6, gram7], [near6_ref[...], near78_ref[...]], [inverse6, inverse]
     )
     for iterate, w_ref, new_ref, low_ref in (
         (iterate6, w6_ref, new6_ref, low6_ref),
@@ -936,7 +955,7 @@
     kept = codes(rest, True, (out7,))
     near56 = swap(add((5, 5), (kept, got), 2), wide_perm(0))
     near4 = swap(add((4, 4), (kept, got), 1), wide_perm(0))
-    far3 = add((3, 3, 0), (kept, got, near7), 1)
+    far3 = add((3, 3, 0), (kept, got, near7), 1, name="add_far3")
     near56 = passed(near56, (far3,), "passed_near")
     totals = call(
         totals_kernel,
@@ -950,10 +969,18 @@
     far3 = swap(far3, wide_perm(1))
     far2 = add((2, 2, 1), (kept, got, near56), 1, name="add_far2")
     far2 = swap(far2, wide_perm(1))
-    last = add((1, 1, 0, 0), (kept, got, near56, far3), 1, [(HBM, row) for row in flat])
+    last = add(
+        (1, 1, 0, 0),
+        (kept, got, near56, far3),
+        1,
+        [(HBM, row) for row in flat],
+        name="add_last",
+    )
     new_resid6 = new_resid6_part(0, ins // 2, last, head, acc6, noise6)
     last = swap(last, wide_perm(2))
-    mine = add((0,) * 5, (kept, got, near4, far2, last), 1, [(HBM, new_resid6)])
+    mine = add(
+        (0,) * 5, (kept, got, near4, far2, last), 1, [(HBM, new_resid6)], name="add_mine"
+    )
     held = hold_moments(mine, moment6, moment7, moment8)
     theirs = swap(mine, grp_perm(2))
 
@@ -1000,12 +1027,24 @@
             ],
             [pltpu.VMEM(moment7.shape, F32), pltpu.SemaphoreType.DMA((3,))],
         )(again, swap(again, grp_perm(1)))
-        return four, [momenta[3], *early, *momenta]
+
+        def begun(trio4, other_four):
+            middle = call(
+                functools.partial(middle_kernel, sizes),
+                "middle_grams",
+                [VMEM] * 4,
+                [VMEM] * 4,
+                grams * 2,
+                megabytes=8,
+            )(*early, trio4, other_four)
+            return [momenta[3], middle[0], middle[2], *middle, *momenta]
+
+        return four, begun
 
     moments, done = gather_halves(
         moment_low, [(HBM, new_resid6), (HBM, new_resid8)], beside_last
     )
-    early, (mom6, mom7, mom8, near6, near78) = done[1:3], done[3:]
+    middle, (mom6, mom7, mom8, near6, near78) = done[3:7], done[7:]
     late = call(
         functools.partial(late_kernel, sizes),
         "late_grams",
@@ -1013,7 +1052,7 @@
         [VMEM] * 4,
         grams * 2,
         megabytes=8,
-    )(*early, *moments[1:5])
+    )(*middle, moments[2], moments[4])
 
     updated = call(
         functools.partial(update_kernel, sizes),

time: 98.3 us -> 97.7 us (level)
  starting transfers between devices: 20.2 us -> 18.6 us
    ppermute x26, starting transfers between devices: 20.2 us -> 18.6 us  [swap(): return lax.ppermute(array, BOTH, perm)]
    pallas_call x33 -> x36, Pallas kernels: 34.3 us -> 34.2 us  [run(): kernel_call(*[pltpu.with_memory_space_constraint(array, pltpu.HBM) if spe...]
  transfers between devices with their start and end apart: 26 -> 26, of which waited for: 15 -> 17; matrix products, arithmetic and copies ran while one was open for 0% -> 0% of each run, Pallas kernels for 17% -> 17%
where the time goes in v4:
time: 97.7 us; the launch traced here: 97.5 us
  Pallas kernels  34.2 us (35%)
  waiting for transfers between devices  30.1 us (31%)
  starting transfers between devices  18.6 us (19%)
  blocking collectives  13 us (13%)
  between operations  1.6 us (2%)
    pallas_call x36, Pallas kernels, run(): kernel_call(*[pltpu.with_memory_space_constraint(array, pltpu.HBM) if spe...  34.2 us
    ppermute x26, waiting for transfers between devices, swap(): return lax.ppermute(array, BOTH, perm)  30.1 us
    ppermute x26, starting transfers between devices, swap(): return lax.ppermute(array, BOTH, perm)  18.6 us
    all_to_all x1, blocking collectives, paired_plan(): all_stats = lax.all_to_all(stats, BOTH, 0, 0, tiled=True)  13 us
  transfers between devices with their start and end apart: 26, of which 17 were waited for; matrix products, arithmetic and copies ran while one was open for 0% of the time, Pallas kernels for 17%

profile of v4, /device:TPU:0, one launch (start us, length us, event | category | flops | bytes accessed | tf_op | source)
XLA Modules:
  0.0 97.5 jit_solution(7558021174735911945)
XLA Ops:
  0.7 1.2 %pack_weights.1.after_ref.own_ref = bf16[1,160,384]{2,1,0:T(8,128)(2,1)S(1)} custom-call(f32[288,384]{1,0:T(8,128)} %refs_2_.3, f32[48,192]{1,0:T(8,128)} %refs_3_.3, f32[10,24]{1,0:T(8,128)} %bitcast.13), custom_call_target="tpu_custom_call" | custom-call | tf_op jit(solution)/shard_map/pack_weights/pallas_call | solution.py:306
  1.8 4.1 %collective-permute-start = (bf16[1,160,384]{2,1,0:T(8,128)(2,1)S(1)}, bf16[1,160,384]{2,1,0:T(8,128)(2,1)S(1)}, u32[]{:S(2)}, u32[]{:S(2)}) collective-permute-start(bf16[1,160,384]{2,1,0:T(8,128)(2,1)S(1)} %pack_weights.1.after_ref.own_ref), channel_id=1, source_target_pairs={{0,4},{1,5},{2,6},{3,7},{4,0},{5,1},{6,2},{7,3},{8,12},{9,13},{10,... | collective-permute-start | bytes 368648 | tf_op jit(solution)/shard_map/ppermute | solution.py:203
  5.9 0.7 collective-permute-start.1
  7.2 3.6 %stage.1 = (bf16[192,2304]{1,0:T(8,128)(2,1)S(1)}, s32[1,192]{1,0:T(1,128)S(1)}, f32[1,586]{1,0:T(1,128)S(1)}, f32[1,586]{1,0:T(1,128)S(1)}, f32[1,586]{1,0:T(1,...) custom-call(bf16[1,160,384]{2,1,0:T(8,128)(2,1)S(1)} %pack_weights.1, ...), custom_call_target="tpu_custom_call" | custom-call | tf_op jit(solution)/shard_map/stage/pallas_call | solution.py:306
  10.9 1.0 %collective-permute-done.far_ref = bf16[1,160,384]{2,1,0:T(8,128)(2,1)S(1)} collective-permute-done((bf16[1,160,384]{2,1,0:T(8,128)(2,1)S(1)}, bf16[1,160,384]{2,1,0:T(8,128)(2,1)S(1)}, u32[]{:S(2)}, u32[]{:S(2)}) %collective-permute-start) | collective-permute-done | bytes 122912 | tf_op jit(solution)/shard_map/ppermute | solution.py:203
  12.1 1.8 %collective-permute-start.3 = (bf16[3,160,384]{2,1,0:T(8,128)(2,1)S(1)}, bf16[3,160,384]{2,1,0:T(8,128)(2,1)S(1)}, u32[]{:S(2)}, u32[]{:S(2)}) collective-permute-start(bf16[3,160,384]{2,1,0:T(8,128)(2,1)S(1)} %get-tuple-element.74.trio_ref), channel_id=1, source_target_pairs={{0,10},{1,8},{2,11},{3,9},{4,14},{5,12},{6,15},{7,13},{8,1},{9,3},... | collective-permute-start | bytes 1105928 | tf_op jit(solution)/shard_map/ppermute | solution.py:203
  13.9 2.7 %collective-permute-done.2.in_ref = bf16[1,160,384]{2,1,0:T(8,128)(2,1)S(1)} collective-permute-done((bf16[1,160,384]{2,1,0:T(8,128)(2,1)S(1)}, bf16[1,160,384]{2,1,0:T(8,128)(2,1)S(1)}, u32[]{:S(2)}, u32[]{:S(2)}) %collective-permute-start.2) | collective-permute-done | bytes 122912 | tf_op jit(solution)/shard_map/ppermute | solution.py:203
  16.7 2.5 %collective-permute-start.4 = (bf16[1,160,384]{2,1,0:T(8,128)(2,1)S(1)}, bf16[1,160,384]{2,1,0:T(8,128)(2,1)S(1)}, u32[]{:S(2)}, u32[]{:S(2)}) collective-permute-start(bf16[1,160,384]{2,1,0:T(8,128)(2,1)S(1)} %passed_one.2.one_ref), channel_id=1, source_target_pairs={{0,10},{1,8},{2,11},{3,9},{4,14},{5,12},{6,15},{7,13},{8,1},{9,3},... | collective-permute-start | bytes 368648 | tf_op jit(solution)/shard_map/ppermute | solution.py:203
  19.2 1.2 %collective-permute-done.3.in_ref = bf16[3,160,384]{2,1,0:T(8,128)(2,1)S(1)} collective-permute-done((bf16[3,160,384]{2,1,0:T(8,128)(2,1)S(1)}, bf16[3,160,384]{2,1,0:T(8,128)(2,1)S(1)}, u32[]{:S(2)}, u32[]{:S(2)}) %collective-permute-start.3) | collective-permute-done | bytes 368672 | tf_op jit(solution)/shard_map/ppermute | solution.py:203
  20.6 1.2 %collective-permute-done.4.in_ref = bf16[1,160,384]{2,1,0:T(8,128)(2,1)S(1)} collective-permute-done((bf16[1,160,384]{2,1,0:T(8,128)(2,1)S(1)}, bf16[1,160,384]{2,1,0:T(8,128)(2,1)S(1)}, u32[]{:S(2)}, u32[]{:S(2)}) %collective-permute-start.4) | collective-permute-done | bytes 122912 | tf_op jit(solution)/shard_map/ppermute | solution.py:203
  21.8 0.7 collective-permute-start.7
  22.5 1.0 %collective-permute-done.7.refs_5_ = bf16[1,160,384]{2,1,0:T(8,128)(2,1)S(1)} collective-permute-done((bf16[1,160,384]{2,1,0:T(8,128)(2,1)S(1)}, bf16[1,160,384]{2,1,0:T(8,128)(2,1)S(1)}, u32[]{:S(2)}, u32[]{:S(2)}) %collective-permute-start.7) | collective-permute-done | bytes 122912 | tf_op jit(solution)/shard_map/ppermute | solution.py:203
  23.5 2.9 %worker.1 = (f32[2304,384]{1,0:T(8,128)S(1)}, f32[192,384]{1,0:T(8,128)S(1)}, f32[10,192]{1,0:T(8,128)S(1)}, f32[32,1,640]{2,1,0:T(1,128)S(1)}) custom-call(bf16[4,160,384]{2,1,0:T(8,128)(2,1)S(1)} %relay.2.refs_0_, bf16[3,160,384]{2,1,0:T(8,128)(2,1)S(1)} %passed.2.refs_1_, bf16[1,160,384]{2,1,0:T(8,128)(2,1)S(1)} %passed_last.2.refs_2_, ...), custom_call_target="tpu_custom_call" | custom-call | tf_op jit(solution)/shard_map/worker/pallas_call | solution.py:306
  26.4 13.0 %all_to_all.5.stats_ref = f32[32,1,640]{2,1,0:T(1,128)S(1)} all-to-all(f32[32,1,640]{2,1,0:T(1,128)S(1)} %get-tuple-element.82.mine_ref), channel_id=1, replica_groups=mesh['grp'=4,'wide'=8] {'grp','wide'}, dimensions={0} | all-to-all | bytes 163840 | tf_op jit(solution)/shard_map/all_to_all | solution.py:923
  39.4 0.6 codes_first.1
  40.4 1.1 %collective-permute-done.8.refs_1_ = bf16[1,160,384]{2,1,0:T(8,128)(2,1)S(1)} collective-permute-done((bf16[1,160,384]{2,1,0:T(8,128)(2,1)S(1)}, bf16[1,160,384]{2,1,0:T(8,128)(2,1)S(1)}, u32[]{:S(2)}, u32[]{:S(2)}) %collective-permute-start.8) | collective-permute-done | bytes 122912 | tf_op jit(solution)/shard_map/ppermute | solution.py:203
  41.5 0.9 codes.5
  42.6 0.5 collective-permute-start.12
  43.1 0.9 codes.4.refs_0_
  44.0 0.8 collective-permute-done.9.refs_1_
  44.9 0.5 collective-permute-start.11
  45.4 1.5 %collective-permute-done.12.refs_2_ = bf16[1,160,384]{2,1,0:T(8,128)(2,1)S(1)} collective-permute-done((bf16[1,160,384]{2,1,0:T(8,128)(2,1)S(1)}, bf16[1,160,384]{2,1,0:T(8,128)(2,1)S(1)}, u32[]{:S(2)}, u32[]{:S(2)}) %collective-permute-start.12) | collective-permute-done | bytes 122912 | tf_op jit(solution)/shard_map/ppermute | solution.py:203
  47.0 0.9 collective-permute-start.14
  47.9 0.4 collective-permute-start.10
  48.3 1.3 %totals.1 = (f32[586]{0:T(1024)}, f32[586]{0:T(1024)}, f32[586]{0:T(1024)}, f32[1,1]{1,0:T(1,128)}, f32[1,1]{1,0:T(1,128)}) custom-call(bf16[1,160,384]{2,1,0:T(8,128)(2,1)S(1)} %add_far3.1.refs_0_.after_ref, f32[32,1,640]{2,1,0:T(1,128)S(1)} %all_to_all.5.stats_ref, f32[1,586]{1,0:T(1,128)S(1)} %get-tuple-element.78.refs_9_.bias_ref, ...), custom_call_target="tpu_custom_call" | custom-call | tf_op jit(solution)/shard_map/totals/pallas_call | solution.py:306
  49.6 1.0 %collective-permute-done.11.in_ref = bf16[2,160,384]{2,1,0:T(8,128)(2,1)S(1)} collective-permute-done((bf16[2,160,384]{2,1,0:T(8,128)(2,1)S(1)}, bf16[2,160,384]{2,1,0:T(8,128)(2,1)S(1)}, u32[]{:S(2)}, u32[]{:S(2)}) %collective-permute-start.11) | collective-permute-done | bytes 245792 | tf_op jit(solution)/shard_map/ppermute | solution.py:203
  50.6 2.1 %collective-permute-done.14.refs_3_ = bf16[1,160,384]{2,1,0:T(8,128)(2,1)S(1)} collective-permute-done((bf16[1,160,384]{2,1,0:T(8,128)(2,1)S(1)}, bf16[1,160,384]{2,1,0:T(8,128)(2,1)S(1)}, u32[]{:S(2)}, u32[]{:S(2)}) %collective-permute-start.14) | collective-permute-done | bytes 122912 | tf_op jit(solution)/shard_map/ppermute | solution.py:203
  52.8 1.0 %collective-permute-start.15 = (bf16[1,160,384]{2,1,0:T(8,128)(2,1)S(1)}, bf16[1,160,384]{2,1,0:T(8,128)(2,1)S(1)}, u32[]{:S(2)}, u32[]{:S(2)}) collective-permute-start(bf16[1,160,384]{2,1,0:T(8,128)(2,1)S(1)} %add_last.1.after_ref), channel_id=1, source_target_pairs={{0,4},{1,5},{2,6},{3,7},{4,0},{5,1},{6,2},{7,3},{8,12},{9,13},{10,... | collective-permute-start | bytes 368648 | tf_op jit(solution)/shard_map/ppermute | solution.py:203
  53.8 0.4 collective-permute-start.13
  54.2 2.4 %new_resid.2.refs_5_.refs_0_ = f32[2304,384]{1,0:T(8,128)} custom-call(bf16[1,160,384]{2,1,0:T(8,128)(2,1)S(1)} %add_last.1.after_ref, f32[1,128]{1,0:T(1,128)S(1)} %get-tuple-element.89.head_ref, f32[2304,384]{1,0:T(8,128)S(1)} %get-tuple-element.83.acc6_ref.acc6, s32[2304,384]{1,0:T(8,128)S(1)} %get-tuple-element.84.noise6_ref.noise6), custom_call_target="tpu_custom_call" | custom-call | tf_op jit(solution)/shard_map/new_resid/pallas_call | solution.py:306
  56.6 4.6 %collective-permute-done.15.refs_4_ = bf16[1,160,384]{2,1,0:T(8,128)(2,1)S(1)} collective-permute-done((bf16[1,160,384]{2,1,0:T(8,128)(2,1)S(1)}, bf16[1,160,384]{2,1,0:T(8,128)(2,1)S(1)}, u32[]{:S(2)}, u32[]{:S(2)}) %collective-permute-start.15) | collective-permute-done | bytes 122912 | tf_op jit(solution)/shard_map/ppermute | solution.py:203
  61.4 0.6 collective-permute-start.16
  62.0 1.2 %hold_moments.1.held_ref = f32[1,160,384]{2,1,0:T(8,128)S(1)} custom-call(bf16[1,160,384]{2,1,0:T(8,128)(2,1)S(1)} %add_mine.1.after_ref.mine_ref, f32[288,384]{1,0:T(8,128)} %m6_ref.1, f32[48,192]{1,0:T(8,128)} %m7_ref.1, f32[10,24]{1,0:T(8,128)} %bitcast.20), custom_call_target="tpu_custom_call" | custom-call | tf_op jit(solution)/shard_map/hold_moments/pallas_call | solution.py:306
  63.1 3.5 %collective-permute-done.16.theirs_ref = bf16[1,160,384]{2,1,0:T(8,128)(2,1)S(1)} collective-permute-done((bf16[1,160,384]{2,1,0:T(8,128)(2,1)S(1)}, bf16[1,160,384]{2,1,0:T(8,128)(2,1)S(1)}, u32[]{:S(2)}, u32[]{:S(2)}) %collective-permute-start.16) | collective-permute-done | bytes 122912 | tf_op jit(solution)/shard_map/ppermute | solution.py:203
  66.8 0.4 collective-permute-start.18
  67.3 1.0 small_resids.1
  68.2 2.4 %new_resid.3.refs_0_ = f32[2304,384]{1,0:T(8,128)} custom-call(bf16[1,160,384]{2,1,0:T(8,128)(2,1)S(1)} %get-tuple-element.98.after_ref.own_ref, f32[1,128]{1,0:T(1,128)S(1)} %get-tuple-element.89.head_ref, f32[2304,384]{1,0:T(8,128)S(1)} %get-tuple-element.83.acc6_ref.acc6, ...), custom_call_target="tpu_custom_call", output_to_operand_aliasing={{}: (4, {})} | custom-call | tf_op jit(solution)/shard_map/new_resid/pallas_call | solution.py:306
  70.7 2.7 %collective-permute-done.17.far_ref = bf16[1,160,384]{2,1,0:T(8,128)(2,1)S(1)} collective-permute-done((bf16[1,160,384]{2,1,0:T(8,128)(2,1)S(1)}, bf16[1,160,384]{2,1,0:T(8,128)(2,1)S(1)}, u32[]{:S(2)}, u32[]{:S(2)}) %collective-permute-start.17) | collective-permute-done | bytes 122912 | tf_op jit(solution)/shard_map/ppermute | solution.py:203
  73.5 0.5 collective-permute-start.19
  74.0 4.7 %collective-permute-done.19.in_ref = bf16[1,160,384]{2,1,0:T(8,128)(2,1)S(1)} collective-permute-done((bf16[1,160,384]{2,1,0:T(8,128)(2,1)S(1)}, bf16[1,160,384]{2,1,0:T(8,128)(2,1)S(1)}, u32[]{:S(2)}, u32[]{:S(2)}) %collective-permute-start.19) | collective-permute-done | bytes 122912 | tf_op jit(solution)/shard_map/ppermute | solution.py:203
  78.8 0.5 early_grams.1
  79.3 0.6 collective-permute-start.21
  79.9 0.4 collective-permute-done.23.theirs_ref
  80.3 1.4 %momenta.1 = (f32[288,384]{1,0:T(8,128)}, f32[48,192]{1,0:T(8,128)}, f32[10,24]{1,0:T(8,128)}, f32[288,384]{1,0:T(8,128)S(1)}, f32[72,256]{1,0:T(8,128)S(1)}) custom-call(f32[1,160,384]{2,1,0:T(8,128)S(1)} %get-tuple-element.110.mine_ref, f32[1,160,384]{2,1,0:T(8,128)S(1)} %collective-permute-done.23.theirs_ref), custom_call_target="tpu_custom_call" | custom-call | tf_op jit(solution)/shard_map/momenta/pallas_call | solution.py:306
  81.8 1.9 %collective-permute-start.24 = (bf16[3,160,384]{2,1,0:T(8,128)(2,1)S(1)}, bf16[3,160,384]{2,1,0:T(8,128)(2,1)S(1)}, u32[]{:S(2)}, u32[]{:S(2)}) collective-permute-start(bf16[3,160,384]{2,1,0:T(8,128)(2,1)S(1)} %passed.3.trio_ref), channel_id=1, source_target_pairs={{0,8},{1,9},{2,10},{3,11},{4,12},{5,13},{6,14},{7,15},{8,0},{9,1},... | collective-permute-start | bytes 1105928 | tf_op jit(solution)/shard_map/ppermute | solution.py:203
  83.7 0.8 middle_grams.1
  85.0 0.6 late_grams.1
  85.9 11.6 %update.1 = (f32[288,384]{1,0:T(8,128)}, f32[48,192]{1,0:T(8,128)}, f32[10,24]{1,0:T(8,128)}, bf16[288,384]{1,0:T(8,128)(2,1)}, bf16[48,192]{1,0:T(8,128)(2,1)}, /*index=5*/bf16[10,24]{1,0:T(8,128)(2,1)}) custom-call(f32[384,384]{1,0:T(8,128)S(1)} %get-tuple-element.112.own6, f32[256,256]{1,0:T(8,128)S(1)} %get-tuple-element.113.own78, ...), custom_call_target="tpu_custom_call" | custom-call | tf_op jit(solution)/shard_map/update/pallas_call | solution.py:306
  (47 shorter events, 2.6 us)
Async XLA Ops:
  1.8 10.1 %collective-permute-start = (bf16[1,160,384]{2,1,0:T(8,128)(2,1)S(1)}, bf16[1,160,384]{2,1,0:T(8,128)(2,1)S(1)}, u32[]{:S(2)}, u32[]{:S(2)}) collective-permute-start(bf16[1,160,384]{2,1,0:T(8,128)(2,1)S(1)} %pack_weights.1.after_ref.own_ref), channel_id=1, source_target_pairs={{0,4},{1,5},{2,6},{3,7},{4,0},{5,1},{6,2},{7,3},{8,12},{9,13},{10,... | collective-permute-start | bytes 368648 | tf_op jit(solution)/shard_map/ppermute | solution.py:203
  5.9 6.0 %collective-permute-start.1 = (bf16[1,160,384]{2,1,0:T(8,128)(2,1)S(1)}, bf16[1,160,384]{2,1,0:T(8,128)(2,1)S(1)}, u32[]{:S(2)}, u32[]{:S(2)}) collective-permute-start(bf16[1,160,384]{2,1,0:T(8,128)(2,1)S(1)} %pack_weights.1.after_ref.own_ref), channel_id=1, source_target_pairs={{0,9},{1,11},{2,8},{3,10},{4,13},{5,15},{6,12},{7,14},{8,2},{9,0},... | collective-permute-start | bytes 368648 | tf_op jit(solution)/shard_map/ppermute | solution.py:203
  11.9 4.7 %collective-permute-start.2 = (bf16[1,160,384]{2,1,0:T(8,128)(2,1)S(1)}, bf16[1,160,384]{2,1,0:T(8,128)(2,1)S(1)}, u32[]{:S(2)}, u32[]{:S(2)}) collective-permute-start(bf16[1,160,384]{2,1,0:T(8,128)(2,1)S(1)} %get-tuple-element.75), channel_id=1, source_target_pairs={{0,9},{1,11},{2,8},{3,10},{4,13},{5,15},{6,12},{7,14},{8,2},{9,0},... | collective-permute-start | bytes 368648 | tf_op jit(solution)/shard_map/ppermute | solution.py:203
  12.1 8.3 %collective-permute-start.3 = (bf16[3,160,384]{2,1,0:T(8,128)(2,1)S(1)}, bf16[3,160,384]{2,1,0:T(8,128)(2,1)S(1)}, u32[]{:S(2)}, u32[]{:S(2)}) collective-permute-start(bf16[3,160,384]{2,1,0:T(8,128)(2,1)S(1)} %get-tuple-element.74.trio_ref), channel_id=1, source_target_pairs={{0,10},{1,8},{2,11},{3,9},{4,14},{5,12},{6,15},{7,13},{8,1},{9,3},... | collective-permute-start | bytes 1105928 | tf_op jit(solution)/shard_map/ppermute | solution.py:203
  16.7 5.1 %collective-permute-start.4 = (bf16[1,160,384]{2,1,0:T(8,128)(2,1)S(1)}, bf16[1,160,384]{2,1,0:T(8,128)(2,1)S(1)}, u32[]{:S(2)}, u32[]{:S(2)}) collective-permute-start(bf16[1,160,384]{2,1,0:T(8,128)(2,1)S(1)} %passed_one.2.one_ref), channel_id=1, source_target_pairs={{0,10},{1,8},{2,11},{3,9},{4,14},{5,12},{6,15},{7,13},{8,1},{9,3},... | collective-permute-start | bytes 368648 | tf_op jit(solution)/shard_map/ppermute | solution.py:203
  19.2 4.3 %collective-permute-start.5 = (bf16[4,160,384]{2,1,0:T(8,128)(2,1)S(1)}, bf16[4,160,384]{2,1,0:T(8,128)(2,1)S(1)}, u32[]{:S(2)}, u32[]{:S(2)}) collective-permute-start(bf16[4,160,384]{2,1,0:T(8,128)(2,1)S(1)} %relay.2.refs_0_), channel_id=1, source_target_pairs={{0,8},{1,9},{2,10},{3,11},{4,12},{5,13},{6,14},{7,15},{8,0},{9,1},... | collective-permute-start | bytes 1474568 | tf_op jit(solution)/shard_map/ppermute | solution.py:203
  20.5 3.0 %collective-permute-start.6 = (bf16[3,160,384]{2,1,0:T(8,128)(2,1)S(1)}, bf16[3,160,384]{2,1,0:T(8,128)(2,1)S(1)}, u32[]{:S(2)}, u32[]{:S(2)}) collective-permute-start(bf16[3,160,384]{2,1,0:T(8,128)(2,1)S(1)} %passed.2.refs_1_), channel_id=1, source_target_pairs={{0,8},{1,9},{2,10},{3,11},{4,12},{5,13},{6,14},{7,15},{8,0},{9,1},... | collective-permute-start | bytes 1105928 | tf_op jit(solution)/shard_map/ppermute | solution.py:203
  21.8 1.7 %collective-permute-start.7 = (bf16[1,160,384]{2,1,0:T(8,128)(2,1)S(1)}, bf16[1,160,384]{2,1,0:T(8,128)(2,1)S(1)}, u32[]{:S(2)}, u32[]{:S(2)}) collective-permute-start(bf16[1,160,384]{2,1,0:T(8,128)(2,1)S(1)} %passed_last.2.refs_2_), channel_id=1, source_target_pairs={{0,8},{1,9},{2,10},{3,11},{4,12},{5,13},{6,14},{7,15},{8,0},{9,1},... | collective-permute-start | bytes 368648 | tf_op jit(solution)/shard_map/ppermute | solution.py:203
  40.0 1.4 %collective-permute-start.8 = (bf16[1,160,384]{2,1,0:T(8,128)(2,1)S(1)}, bf16[1,160,384]{2,1,0:T(8,128)(2,1)S(1)}, u32[]{:S(2)}, u32[]{:S(2)}) collective-permute-start(bf16[1,160,384]{2,1,0:T(8,128)(2,1)S(1)} %get-tuple-element.92), channel_id=1, source_target_pairs={{0,8},{1,9},{2,10},{3,11},{4,12},{5,13},{6,14},{7,15},{8,0},{9,1},... | collective-permute-start | bytes 368648 | tf_op jit(solution)/shard_map/ppermute | solution.py:203
  42.4 2.5 %collective-permute-start.9 = (bf16[7,160,384]{2,1,0:T(8,128)(2,1)S(1)}, bf16[7,160,384]{2,1,0:T(8,128)(2,1)S(1)}, u32[]{:S(2)}, u32[]{:S(2)}) collective-permute-start(bf16[7,160,384]{2,1,0:T(8,128)(2,1)S(1)} %codes.5), channel_id=1, source_target_pairs={{0,8},{1,9},{2,10},{3,11},{4,12},{5,13},{6,14},{7,15},{8,0},{9,1},... | collective-permute-start | bytes 2580488 | tf_op jit(solution)/shard_map/ppermute | solution.py:203
  42.6 4.3 %collective-permute-start.12 = (bf16[1,160,384]{2,1,0:T(8,128)(2,1)S(1)}, bf16[1,160,384]{2,1,0:T(8,128)(2,1)S(1)}, u32[]{:S(2)}, u32[]{:S(2)}) collective-permute-start(bf16[1,160,384]{2,1,0:T(8,128)(2,1)S(1)} %add.3.refs_0_), channel_id=1, source_target_pairs={{0,10},{1,8},{2,11},{3,9},{4,14},{5,12},{6,15},{7,13},{8,1},{9,3},... | collective-permute-start | bytes 368648 | tf_op jit(solution)/shard_map/ppermute | solution.py:203
  44.9 5.7 %collective-permute-start.11 = (bf16[2,160,384]{2,1,0:T(8,128)(2,1)S(1)}, bf16[2,160,384]{2,1,0:T(8,128)(2,1)S(1)}, u32[]{:S(2)}, u32[]{:S(2)}) collective-permute-start(bf16[2,160,384]{2,1,0:T(8,128)(2,1)S(1)} %add.5), channel_id=1, source_target_pairs={{0,10},{1,8},{2,11},{3,9},{4,14},{5,12},{6,15},{7,13},{8,1},{9,3},... | collective-permute-start | bytes 737288 | tf_op jit(solution)/shard_map/ppermute | solution.py:203
  47.0 5.8 %collective-permute-start.14 = (bf16[1,160,384]{2,1,0:T(8,128)(2,1)S(1)}, bf16[1,160,384]{2,1,0:T(8,128)(2,1)S(1)}, u32[]{:S(2)}, u32[]{:S(2)}) collective-permute-start(bf16[1,160,384]{2,1,0:T(8,128)(2,1)S(1)} %add_far3.1.refs_0_.after_ref), channel_id=1, source_target_pairs={{0,9},{1,11},{2,8},{3,10},{4,13},{5,15},{6,12},{7,14},{8,2},{9,0},... | collective-permute-start | bytes 368648 | tf_op jit(solution)/shard_map/ppermute | solution.py:203
  47.9 8.8 %collective-permute-start.10 = (bf16[1,160,384]{2,1,0:T(8,128)(2,1)S(1)}, bf16[1,160,384]{2,1,0:T(8,128)(2,1)S(1)}, u32[]{:S(2)}, u32[]{:S(2)}) collective-permute-start(bf16[1,160,384]{2,1,0:T(8,128)(2,1)S(1)} %add.4), channel_id=1, source_target_pairs={{0,10},{1,8},{2,11},{3,9},{4,14},{5,12},{6,15},{7,13},{8,1},{9,3},... | collective-permute-start | bytes 368648 | tf_op jit(solution)/shard_map/ppermute | solution.py:203
  52.8 8.5 %collective-permute-start.15 = (bf16[1,160,384]{2,1,0:T(8,128)(2,1)S(1)}, bf16[1,160,384]{2,1,0:T(8,128)(2,1)S(1)}, u32[]{:S(2)}, u32[]{:S(2)}) collective-permute-start(bf16[1,160,384]{2,1,0:T(8,128)(2,1)S(1)} %add_last.1.after_ref), channel_id=1, source_target_pairs={{0,4},{1,5},{2,6},{3,7},{4,0},{5,1},{6,2},{7,3},{8,12},{9,13},{10,... | collective-permute-start | bytes 368648 | tf_op jit(solution)/shard_map/ppermute | solution.py:203
  53.8 7.4 %collective-permute-start.13 = (bf16[1,160,384]{2,1,0:T(8,128)(2,1)S(1)}, bf16[1,160,384]{2,1,0:T(8,128)(2,1)S(1)}, u32[]{:S(2)}, u32[]{:S(2)}) collective-permute-start(bf16[1,160,384]{2,1,0:T(8,128)(2,1)S(1)} %add_far2.1), channel_id=1, source_target_pairs={{0,9},{1,11},{2,8},{3,10},{4,13},{5,15},{6,12},{7,14},{8,2},{9,0},... | collective-permute-start | bytes 368648 | tf_op jit(solution)/shard_map/ppermute | solution.py:203
  61.4 5.3 %collective-permute-start.16 = (bf16[1,160,384]{2,1,0:T(8,128)(2,1)S(1)}, bf16[1,160,384]{2,1,0:T(8,128)(2,1)S(1)}, u32[]{:S(2)}, u32[]{:S(2)}) collective-permute-start(bf16[1,160,384]{2,1,0:T(8,128)(2,1)S(1)} %add_mine.1.after_ref.mine_ref), channel_id=1, source_target_pairs={{0,16},{1,17},{2,18},{3,19},{4,20},{5,21},{6,22},{7,23},{8,24},{9,... | collective-permute-start | bytes 368648 | tf_op jit(solution)/shard_map/ppermute | solution.py:203
  66.8 6.7 %collective-permute-start.17 = (bf16[1,160,384]{2,1,0:T(8,128)(2,1)S(1)}, bf16[1,160,384]{2,1,0:T(8,128)(2,1)S(1)}, u32[]{:S(2)}, u32[]{:S(2)}) collective-permute-start(bf16[1,160,384]{2,1,0:T(8,128)(2,1)S(1)} %get-tuple-element.98.after_ref.own_ref), channel_id=1, source_target_pairs={{0,4},{1,5},{2,6},{3,7},{4,0},{5,1},{6,2},{7,3},{8,12},{9,13},{10,... | collective-permute-start | bytes 368648 | tf_op jit(solution)/shard_map/ppermute | solution.py:203
  66.8 6.6 %collective-permute-start.18 = (bf16[1,160,384]{2,1,0:T(8,128)(2,1)S(1)}, bf16[1,160,384]{2,1,0:T(8,128)(2,1)S(1)}, u32[]{:S(2)}, u32[]{:S(2)}) collective-permute-start(bf16[1,160,384]{2,1,0:T(8,128)(2,1)S(1)} %get-tuple-element.98.after_ref.own_ref), channel_id=1, source_target_pairs={{0,9},{1,11},{2,8},{3,10},{4,13},{5,15},{6,12},{7,14},{8,2},{9,0},... | collective-permute-start | bytes 368648 | tf_op jit(solution)/shard_map/ppermute | solution.py:203
  73.5 5.2 %collective-permute-start.19 = (bf16[1,160,384]{2,1,0:T(8,128)(2,1)S(1)}, bf16[1,160,384]{2,1,0:T(8,128)(2,1)S(1)}, u32[]{:S(2)}, u32[]{:S(2)}) collective-permute-start(bf16[1,160,384]{2,1,0:T(8,128)(2,1)S(1)} %get-tuple-element.101), channel_id=1, source_target_pairs={{0,9},{1,11},{2,8},{3,10},{4,13},{5,15},{6,12},{7,14},{8,2},{9,0},... | collective-permute-start | bytes 368648 | tf_op jit(solution)/shard_map/ppermute | solution.py:203
  74.0 7.8 %collective-permute-start.20 = (bf16[3,160,384]{2,1,0:T(8,128)(2,1)S(1)}, bf16[3,160,384]{2,1,0:T(8,128)(2,1)S(1)}, u32[]{:S(2)}, u32[]{:S(2)}) collective-permute-start(bf16[3,160,384]{2,1,0:T(8,128)(2,1)S(1)} %get-tuple-element.100.trio_ref), channel_id=1, source_target_pairs={{0,10},{1,8},{2,11},{3,9},{4,14},{5,12},{6,15},{7,13},{8,1},{9,3},... | collective-permute-start | bytes 1105928 | tf_op jit(solution)/shard_map/ppermute | solution.py:203
  78.7 1.6 %collective-permute-start.23 = (f32[1,160,384]{2,1,0:T(8,128)S(1)}, f32[1,160,384]{2,1,0:T(8,128)S(1)}, u32[]{:S(2)}, u32[]{:S(2)}) collective-permute-start(f32[1,160,384]{2,1,0:T(8,128)S(1)} %get-tuple-element.110.mine_ref), channel_id=1, source_target_pairs={{0,8},{1,9},{2,10},{3,11},{4,12},{5,13},{6,14},{7,15},{8,0},{9,1},... | collective-permute-start | bytes 737288 | tf_op jit(solution)/shard_map/ppermute | solution.py:203
  79.3 4.3 %collective-permute-start.21 = (bf16[4,160,384]{2,1,0:T(8,128)(2,1)S(1)}, bf16[4,160,384]{2,1,0:T(8,128)(2,1)S(1)}, u32[]{:S(2)}, u32[]{:S(2)}) collective-permute-start(bf16[4,160,384]{2,1,0:T(8,128)(2,1)S(1)} %get-tuple-element.103.four_ref.refs_0_), channel_id=1, source_target_pairs={{0,8},{1,9},{2,10},{3,11},{4,12},{5,13},{6,14},{7,15},{8,0},{9,1},... | collective-permute-start | bytes 1474568 | tf_op jit(solution)/shard_map/ppermute | solution.py:203
  79.9 4.5 %collective-permute-start.22 = (bf16[1,160,384]{2,1,0:T(8,128)(2,1)S(1)}, bf16[1,160,384]{2,1,0:T(8,128)(2,1)S(1)}, u32[]{:S(2)}, u32[]{:S(2)}) collective-permute-start(bf16[1,160,384]{2,1,0:T(8,128)(2,1)S(1)} %passed_one.3.one_ref), channel_id=1, source_target_pairs={{0,10},{1,8},{2,11},{3,9},{4,14},{5,12},{6,15},{7,13},{8,1},{9,3},... | collective-permute-start | bytes 368648 | tf_op jit(solution)/shard_map/ppermute | solution.py:203
  81.8 3.2 %collective-permute-start.24 = (bf16[3,160,384]{2,1,0:T(8,128)(2,1)S(1)}, bf16[3,160,384]{2,1,0:T(8,128)(2,1)S(1)}, u32[]{:S(2)}, u32[]{:S(2)}) collective-permute-start(bf16[3,160,384]{2,1,0:T(8,128)(2,1)S(1)} %passed.3.trio_ref), channel_id=1, source_target_pairs={{0,8},{1,9},{2,10},{3,11},{4,12},{5,13},{6,14},{7,15},{8,0},{9,1},... | collective-permute-start | bytes 1105928 | tf_op jit(solution)/shard_map/ppermute | solution.py:203
  84.4 1.5 %copy-start = (f32[288,384]{1,0:T(8,128)S(1)}, f32[288,384]{1,0:T(8,128)}, u32[]{:S(2)}) copy-start(f32[288,384]{1,0:T(8,128)} %refs_2_.3) | copy-start | bytes 1327108
  84.5 1.5 %copy-start.1 = (f32[48,192]{1,0:T(8,128)S(1)}, f32[48,192]{1,0:T(8,128)}, u32[]{:S(2)}) copy-start(f32[48,192]{1,0:T(8,128)} %refs_3_.3) | copy-start | bytes 110596
  84.5 1.4 %copy-start.2 = (f32[24,10]{0,1:T(8,128)S(1)}, f32[24,10]{0,1:T(8,128)}, u32[]{:S(2)}) copy-start(f32[24,10]{0,1:T(8,128)} %param.23) | copy-start | bytes 2884
  84.5 1.4 %collective-permute-start.25 = (bf16[1,160,384]{2,1,0:T(8,128)(2,1)S(1)}, bf16[1,160,384]{2,1,0:T(8,128)(2,1)S(1)}, u32[]{:S(2)}, u32[]{:S(2)}) collective-permute-start(bf16[1,160,384]{2,1,0:T(8,128)(2,1)S(1)} %passed_last.3.one_ref), channel_id=1, source_target_pairs={{0,8},{1,9},{2,10},{3,11},{4,12},{5,13},{6,14},{7,15},{8,0},{9,1},... | collective-permute-start | bytes 368648 | tf_op jit(solution)/shard_map/ppermute | solution.py:203

commit v5 on v4

--- a/solution.py
+++ b/solution.py
@@ -271,7 +271,7 @@
     return jax.ShapeDtypeStruct(shape, dtype)
 
 
-MICROS = {"passed": 5.0, "passed_last": 20.0, "passed_one": 20.0, "add_far3": 20.0}
+MICROS = {"passed": 5.0, "passed_last": 20.0, "passed_one": 20.0, "add_far3": 20.0, "relay": 10.0, "first_join": 20.0}
 
 
 def placed(shape, spec):

time: 97.7 us -> 97.7 us (level)
  no operation moved by 1% of the time
where the time goes in v5:
time: 97.7 us; the launch traced here: 97.5 us
  Pallas kernels  34.2 us (35%)
  waiting for transfers between devices  30.1 us (31%)
  starting transfers between devices  18.6 us (19%)
  blocking collectives  13 us (13%)
  between operations  1.6 us (2%)
    pallas_call x36, Pallas kernels, run(): kernel_call(*[pltpu.with_memory_space_constraint(array, pltpu.HBM) if spe...  34.2 us
    ppermute x26, waiting for transfers between devices, swap(): return lax.ppermute(array, BOTH, perm)  30.1 us
    ppermute x26, starting transfers between devices, swap(): return lax.ppermute(array, BOTH, perm)  18.6 us
    all_to_all x1, blocking collectives, paired_plan(): all_stats = lax.all_to_all(stats, BOTH, 0, 0, tiled=True)  13 us
  transfers between devices with their start and end apart: 26, of which 17 were waited for; matrix products, arithmetic and copies ran while one was open for 0% of the time, Pallas kernels for 17%

profile of v5, /device:TPU:0, one launch (start us, length us, event | category | flops | bytes accessed | tf_op | source)
XLA Modules:
  0.0 97.5 jit_solution(16289105897147209689)
XLA Ops:
  0.7 1.2 %pack_weights.1.after_ref.own_ref = bf16[1,160,384]{2,1,0:T(8,128)(2,1)S(1)} custom-call(f32[288,384]{1,0:T(8,128)} %refs_2_.3, f32[48,192]{1,0:T(8,128)} %refs_3_.3, f32[10,24]{1,0:T(8,128)} %bitcast.13), custom_call_target="tpu_custom_call" | custom-call | tf_op jit(solution)/shard_map/pack_weights/pallas_call | solution.py:306
  1.8 4.1 %collective-permute-start = (bf16[1,160,384]{2,1,0:T(8,128)(2,1)S(1)}, bf16[1,160,384]{2,1,0:T(8,128)(2,1)S(1)}, u32[]{:S(2)}, u32[]{:S(2)}) collective-permute-start(bf16[1,160,384]{2,1,0:T(8,128)(2,1)S(1)} %pack_weights.1.after_ref.own_ref), channel_id=1, source_target_pairs={{0,4},{1,5},{2,6},{3,7},{4,0},{5,1},{6,2},{7,3},{8,12},{9,13},{10,... | collective-permute-start | bytes 368648 | tf_op jit(solution)/shard_map/ppermute | solution.py:203
  5.9 0.7 collective-permute-start.1
  7.2 3.6 %stage.1 = (bf16[192,2304]{1,0:T(8,128)(2,1)S(1)}, s32[1,192]{1,0:T(1,128)S(1)}, f32[1,586]{1,0:T(1,128)S(1)}, f32[1,586]{1,0:T(1,128)S(1)}, f32[1,586]{1,0:T(1,...) custom-call(bf16[1,160,384]{2,1,0:T(8,128)(2,1)S(1)} %pack_weights.1, ...), custom_call_target="tpu_custom_call" | custom-call | tf_op jit(solution)/shard_map/stage/pallas_call | solution.py:306
  10.9 1.0 %collective-permute-done.far_ref = bf16[1,160,384]{2,1,0:T(8,128)(2,1)S(1)} collective-permute-done((bf16[1,160,384]{2,1,0:T(8,128)(2,1)S(1)}, bf16[1,160,384]{2,1,0:T(8,128)(2,1)S(1)}, u32[]{:S(2)}, u32[]{:S(2)}) %collective-permute-start) | collective-permute-done | bytes 122912 | tf_op jit(solution)/shard_map/ppermute | solution.py:203
  12.1 1.8 %collective-permute-start.3 = (bf16[3,160,384]{2,1,0:T(8,128)(2,1)S(1)}, bf16[3,160,384]{2,1,0:T(8,128)(2,1)S(1)}, u32[]{:S(2)}, u32[]{:S(2)}) collective-permute-start(bf16[3,160,384]{2,1,0:T(8,128)(2,1)S(1)} %get-tuple-element.74.trio_ref), channel_id=1, source_target_pairs={{0,10},{1,8},{2,11},{3,9},{4,14},{5,12},{6,15},{7,13},{8,1},{9,3},... | collective-permute-start | bytes 1105928 | tf_op jit(solution)/shard_map/ppermute | solution.py:203
  13.9 2.7 %collective-permute-done.2.in_ref = bf16[1,160,384]{2,1,0:T(8,128)(2,1)S(1)} collective-permute-done((bf16[1,160,384]{2,1,0:T(8,128)(2,1)S(1)}, bf16[1,160,384]{2,1,0:T(8,128)(2,1)S(1)}, u32[]{:S(2)}, u32[]{:S(2)}) %collective-permute-start.2) | collective-permute-done | bytes 122912 | tf_op jit(solution)/shard_map/ppermute | solution.py:203
  16.7 2.5 %collective-permute-start.4 = (bf16[1,160,384]{2,1,0:T(8,128)(2,1)S(1)}, bf16[1,160,384]{2,1,0:T(8,128)(2,1)S(1)}, u32[]{:S(2)}, u32[]{:S(2)}) collective-permute-start(bf16[1,160,384]{2,1,0:T(8,128)(2,1)S(1)} %passed_one.2.one_ref), channel_id=1, source_target_pairs={{0,10},{1,8},{2,11},{3,9},{4,14},{5,12},{6,15},{7,13},{8,1},{9,3},... | collective-permute-start | bytes 368648 | tf_op jit(solution)/shard_map/ppermute | solution.py:203
  19.2 1.2 %collective-permute-done.3.in_ref = bf16[3,160,384]{2,1,0:T(8,128)(2,1)S(1)} collective-permute-done((bf16[3,160,384]{2,1,0:T(8,128)(2,1)S(1)}, bf16[3,160,384]{2,1,0:T(8,128)(2,1)S(1)}, u32[]{:S(2)}, u32[]{:S(2)}) %collective-permute-start.3) | collective-permute-done | bytes 368672 | tf_op jit(solution)/shard_map/ppermute | solution.py:203
  20.6 1.2 %collective-permute-done.4.in_ref = bf16[1,160,384]{2,1,0:T(8,128)(2,1)S(1)} collective-permute-done((bf16[1,160,384]{2,1,0:T(8,128)(2,1)S(1)}, bf16[1,160,384]{2,1,0:T(8,128)(2,1)S(1)}, u32[]{:S(2)}, u32[]{:S(2)}) %collective-permute-start.4) | collective-permute-done | bytes 122912 | tf_op jit(solution)/shard_map/ppermute | solution.py:203
  21.8 0.7 collective-permute-start.7
  22.5 1.0 %collective-permute-done.7.refs_5_ = bf16[1,160,384]{2,1,0:T(8,128)(2,1)S(1)} collective-permute-done((bf16[1,160,384]{2,1,0:T(8,128)(2,1)S(1)}, bf16[1,160,384]{2,1,0:T(8,128)(2,1)S(1)}, u32[]{:S(2)}, u32[]{:S(2)}) %collective-permute-start.7) | collective-permute-done | bytes 122912 | tf_op jit(solution)/shard_map/ppermute | solution.py:203
  23.5 2.9 %worker.1 = (f32[2304,384]{1,0:T(8,128)S(1)}, f32[192,384]{1,0:T(8,128)S(1)}, f32[10,192]{1,0:T(8,128)S(1)}, f32[32,1,640]{2,1,0:T(1,128)S(1)}) custom-call(bf16[4,160,384]{2,1,0:T(8,128)(2,1)S(1)} %relay.2.refs_0_, bf16[3,160,384]{2,1,0:T(8,128)(2,1)S(1)} %passed.2.refs_1_, bf16[1,160,384]{2,1,0:T(8,128)(2,1)S(1)} %passed_last.2.refs_2_, ...), custom_call_target="tpu_custom_call" | custom-call | tf_op jit(solution)/shard_map/worker/pallas_call | solution.py:306
  26.4 13.0 %all_to_all.5.stats_ref = f32[32,1,640]{2,1,0:T(1,128)S(1)} all-to-all(f32[32,1,640]{2,1,0:T(1,128)S(1)} %get-tuple-element.82.mine_ref), channel_id=1, replica_groups=mesh['grp'=4,'wide'=8] {'grp','wide'}, dimensions={0} | all-to-all | bytes 163840 | tf_op jit(solution)/shard_map/all_to_all | solution.py:923
  39.4 0.6 codes_first.1
  40.4 1.1 %collective-permute-done.8.refs_1_ = bf16[1,160,384]{2,1,0:T(8,128)(2,1)S(1)} collective-permute-done((bf16[1,160,384]{2,1,0:T(8,128)(2,1)S(1)}, bf16[1,160,384]{2,1,0:T(8,128)(2,1)S(1)}, u32[]{:S(2)}, u32[]{:S(2)}) %collective-permute-start.8) | collective-permute-done | bytes 122912 | tf_op jit(solution)/shard_map/ppermute | solution.py:203
  41.5 0.9 codes.5
  42.6 0.5 collective-permute-start.12
  43.1 0.9 codes.4.refs_0_
  44.0 0.8 collective-permute-done.9.refs_1_
  44.9 0.5 collective-permute-start.11
  45.4 1.5 %collective-permute-done.12.refs_2_ = bf16[1,160,384]{2,1,0:T(8,128)(2,1)S(1)} collective-permute-done((bf16[1,160,384]{2,1,0:T(8,128)(2,1)S(1)}, bf16[1,160,384]{2,1,0:T(8,128)(2,1)S(1)}, u32[]{:S(2)}, u32[]{:S(2)}) %collective-permute-start.12) | collective-permute-done | bytes 122912 | tf_op jit(solution)/shard_map/ppermute | solution.py:203
  47.0 0.9 collective-permute-start.14
  47.9 0.4 collective-permute-start.10
  48.3 1.3 %totals.1 = (f32[586]{0:T(1024)}, f32[586]{0:T(1024)}, f32[586]{0:T(1024)}, f32[1,1]{1,0:T(1,128)}, f32[1,1]{1,0:T(1,128)}) custom-call(bf16[1,160,384]{2,1,0:T(8,128)(2,1)S(1)} %add_far3.1.refs_0_.after_ref, f32[32,1,640]{2,1,0:T(1,128)S(1)} %all_to_all.5.stats_ref, f32[1,586]{1,0:T(1,128)S(1)} %get-tuple-element.78.refs_9_.bias_ref, ...), custom_call_target="tpu_custom_call" | custom-call | tf_op jit(solution)/shard_map/totals/pallas_call | solution.py:306
  49.6 1.0 %collective-permute-done.11.in_ref = bf16[2,160,384]{2,1,0:T(8,128)(2,1)S(1)} collective-permute-done((bf16[2,160,384]{2,1,0:T(8,128)(2,1)S(1)}, bf16[2,160,384]{2,1,0:T(8,128)(2,1)S(1)}, u32[]{:S(2)}, u32[]{:S(2)}) %collective-permute-start.11) | collective-permute-done | bytes 245792 | tf_op jit(solution)/shard_map/ppermute | solution.py:203
  50.6 2.1 %collective-permute-done.14.refs_3_ = bf16[1,160,384]{2,1,0:T(8,128)(2,1)S(1)} collective-permute-done((bf16[1,160,384]{2,1,0:T(8,128)(2,1)S(1)}, bf16[1,160,384]{2,1,0:T(8,128)(2,1)S(1)}, u32[]{:S(2)}, u32[]{:S(2)}) %collective-permute-start.14) | collective-permute-done | bytes 122912 | tf_op jit(solution)/shard_map/ppermute | solution.py:203
  52.8 1.0 %collective-permute-start.15 = (bf16[1,160,384]{2,1,0:T(8,128)(2,1)S(1)}, bf16[1,160,384]{2,1,0:T(8,128)(2,1)S(1)}, u32[]{:S(2)}, u32[]{:S(2)}) collective-permute-start(bf16[1,160,384]{2,1,0:T(8,128)(2,1)S(1)} %add_last.1.after_ref), channel_id=1, source_target_pairs={{0,4},{1,5},{2,6},{3,7},{4,0},{5,1},{6,2},{7,3},{8,12},{9,13},{10,... | collective-permute-start | bytes 368648 | tf_op jit(solution)/shard_map/ppermute | solution.py:203
  53.8 0.4 collective-permute-start.13
  54.2 2.4 %new_resid.2.refs_5_.refs_0_ = f32[2304,384]{1,0:T(8,128)} custom-call(bf16[1,160,384]{2,1,0:T(8,128)(2,1)S(1)} %add_last.1.after_ref, f32[1,128]{1,0:T(1,128)S(1)} %get-tuple-element.89.head_ref, f32[2304,384]{1,0:T(8,128)S(1)} %get-tuple-element.83.acc6_ref.acc6, s32[2304,384]{1,0:T(8,128)S(1)} %get-tuple-element.84.noise6_ref.noise6), custom_call_target="tpu_custom_call" | custom-call | tf_op jit(solution)/shard_map/new_resid/pallas_call | solution.py:306
  56.6 4.6 %collective-permute-done.15.refs_4_ = bf16[1,160,384]{2,1,0:T(8,128)(2,1)S(1)} collective-permute-done((bf16[1,160,384]{2,1,0:T(8,128)(2,1)S(1)}, bf16[1,160,384]{2,1,0:T(8,128)(2,1)S(1)}, u32[]{:S(2)}, u32[]{:S(2)}) %collective-permute-start.15) | collective-permute-done | bytes 122912 | tf_op jit(solution)/shard_map/ppermute | solution.py:203
  61.4 0.6 collective-permute-start.16
  62.0 1.2 %hold_moments.1.held_ref = f32[1,160,384]{2,1,0:T(8,128)S(1)} custom-call(bf16[1,160,384]{2,1,0:T(8,128)(2,1)S(1)} %add_mine.1.after_ref.mine_ref, f32[288,384]{1,0:T(8,128)} %m6_ref.1, f32[48,192]{1,0:T(8,128)} %m7_ref.1, f32[10,24]{1,0:T(8,128)} %bitcast.19), custom_call_target="tpu_custom_call" | custom-call | tf_op jit(solution)/shard_map/hold_moments/pallas_call | solution.py:306
  63.1 3.5 %collective-permute-done.16.theirs_ref = bf16[1,160,384]{2,1,0:T(8,128)(2,1)S(1)} collective-permute-done((bf16[1,160,384]{2,1,0:T(8,128)(2,1)S(1)}, bf16[1,160,384]{2,1,0:T(8,128)(2,1)S(1)}, u32[]{:S(2)}, u32[]{:S(2)}) %collective-permute-start.16) | collective-permute-done | bytes 122912 | tf_op jit(solution)/shard_map/ppermute | solution.py:203
  66.8 0.4 collective-permute-start.18
  67.3 1.0 small_resids.1
  68.2 2.4 %new_resid.3.refs_0_ = f32[2304,384]{1,0:T(8,128)} custom-call(bf16[1,160,384]{2,1,0:T(8,128)(2,1)S(1)} %get-tuple-element.98.after_ref.own_ref, f32[1,128]{1,0:T(1,128)S(1)} %get-tuple-element.89.head_ref, f32[2304,384]{1,0:T(8,128)S(1)} %get-tuple-element.83.acc6_ref.acc6, ...), custom_call_target="tpu_custom_call", output_to_operand_aliasing={{}: (4, {})} | custom-call | tf_op jit(solution)/shard_map/new_resid/pallas_call | solution.py:306
  70.7 2.7 %collective-permute-done.17.far_ref = bf16[1,160,384]{2,1,0:T(8,128)(2,1)S(1)} collective-permute-done((bf16[1,160,384]{2,1,0:T(8,128)(2,1)S(1)}, bf16[1,160,384]{2,1,0:T(8,128)(2,1)S(1)}, u32[]{:S(2)}, u32[]{:S(2)}) %collective-permute-start.17) | collective-permute-done | bytes 122912 | tf_op jit(solution)/shard_map/ppermute | solution.py:203
  73.5 0.5 collective-permute-start.19
  74.0 4.7 %collective-permute-done.19.in_ref = bf16[1,160,384]{2,1,0:T(8,128)(2,1)S(1)} collective-permute-done((bf16[1,160,384]{2,1,0:T(8,128)(2,1)S(1)}, bf16[1,160,384]{2,1,0:T(8,128)(2,1)S(1)}, u32[]{:S(2)}, u32[]{:S(2)}) %collective-permute-start.19) | collective-permute-done | bytes 122912 | tf_op jit(solution)/shard_map/ppermute | solution.py:203
  78.8 0.5 early_grams.1
  79.3 0.6 collective-permute-start.21
  79.9 0.4 collective-permute-done.23.theirs_ref
  80.3 1.4 %momenta.1 = (f32[288,384]{1,0:T(8,128)}, f32[48,192]{1,0:T(8,128)}, f32[10,24]{1,0:T(8,128)}, f32[288,384]{1,0:T(8,128)S(1)}, f32[72,256]{1,0:T(8,128)S(1)}) custom-call(f32[1,160,384]{2,1,0:T(8,128)S(1)} %get-tuple-element.110.mine_ref, f32[1,160,384]{2,1,0:T(8,128)S(1)} %collective-permute-done.23.theirs_ref), custom_call_target="tpu_custom_call" | custom-call | tf_op jit(solution)/shard_map/momenta/pallas_call | solution.py:306
  81.8 1.9 %collective-permute-start.24 = (bf16[3,160,384]{2,1,0:T(8,128)(2,1)S(1)}, bf16[3,160,384]{2,1,0:T(8,128)(2,1)S(1)}, u32[]{:S(2)}, u32[]{:S(2)}) collective-permute-start(bf16[3,160,384]{2,1,0:T(8,128)(2,1)S(1)} %passed.3.trio_ref), channel_id=1, source_target_pairs={{0,8},{1,9},{2,10},{3,11},{4,12},{5,13},{6,14},{7,15},{8,0},{9,1},... | collective-permute-start | bytes 1105928 | tf_op jit(solution)/shard_map/ppermute | solution.py:203
  83.7 0.7 middle_grams.1
  85.0 0.6 late_grams.1
  85.9 11.6 %update.1 = (f32[288,384]{1,0:T(8,128)}, f32[48,192]{1,0:T(8,128)}, f32[10,24]{1,0:T(8,128)}, bf16[288,384]{1,0:T(8,128)(2,1)}, bf16[48,192]{1,0:T(8,128)(2,1)}, /*index=5*/bf16[10,24]{1,0:T(8,128)(2,1)}) custom-call(f32[384,384]{1,0:T(8,128)S(1)} %get-tuple-element.112.own6, f32[256,256]{1,0:T(8,128)S(1)} %get-tuple-element.113.own78, ...), custom_call_target="tpu_custom_call" | custom-call | tf_op jit(solution)/shard_map/update/pallas_call | solution.py:306
  (47 shorter events, 2.6 us)
Async XLA Ops:
  1.8 10.1 %collective-permute-start = (bf16[1,160,384]{2,1,0:T(8,128)(2,1)S(1)}, bf16[1,160,384]{2,1,0:T(8,128)(2,1)S(1)}, u32[]{:S(2)}, u32[]{:S(2)}) collective-permute-start(bf16[1,160,384]{2,1,0:T(8,128)(2,1)S(1)} %pack_weights.1.after_ref.own_ref), channel_id=1, source_target_pairs={{0,4},{1,5},{2,6},{3,7},{4,0},{5,1},{6,2},{7,3},{8,12},{9,13},{10,... | collective-permute-start | bytes 368648 | tf_op jit(solution)/shard_map/ppermute | solution.py:203
  5.9 6.0 %collective-permute-start.1 = (bf16[1,160,384]{2,1,0:T(8,128)(2,1)S(1)}, bf16[1,160,384]{2,1,0:T(8,128)(2,1)S(1)}, u32[]{:S(2)}, u32[]{:S(2)}) collective-permute-start(bf16[1,160,384]{2,1,0:T(8,128)(2,1)S(1)} %pack_weights.1.after_ref.own_ref), channel_id=1, source_target_pairs={{0,9},{1,11},{2,8},{3,10},{4,13},{5,15},{6,12},{7,14},{8,2},{9,0},... | collective-permute-start | bytes 368648 | tf_op jit(solution)/shard_map/ppermute | solution.py:203
  11.9 4.7 %collective-permute-start.2 = (bf16[1,160,384]{2,1,0:T(8,128)(2,1)S(1)}, bf16[1,160,384]{2,1,0:T(8,128)(2,1)S(1)}, u32[]{:S(2)}, u32[]{:S(2)}) collective-permute-start(bf16[1,160,384]{2,1,0:T(8,128)(2,1)S(1)} %get-tuple-element.75), channel_id=1, source_target_pairs={{0,9},{1,11},{2,8},{3,10},{4,13},{5,15},{6,12},{7,14},{8,2},{9,0},... | collective-permute-start | bytes 368648 | tf_op jit(solution)/shard_map/ppermute | solution.py:203
  12.1 8.3 %collective-permute-start.3 = (bf16[3,160,384]{2,1,0:T(8,128)(2,1)S(1)}, bf16[3,160,384]{2,1,0:T(8,128)(2,1)S(1)}, u32[]{:S(2)}, u32[]{:S(2)}) collective-permute-start(bf16[3,160,384]{2,1,0:T(8,128)(2,1)S(1)} %get-tuple-element.74.trio_ref), channel_id=1, source_target_pairs={{0,10},{1,8},{2,11},{3,9},{4,14},{5,12},{6,15},{7,13},{8,1},{9,3},... | collective-permute-start | bytes 1105928 | tf_op jit(solution)/shard_map/ppermute | solution.py:203
  16.7 5.1 %collective-permute-start.4 = (bf16[1,160,384]{2,1,0:T(8,128)(2,1)S(1)}, bf16[1,160,384]{2,1,0:T(8,128)(2,1)S(1)}, u32[]{:S(2)}, u32[]{:S(2)}) collective-permute-start(bf16[1,160,384]{2,1,0:T(8,128)(2,1)S(1)} %passed_one.2.one_ref), channel_id=1, source_target_pairs={{0,10},{1,8},{2,11},{3,9},{4,14},{5,12},{6,15},{7,13},{8,1},{9,3},... | collective-permute-start | bytes 368648 | tf_op jit(solution)/shard_map/ppermute | solution.py:203
  19.2 4.3 %collective-permute-start.5 = (bf16[4,160,384]{2,1,0:T(8,128)(2,1)S(1)}, bf16[4,160,384]{2,1,0:T(8,128)(2,1)S(1)}, u32[]{:S(2)}, u32[]{:S(2)}) collective-permute-start(bf16[4,160,384]{2,1,0:T(8,128)(2,1)S(1)} %relay.2.refs_0_), channel_id=1, source_target_pairs={{0,8},{1,9},{2,10},{3,11},{4,12},{5,13},{6,14},{7,15},{8,0},{9,1},... | collective-permute-start | bytes 1474568 | tf_op jit(solution)/shard_map/ppermute | solution.py:203
  20.5 3.0 %collective-permute-start.6 = (bf16[3,160,384]{2,1,0:T(8,128)(2,1)S(1)}, bf16[3,160,384]{2,1,0:T(8,128)(2,1)S(1)}, u32[]{:S(2)}, u32[]{:S(2)}) collective-permute-start(bf16[3,160,384]{2,1,0:T(8,128)(2,1)S(1)} %passed.2.refs_1_), channel_id=1, source_target_pairs={{0,8},{1,9},{2,10},{3,11},{4,12},{5,13},{6,14},{7,15},{8,0},{9,1},... | collective-permute-start | bytes 1105928 | tf_op jit(solution)/shard_map/ppermute | solution.py:203
  21.8 1.7 %collective-permute-start.7 = (bf16[1,160,384]{2,1,0:T(8,128)(2,1)S(1)}, bf16[1,160,384]{2,1,0:T(8,128)(2,1)S(1)}, u32[]{:S(2)}, u32[]{:S(2)}) collective-permute-start(bf16[1,160,384]{2,1,0:T(8,128)(2,1)S(1)} %passed_last.2.refs_2_), channel_id=1, source_target_pairs={{0,8},{1,9},{2,10},{3,11},{4,12},{5,13},{6,14},{7,15},{8,0},{9,1},... | collective-permute-start | bytes 368648 | tf_op jit(solution)/shard_map/ppermute | solution.py:203
  40.0 1.4 %collective-permute-start.8 = (bf16[1,160,384]{2,1,0:T(8,128)(2,1)S(1)}, bf16[1,160,384]{2,1,0:T(8,128)(2,1)S(1)}, u32[]{:S(2)}, u32[]{:S(2)}) collective-permute-start(bf16[1,160,384]{2,1,0:T(8,128)(2,1)S(1)} %get-tuple-element.92), channel_id=1, source_target_pairs={{0,8},{1,9},{2,10},{3,11},{4,12},{5,13},{6,14},{7,15},{8,0},{9,1},... | collective-permute-start | bytes 368648 | tf_op jit(solution)/shard_map/ppermute | solution.py:203
  42.4 2.5 %collective-permute-start.9 = (bf16[7,160,384]{2,1,0:T(8,128)(2,1)S(1)}, bf16[7,160,384]{2,1,0:T(8,128)(2,1)S(1)}, u32[]{:S(2)}, u32[]{:S(2)}) collective-permute-start(bf16[7,160,384]{2,1,0:T(8,128)(2,1)S(1)} %codes.5), channel_id=1, source_target_pairs={{0,8},{1,9},{2,10},{3,11},{4,12},{5,13},{6,14},{7,15},{8,0},{9,1},... | collective-permute-start | bytes 2580488 | tf_op jit(solution)/shard_map/ppermute | solution.py:203
  42.6 4.3 %collective-permute-start.12 = (bf16[1,160,384]{2,1,0:T(8,128)(2,1)S(1)}, bf16[1,160,384]{2,1,0:T(8,128)(2,1)S(1)}, u32[]{:S(2)}, u32[]{:S(2)}) collective-permute-start(bf16[1,160,384]{2,1,0:T(8,128)(2,1)S(1)} %add.3.refs_0_), channel_id=1, source_target_pairs={{0,10},{1,8},{2,11},{3,9},{4,14},{5,12},{6,15},{7,13},{8,1},{9,3},... | collective-permute-start | bytes 368648 | tf_op jit(solution)/shard_map/ppermute | solution.py:203
  44.9 5.7 %collective-permute-start.11 = (bf16[2,160,384]{2,1,0:T(8,128)(2,1)S(1)}, bf16[2,160,384]{2,1,0:T(8,128)(2,1)S(1)}, u32[]{:S(2)}, u32[]{:S(2)}) collective-permute-start(bf16[2,160,384]{2,1,0:T(8,128)(2,1)S(1)} %add.5), channel_id=1, source_target_pairs={{0,10},{1,8},{2,11},{3,9},{4,14},{5,12},{6,15},{7,13},{8,1},{9,3},... | collective-permute-start | bytes 737288 | tf_op jit(solution)/shard_map/ppermute | solution.py:203
  47.0 5.8 %collective-permute-start.14 = (bf16[1,160,384]{2,1,0:T(8,128)(2,1)S(1)}, bf16[1,160,384]{2,1,0:T(8,128)(2,1)S(1)}, u32[]{:S(2)}, u32[]{:S(2)}) collective-permute-start(bf16[1,160,384]{2,1,0:T(8,128)(2,1)S(1)} %add_far3.1.refs_0_.after_ref), channel_id=1, source_target_pairs={{0,9},{1,11},{2,8},{3,10},{4,13},{5,15},{6,12},{7,14},{8,2},{9,0},... | collective-permute-start | bytes 368648 | tf_op jit(solution)/shard_map/ppermute | solution.py:203
  47.9 8.8 %collective-permute-start.10 = (bf16[1,160,384]{2,1,0:T(8,128)(2,1)S(1)}, bf16[1,160,384]{2,1,0:T(8,128)(2,1)S(1)}, u32[]{:S(2)}, u32[]{:S(2)}) collective-permute-start(bf16[1,160,384]{2,1,0:T(8,128)(2,1)S(1)} %add.4), channel_id=1, source_target_pairs={{0,10},{1,8},{2,11},{3,9},{4,14},{5,12},{6,15},{7,13},{8,1},{9,3},... | collective-permute-start | bytes 368648 | tf_op jit(solution)/shard_map/ppermute | solution.py:203
  52.8 8.5 %collective-permute-start.15 = (bf16[1,160,384]{2,1,0:T(8,128)(2,1)S(1)}, bf16[1,160,384]{2,1,0:T(8,128)(2,1)S(1)}, u32[]{:S(2)}, u32[]{:S(2)}) collective-permute-start(bf16[1,160,384]{2,1,0:T(8,128)(2,1)S(1)} %add_last.1.after_ref), channel_id=1, source_target_pairs={{0,4},{1,5},{2,6},{3,7},{4,0},{5,1},{6,2},{7,3},{8,12},{9,13},{10,... | collective-permute-start | bytes 368648 | tf_op jit(solution)/shard_map/ppermute | solution.py:203
  53.8 7.4 %collective-permute-start.13 = (bf16[1,160,384]{2,1,0:T(8,128)(2,1)S(1)}, bf16[1,160,384]{2,1,0:T(8,128)(2,1)S(1)}, u32[]{:S(2)}, u32[]{:S(2)}) collective-permute-start(bf16[1,160,384]{2,1,0:T(8,128)(2,1)S(1)} %add_far2.1), channel_id=1, source_target_pairs={{0,9},{1,11},{2,8},{3,10},{4,13},{5,15},{6,12},{7,14},{8,2},{9,0},... | collective-permute-start | bytes 368648 | tf_op jit(solution)/shard_map/ppermute | solution.py:203
  61.4 5.3 %collective-permute-start.16 = (bf16[1,160,384]{2,1,0:T(8,128)(2,1)S(1)}, bf16[1,160,384]{2,1,0:T(8,128)(2,1)S(1)}, u32[]{:S(2)}, u32[]{:S(2)}) collective-permute-start(bf16[1,160,384]{2,1,0:T(8,128)(2,1)S(1)} %add_mine.1.after_ref.mine_ref), channel_id=1, source_target_pairs={{0,16},{1,17},{2,18},{3,19},{4,20},{5,21},{6,22},{7,23},{8,24},{9,... | collective-permute-start | bytes 368648 | tf_op jit(solution)/shard_map/ppermute | solution.py:203
  66.8 6.7 %collective-permute-start.17 = (bf16[1,160,384]{2,1,0:T(8,128)(2,1)S(1)}, bf16[1,160,384]{2,1,0:T(8,128)(2,1)S(1)}, u32[]{:S(2)}, u32[]{:S(2)}) collective-permute-start(bf16[1,160,384]{2,1,0:T(8,128)(2,1)S(1)} %get-tuple-element.98.after_ref.own_ref), channel_id=1, source_target_pairs={{0,4},{1,5},{2,6},{3,7},{4,0},{5,1},{6,2},{7,3},{8,12},{9,13},{10,... | collective-permute-start | bytes 368648 | tf_op jit(solution)/shard_map/ppermute | solution.py:203
  66.8 6.6 %collective-permute-start.18 = (bf16[1,160,384]{2,1,0:T(8,128)(2,1)S(1)}, bf16[1,160,384]{2,1,0:T(8,128)(2,1)S(1)}, u32[]{:S(2)}, u32[]{:S(2)}) collective-permute-start(bf16[1,160,384]{2,1,0:T(8,128)(2,1)S(1)} %get-tuple-element.98.after_ref.own_ref), channel_id=1, source_target_pairs={{0,9},{1,11},{2,8},{3,10},{4,13},{5,15},{6,12},{7,14},{8,2},{9,0},... | collective-permute-start | bytes 368648 | tf_op jit(solution)/shard_map/ppermute | solution.py:203
  73.5 5.2 %collective-permute-start.19 = (bf16[1,160,384]{2,1,0:T(8,128)(2,1)S(1)}, bf16[1,160,384]{2,1,0:T(8,128)(2,1)S(1)}, u32[]{:S(2)}, u32[]{:S(2)}) collective-permute-start(bf16[1,160,384]{2,1,0:T(8,128)(2,1)S(1)} %get-tuple-element.101), channel_id=1, source_target_pairs={{0,9},{1,11},{2,8},{3,10},{4,13},{5,15},{6,12},{7,14},{8,2},{9,0},... | collective-permute-start | bytes 368648 | tf_op jit(solution)/shard_map/ppermute | solution.py:203
  74.0 7.8 %collective-permute-start.20 = (bf16[3,160,384]{2,1,0:T(8,128)(2,1)S(1)}, bf16[3,160,384]{2,1,0:T(8,128)(2,1)S(1)}, u32[]{:S(2)}, u32[]{:S(2)}) collective-permute-start(bf16[3,160,384]{2,1,0:T(8,128)(2,1)S(1)} %get-tuple-element.100.trio_ref), channel_id=1, source_target_pairs={{0,10},{1,8},{2,11},{3,9},{4,14},{5,12},{6,15},{7,13},{8,1},{9,3},... | collective-permute-start | bytes 1105928 | tf_op jit(solution)/shard_map/ppermute | solution.py:203
  78.7 1.6 %collective-permute-start.23 = (f32[1,160,384]{2,1,0:T(8,128)S(1)}, f32[1,160,384]{2,1,0:T(8,128)S(1)}, u32[]{:S(2)}, u32[]{:S(2)}) collective-permute-start(f32[1,160,384]{2,1,0:T(8,128)S(1)} %get-tuple-element.110.mine_ref), channel_id=1, source_target_pairs={{0,8},{1,9},{2,10},{3,11},{4,12},{5,13},{6,14},{7,15},{8,0},{9,1},... | collective-permute-start | bytes 737288 | tf_op jit(solution)/shard_map/ppermute | solution.py:203
  79.3 4.3 %collective-permute-start.21 = (bf16[4,160,384]{2,1,0:T(8,128)(2,1)S(1)}, bf16[4,160,384]{2,1,0:T(8,128)(2,1)S(1)}, u32[]{:S(2)}, u32[]{:S(2)}) collective-permute-start(bf16[4,160,384]{2,1,0:T(8,128)(2,1)S(1)} %get-tuple-element.103.four_ref.refs_0_), channel_id=1, source_target_pairs={{0,8},{1,9},{2,10},{3,11},{4,12},{5,13},{6,14},{7,15},{8,0},{9,1},... | collective-permute-start | bytes 1474568 | tf_op jit(solution)/shard_map/ppermute | solution.py:203
  79.9 4.5 %collective-permute-start.22 = (bf16[1,160,384]{2,1,0:T(8,128)(2,1)S(1)}, bf16[1,160,384]{2,1,0:T(8,128)(2,1)S(1)}, u32[]{:S(2)}, u32[]{:S(2)}) collective-permute-start(bf16[1,160,384]{2,1,0:T(8,128)(2,1)S(1)} %passed_one.3.one_ref), channel_id=1, source_target_pairs={{0,10},{1,8},{2,11},{3,9},{4,14},{5,12},{6,15},{7,13},{8,1},{9,3},... | collective-permute-start | bytes 368648 | tf_op jit(solution)/shard_map/ppermute | solution.py:203
  81.8 3.2 %collective-permute-start.24 = (bf16[3,160,384]{2,1,0:T(8,128)(2,1)S(1)}, bf16[3,160,384]{2,1,0:T(8,128)(2,1)S(1)}, u32[]{:S(2)}, u32[]{:S(2)}) collective-permute-start(bf16[3,160,384]{2,1,0:T(8,128)(2,1)S(1)} %passed.3.trio_ref), channel_id=1, source_target_pairs={{0,8},{1,9},{2,10},{3,11},{4,12},{5,13},{6,14},{7,15},{8,0},{9,1},... | collective-permute-start | bytes 1105928 | tf_op jit(solution)/shard_map/ppermute | solution.py:203
  84.4 1.5 %copy-start = (f32[288,384]{1,0:T(8,128)S(1)}, f32[288,384]{1,0:T(8,128)}, u32[]{:S(2)}) copy-start(f32[288,384]{1,0:T(8,128)} %refs_2_.3) | copy-start | bytes 1327108
  84.4 1.5 %copy-start.1 = (f32[48,192]{1,0:T(8,128)S(1)}, f32[48,192]{1,0:T(8,128)}, u32[]{:S(2)}) copy-start(f32[48,192]{1,0:T(8,128)} %refs_3_.3) | copy-start | bytes 110596
  84.5 1.4 %copy-start.2 = (f32[24,10]{0,1:T(8,128)S(1)}, f32[24,10]{0,1:T(8,128)}, u32[]{:S(2)}) copy-start(f32[24,10]{0,1:T(8,128)} %param.23) | copy-start | bytes 2884
  84.5 1.4 %collective-permute-start.25 = (bf16[1,160,384]{2,1,0:T(8,128)(2,1)S(1)}, bf16[1,160,384]{2,1,0:T(8,128)(2,1)S(1)}, u32[]{:S(2)}, u32[]{:S(2)}) collective-permute-start(bf16[1,160,384]{2,1,0:T(8,128)(2,1)S(1)} %passed_last.3.one_ref), channel_id=1, source_target_pairs={{0,8},{1,9},{2,10},{3,11},{4,12},{5,13},{6,14},{7,15},{8,0},{9,1},... | collective-permute-start | bytes 368648 | tf_op jit(solution)/shard_map/ppermute | solution.py:203
